TPU v7x, 32 devices: a whole 2x2x4 slice. The times are simulated.
32 devices in a mesh: seq: 8 (over z, x), dp: 4 (over y, core).
Axes of the slice: x: 2, y: 2, z: 4, core: 2. Of those that a mesh axis runs over, the one named last changes fastest.
Arguments:
- emb_grad: bfloat16 [4, 8192, 1792], P('dp', 'seq'), may hold values from -6 to 6
- image_map: int32 [4, 8192], P('dp', 'seq'), may hold values from -1 to 8191, as said below
- pre_act: bfloat16 [4, 8192, 2560], P('dp', 'seq'), may hold values from -8 to 8
- w_down: bfloat16 [2560, 1792], P('seq'), may hold values from -0.125 to 0.125
Outputs:
- act_grad: bfloat16 [4, 8192, 2560], P('dp', 'seq')
- w_grad: float32 [2560, 1792], P('seq')
Inputs may be any that keep to these rules, and one draw needn't show every extreme that they name: `image_map`: no two tokens of one replica name the same row. The tokens of one device name at most 128 rows of one device's block of 1024 rows; in every draw some device's block gets exactly 128 rows from every device. Loads of the blocks are skewed.
All inputs are finite; a program needn't handle non-finite values.
Results may differ from a plain program's by a relative error of at most 0.0026.
Values may be sent and summed in bfloat16 or wider, within the bound.
No kernel may reach another device: no remote copies, remote signals or barrier semaphores. Data moves between devices by JAX's collectives and lax.ppermute only.
A program may use at most 128 MiB of HBM per device.

v0:
```python
import math

import jax
import jax.numpy as jnp
from jax import lax
from jax.sharding import PartitionSpec as P


def gelu_parts(pre_rows):
    values = pre_rows.astype(jnp.float32)
    normal_cdf = 0.5 * (1.0 + lax.erf(values * (1.0 / math.sqrt(2.0))))
    density = jnp.exp(-0.5 * values * values) * (1.0 / math.sqrt(2.0 * math.pi))
    return (values * normal_cdf, normal_cdf + values * density)


def local(emb_grad, image_map, pre_act, w_down):
    seq_count = lax.axis_size("seq")
    token_grad = emb_grad[0]
    targets = image_map[0]
    pre_rows = pre_act[0]
    tok_dev = token_grad.shape[0]
    rows_dev = pre_rows.shape[0]
    capacity = rows_dev // seq_count
    token_live = targets >= 0
    owner_dev = jnp.where(token_live, targets // rows_dev, seq_count)
    member_table = (owner_dev[:, None] == jnp.arange(seq_count)[None, :]).astype(jnp.int32)
    before = jnp.cumsum(member_table, axis=0) - member_table
    position = jnp.sum(before * member_table, axis=1)
    slot_index = jnp.where(token_live, owner_dev * capacity + position, rows_dev)
    token_order = jnp.arange(tok_dev, dtype=jnp.int32)
    slot_token = jnp.zeros((rows_dev + 1,), jnp.int32).at[slot_index].set(token_order)
    slot_rows = (
        jnp.full((rows_dev + 1,), -1, jnp.int32)
        .at[slot_index]
        .set(jnp.where(token_live, targets % rows_dev, -1))
    )
    slot_rows = slot_rows[:rows_dev]
    outgoing = jnp.where(
        (slot_rows >= 0)[:, None], token_grad[slot_token[:rows_dev]], jnp.zeros((), jnp.bfloat16)
    )
    outgoing = outgoing.reshape(seq_count, capacity, token_grad.shape[1])
    arrived, arrived_rows = (
        lax.all_to_all(outgoing, "seq", split_axis=0, concat_axis=0, tiled=True),
        lax.all_to_all(
            slot_rows.reshape(seq_count, capacity), "seq", split_axis=0, concat_axis=0, tiled=True
        ),
    )
    flat_rows = arrived_rows.reshape(-1)
    landing = jnp.where(flat_rows >= 0, flat_rows, rows_dev).astype(jnp.int32)
    row_slot = (
        jnp.zeros((rows_dev + 1,), jnp.int32).at[landing].set(jnp.arange(rows_dev, dtype=jnp.int32))
    )
    row_live = jnp.zeros((rows_dev + 1,), jnp.int32).at[landing].set(1)
    flat_arrived = arrived.reshape(rows_dev, token_grad.shape[1])
    placed = jnp.where(
        (row_live[:rows_dev] > 0)[:, None],
        flat_arrived[row_slot[:rows_dev]],
        jnp.zeros((), jnp.bfloat16),
    )
    activation, gelu_slope = gelu_parts(pre_rows)
    hidden_grad = lax.dot_general(
        placed,
        lax.all_gather(w_down, "seq", axis=0, tiled=True),
        (((1,), (1,)), ((), ())),
        preferred_element_type=jnp.float32,
    )
    act_grad = (hidden_grad * gelu_slope).astype(jnp.bfloat16)
    hidden = activation.astype(jnp.bfloat16)
    replicas = lax.axis_size("dp")
    share_rows = lax.psum_scatter(
        lax.dot_general(
            hidden, placed, (((0,), (0,)), ((), ())), preferred_element_type=jnp.float32
        ),
        ("seq", "dp"),
        scatter_dimension=0,
        tiled=True,
    )
    grad_total = lax.all_gather(share_rows, "dp", axis=0, tiled=True)
    normalizer = 1.0 / math.sqrt(replicas * rows_dev * seq_count)
    return (act_grad[None], grad_total * normalizer)


def solution(mesh):
    placed = (P("dp", "seq", None), P("dp", "seq"), P("dp", "seq", None), P("seq", None))
    return jax.shard_map(
        local,
        mesh=mesh,
        in_specs=placed,
        out_specs=(P("dp", "seq", None), P("seq", None)),
        check_vma=False,
    )
```

profile of v0, /device:TPU:1, one launch (start us, length us, event | category | flops | bytes accessed | tf_op | source)
XLA Modules:
  0.0 476.1 jit_solution(3978954913932969963)
XLA Ops:
  8.0 0.7 fusion.19
  8.7 2.3 reduce-window.6
  11.0 0.3 slice_reduce_fusion
  11.3 0.2 reduce-window.9
  11.4 0.1 add_bitcast_fusion
  11.5 0.7 fusion.20
  12.2 0.7 compare_select_fusion.2
  12.9 4.3 scatter_custom_fusion
  17.3 0.6 slice.29
  17.9 6.4 %all-to-all-start = ((s32[8,1,128]{2,1,0:T(1,128)}), s32[8,1,128]{2,1,0:T(1,128)S(1)}, u32[]{:S(2)}, u32[]{:S(2)}) async-start(s32[8,1,128]{2,1,0:T(1,128)} %bitcast.6), calls=%async_computation | async-start | bytes 8192 | tf_op jit(solution)/shard_map/all_to_all | solution.py:44
  24.2 4.3 scatter_custom_fusion.2
  28.6 10.4 %gather_fusion = bf16[1024,1792]{1,0:T(8,128)(2,1)} fusion(bf16[1024,1792]{1,0:T(8,128)(2,1)} %bitcast.60, s32[1024]{0:T(1024)S(1)} %fusion.23), kind=kCustom, calls=%fused_computation | custom fusion | bytes 7344128 | tf_op jit(solution)/shard_map/gather | solution.py:39
  39.0 4.2 broadcast_select_fusion.1
  43.2 0.0 all-to-all-done
  43.2 5.4 %all-to-all-start.1 = ((bf16[8,128,1792]{2,1,0:T(8,128)(2,1)}), bf16[8,128,1792]{2,1,0:T(8,128)(2,1)}, u32[]{:S(2)}, u32[]{:S(2)}) async-start(bf16[8,128,1792]{2,1,0:T(8,128)(2,1)} %broadcast_select_fusion.1), calls=%async_computation.1 | async-start | bytes 7340032 | tf_op jit(solution)/shard_map/all_to_all | solution.py:43
  48.7 0.0 reduce-scatter.2.cloned.1.call-start
  48.7 4.3 scatter_custom_fusion.3
  53.1 4.5 scatter_custom_fusion.1
  57.6 71.7 %all-to-all-done.1 = bf16[8,128,1792]{2,1,0:T(8,128)(2,1)} async-done(((bf16[8,128,1792]{2,1,0:T(8,128)(2,1)}), bf16[8,128,1792]{2,1,0:T(8,128)(2,1)}, u32[]{:S(2)}, u32[]{:S(2)}) %all-to-all-start.1) | async-done | bytes 3670048 | tf_op jit(solution)/shard_map/all_to_all | solution.py:43
  129.3 10.5 %gather_fusion.1 = bf16[1024,1792]{1,0:T(8,128)(2,1)} fusion(bf16[1024,1792]{1,0:T(8,128)(2,1)} %bitcast.12, s32[1024]{0:T(1024)S(1)} %fusion.24), kind=kCustom, calls=%fused_computation.1 | custom fusion | bytes 7344128 | tf_op jit(solution)/shard_map/gather | solution.py:57
  139.7 16.8 %fusion.9 = f32[2560,1792]{1,0:T(8,128)} fusion(bf16[1,1024,2560]{2,1,0:T(8,128)(2,1)} %param.6, bf16[1024,1792]{1,0:T(8,128)(2,1)} %gather_fusion.1, pred[1024]{0:T(1024)(128)(4,1)S(1)} %slice_compare_fusion), kind=kOutput, calls=%fused_computation.20 | convolution fusion | flops 9412804608 | bytes 27264000 | tf_op jit(solution)/shard_map/dot_general | solution.py:71
  156.6 0.0 reduce-scatter.2.cloned.1.call-update
  156.6 0.0 all-gather.3.cloned.1.call-start
  156.6 0.5 all-gather.3.cloned.1.call-update
  157.2 0.0 all-gather.5.cloned.1.call-start
  157.2 286.1 %reduce-scatter.2.cloned.1.call-done = f32[80,1792]{1,0:T(8,128)} async-done(((f32[2560,1792]{1,0:T(8,128)}), f32[80,1792]{1,0:T(8,128)}) %reduce-scatter.2.cloned.1.call-update) | async-done | bytes 573456 | tf_op jit(solution)/shard_map/reduce_scatter | solution.py:70
  443.3 0.0 all-gather.5.cloned.1.call-update
  443.4 0.0 all-gather.3.cloned.1.call-done
  443.4 17.9 %fusion.12 = bf16[1,1024,2560]{2,1,0:T(8,128)(2,1)} fusion(bf16[1,1024,2560]{2,1,0:T(8,128)(2,1)} %param.6, bf16[2560,1792]{1,0:T(8,128)(2,1)} %all-gather.3.cloned.1.call-done, bf16[1024,1792]{1,0:T(8,128)(2,1)} %gather_fusion.1, pred[1024]{0:T(1024)(128)(4,1)S(1)} %slice_compare_fusion), kind=kOutput, calls=%fused_computation.22 | convolution fusion | flops 9425911808 | bytes 23331840 | tf_op jit(solution)/shard_map/dot_general | solution.py:61
  461.3 4.1 all-gather.5.cloned.1.call-done
  465.4 3.2 broadcast_multiply_fusion
  (10 shorter events, 0.1 us)
Async XLA Ops:
  17.9 25.4 %all-to-all-start = ((s32[8,1,128]{2,1,0:T(1,128)}), s32[8,1,128]{2,1,0:T(1,128)S(1)}, u32[]{:S(2)}, u32[]{:S(2)}) async-start(s32[8,1,128]{2,1,0:T(1,128)} %bitcast.6), calls=%async_computation | async-start | bytes 8192 | tf_op jit(solution)/shard_map/all_to_all | solution.py:44
  43.2 86.0 %all-to-all-start.1 = ((bf16[8,128,1792]{2,1,0:T(8,128)(2,1)}), bf16[8,128,1792]{2,1,0:T(8,128)(2,1)}, u32[]{:S(2)}, u32[]{:S(2)}) async-start(bf16[8,128,1792]{2,1,0:T(8,128)(2,1)} %broadcast_select_fusion.1), calls=%async_computation.1 | async-start | bytes 7340032 | tf_op jit(solution)/shard_map/all_to_all | solution.py:43
  48.7 394.7 %reduce-scatter.2.cloned.1.call-start = ((), (), s32[]{:S(2)}) async-start(), calls=%async_computation.4 | async-start | bytes 18923520 | tf_op jit(solution)/shard_map/reduce_scatter | solution.py:70
  156.6 286.8 %all-gather.3.cloned.1.call-start = ((), (), s32[]{:S(2)}) async-start(), calls=%async_computation.3 | async-start | bytes 10321920 | tf_op jit(solution)/shard_map/all_gather | solution.py:63
  157.2 308.3 %all-gather.5.cloned.1.call-start = ((), (), s32[]{:S(2)}) async-start(), calls=%async_computation.5 | async-start | bytes 2867200 | tf_op jit(solution)/shard_map/all_gather | solution.py:78
Sparse Core Ops, SparseCore 0:
  156.7 286.5 reduce-scatter.1
Sparse Core Ops, SparseCore 1:
  159.2 141.5 all-gather.2
  443.4 21.9 all-gather.4
where the time goes:
time: 477 us; the launch traced here: 476 us
  waiting for transfers between devices  363 us (76%)
  local copies, waits for them, and re-layouts  39.2 us (8%)
  matrix products  34.7 us (7%)
  between operations  15.6 us (3%)
  other arithmetic  12.1 us (3%)
  starting transfers between devices  11.9 us (2%)
    reduce_scatter x1, waiting for transfers between devices, local(): lax.psum_scatter(lax.dot_general(hidden, placed, (((0,), (0,)), ((), ()))...  286 us
    all_to_all x1, waiting for transfers between devices, local(): lax.all_to_all(outgoing, 'seq', split_axis=0, concat_axis=0, tiled=True)  71.7 us
    dot_general x1, matrix products, local(): lax.dot_general(placed, lax.all_gather(w_down, 'seq', axis=0, tiled=True)...  17.9 us
    dot_general x1, matrix products, local(): lax.dot_general(hidden, placed, (((0,), (0,)), ((), ())), preferred_eleme...  16.8 us
    gather x1, local copies, waits for them, and re-layouts, local(): flat_arrived[row_slot[:rows_dev]]  10.5 us
    gather x1, local copies, waits for them, and re-layouts, local(): token_grad[slot_token[:rows_dev]]  10.4 us
  transfers between devices with their start and end apart: 5, of which 3 were waited for; matrix products, arithmetic and copies ran while one was open for 10% of the time, Pallas kernels for 0%

commit v1 on v0

v1 whole, which is shorter than its diff:
```python
import functools
import math

import jax
import jax.numpy as jnp
from jax import lax
from jax.experimental import pallas as pl
from jax.experimental.pallas import tpu as pltpu
from jax.sharding import PartitionSpec as P

F32, BF16, I32 = jnp.float32, jnp.bfloat16, jnp.int32
MIB = 2**20
WIDTHS = (256, 512, 512, 256, 256)
ID_BASE = 32
ID_ROWS = 16
GROUP = 640


def dot(a, b, dims=((1,), (0,))):
    return lax.dot_general(a, b, (dims, ((), ())), preferred_element_type=F32)


def params(mib):
    return pltpu.CompilerParams(vmem_limit_bytes=mib * MIB)


def cost(flops, nbytes):
    return pl.CostEstimate(flops=int(flops), bytes_accessed=int(nbytes), transcendentals=0)


def whole(*dims):
    return pl.BlockSpec(dims, lambda *_: (0,) * len(dims))


def reverse(index, bits):
    back = 0
    for bit in range(bits):
        one = lax.bitwise_and(lax.shift_right_logical(index, bit), 1)
        back = back + one * (1 << (bits - 1 - bit))
    return back


def route_kernel(n_seq, cap, rows_dev, map_ref, emb_ref, pick_ref, send_ref):
    targets = map_ref[...]
    groups, lanes = targets.shape
    live = targets >= 0
    safe = jnp.where(live, targets, 0)
    owner = jnp.where(live, lax.div(safe, rows_dev), n_seq)
    members = [(owner == j).astype(F32) for j in range(n_seq)]
    table = jnp.concatenate(members, axis=0).astype(BF16)
    upper = (
        lax.broadcasted_iota(I32, (lanes, lanes), 0) < lax.broadcasted_iota(I32, (lanes, lanes), 1)
    ).astype(F32).astype(BF16)
    inside = dot(table, upper)
    total = n_seq * groups
    row = lax.broadcasted_iota(I32, (total, total), 0)
    col = lax.broadcasted_iota(I32, (total, total), 1)
    earlier = ((lax.div(row, groups) == lax.div(col, groups)) & (col < row)).astype(F32).astype(BF16)
    counts = dot(table, jnp.ones((lanes, lanes), BF16))
    rank_all = inside + dot(earlier, counts.astype(BF16))
    rank = jnp.zeros((groups, lanes), F32)
    for j in range(n_seq):
        rank = rank + members[j] * rank_all[j * groups : (j + 1) * groups]
    slot = jnp.where(live, owner * cap + rank.astype(I32), -1)
    number = jnp.where(live, safe - owner * rows_dev + 1, 0)
    high = lax.div(number, ID_BASE)
    low = (number - high * ID_BASE).astype(F32).astype(BF16)
    high = high.astype(F32).astype(BF16)
    slots = n_seq * cap
    place = lax.broadcasted_iota(I32, (slots, lanes), 0)
    ids = jnp.zeros((ID_ROWS, slots), F32)
    for g in range(groups):
        part = (place == slot[g : g + 1]).astype(F32).astype(BF16)
        pick_ref[:, g * lanes : (g + 1) * lanes] = part
        pair = jnp.concatenate(
            [
                jnp.broadcast_to(high[g : g + 1], (ID_ROWS // 2, lanes)),
                jnp.broadcast_to(low[g : g + 1], (ID_ROWS // 2, lanes)),
            ],
            axis=0,
        )
        ids = ids + dot(pair, part, ((1,), (1,)))
    ids = ids.astype(BF16)
    moved = dot(pick_ref[...], emb_ref[...]).astype(BF16)
    width = emb_ref.shape[1]
    for j in range(n_seq):
        send_ref[j, :cap] = moved[j * cap : (j + 1) * cap]
        digits = ids[:, j * cap : (j + 1) * cap]
        rest = jnp.zeros((ID_ROWS, width - cap), BF16)
        send_ref[j, cap:] = jnp.concatenate([digits, rest], axis=1)


def pack_kernel(n_seq, cap, start, widths, pick_ref, emb_ref, *send_refs):
    first = start
    for send_ref, width in zip(send_refs, widths):
        moved = dot(pick_ref[...], emb_ref[:, first : first + width]).astype(BF16)
        for j in range(n_seq):
            send_ref[j] = moved[j * cap : (j + 1) * cap]
        first += width


def hidden_kernel(height, me_ref, pre_ref, mine_ref, theirs_ref, slope_ref):
    values = pre_ref[...].astype(F32)
    normal_cdf = 0.5 * (1.0 + lax.erf(values * (1.0 / math.sqrt(2.0))))
    density = jnp.exp(-0.5 * values * values) * (1.0 / math.sqrt(2.0 * math.pi))
    slope_ref[...] = normal_cdf + values * density
    hidden = (values * normal_cdf).astype(BF16).T
    even_mine = lax.bitwise_and(me_ref[1], 1) == 0
    for k in range(mine_ref.shape[0] // height):
        even = hidden[2 * k * height : (2 * k + 1) * height]
        odd = hidden[(2 * k + 1) * height : (2 * k + 2) * height]
        mine_ref[k * height : (k + 1) * height] = jnp.where(even_mine, even, odd)
        theirs_ref[k * height : (k + 1) * height] = jnp.where(even_mine, odd, even)


def landing_kernel(n_seq, cap, rows_dev, got_ref, land_ref):
    lows = ID_ROWS // 2
    ids = []
    for i in range(n_seq):
        digits = got_ref[i, cap:].astype(F32)[:, :cap]
        ids.append(digits[0:1] * float(ID_BASE) + digits[lows : lows + 1])
    ids = jnp.concatenate(ids, axis=1).astype(I32) - 1
    slots = ids.shape[1]
    step = 128
    for first in range(0, rows_dev, step):
        row = lax.broadcasted_iota(I32, (step, slots), 0) + first
        land_ref[first : first + step] = (row == ids).astype(F32).astype(BF16)


def place_kernel(n_seq, cap, n_after, land_ref, got_ref, *refs):
    placed_ref = refs[n_after]
    got = jnp.concatenate([got_ref[i, :cap] for i in range(n_seq)], axis=0)
    placed_ref[...] = dot(land_ref[...], got).astype(BF16)


def share_kernel(n_seq, n_pairs, height, me_ref, mine_ref, theirs_ref, own_ref, other_ref, away_ref, keep_ref):
    step = pl.program_id(0)
    share = dot(mine_ref[...], own_ref[...]) + dot(theirs_ref[...], other_ref[...])
    bits = n_seq.bit_length() - 1
    my_pair = lax.shift_right_logical(me_ref[1], 1)
    per_step = mine_ref.shape[0] // (height * n_pairs)
    half = n_pairs // 2
    for a in range(per_step):
        u = reverse(lax.bitwise_xor(step * per_step + a, me_ref[0]), bits)
        for p in range(half):
            low = (a * n_pairs + p) * height
            high = (a * n_pairs + p + half) * height
            low, high = share[low : low + height], share[high : high + height]
            low_mine = my_pair < half
            at = lax.bitwise_xor(p, lax.bitwise_and(my_pair, half - 1)) * n_seq + u
            keep_ref[at] = jnp.where(low_mine, low, high)
            away_ref[at] = jnp.where(low_mine, high, low).astype(BF16)


def act_kernel(n_pieces, n_parts, me_ref, *refs):
    placed_refs, refs = refs[:n_parts], refs[n_parts:]
    mine_refs, refs = refs[:n_pieces], refs[n_pieces:]
    their_refs, refs = refs[:n_pieces], refs[n_pieces:]
    slope_ref, out_ref = refs[0], refs[-1]
    even_mine = lax.bitwise_and(me_ref[1], 1) == 0
    blocks = []
    for mine, theirs in zip(mine_refs, their_refs):
        blocks.append(jnp.where(even_mine, mine[0], theirs[0]))
        blocks.append(jnp.where(even_mine, theirs[0], mine[0]))
    weights = jnp.concatenate(blocks, axis=0)
    placed = jnp.concatenate([r[...] for r in placed_refs], axis=1)
    grad = dot(placed, weights, ((1,), (1,)))
    out_ref[...] = (grad * slope_ref[...]).astype(BF16)


def swap(value, axis, bit):
    size = lax.axis_size(axis)
    return lax.ppermute(value, axis, [(i, i ^ (1 << bit)) for i in range(size)])


def local(emb_grad, image_map, pre_act, w_down):
    n_seq, n_dp = lax.axis_size("seq"), lax.axis_size("dp")
    seq_bits, dp_bits = n_seq.bit_length() - 1, n_dp.bit_length() - 1
    me_s = lax.axis_index("seq").astype(I32)
    me_d = lax.axis_index("dp").astype(I32)
    me = jnp.stack([me_s, me_d])
    tokens, dim = emb_grad.shape[1:]
    rows_dev, hid = pre_act.shape[1:]
    cap = rows_dev // n_seq
    slots = n_seq * cap
    emb, pre = emb_grad[0], pre_act[0]
    n_parts = len(WIDTHS)
    height = hid // (n_seq * n_dp)
    smem = pl.BlockSpec(memory_space=pltpu.SMEM)
    anywhere = pl.BlockSpec(memory_space=pl.ANY)
    shape = jax.ShapeDtypeStruct

    weights = lax.dynamic_slice(w_down, (me_d * height, 0), (height, dim))[None]
    for bit in reversed(range(seq_bits)):
        weights = jnp.concatenate([weights, swap(weights, "seq", bit)], axis=0)
    for bit in reversed(range(1, dp_bits)):
        weights = jnp.concatenate([weights, swap(weights, "dp", bit)], axis=0)
    their_weights = swap(weights, "dp", 0)

    def exchange(blocks):
        return lax.all_to_all(blocks, "seq", split_axis=0, concat_axis=0, tiled=True)

    pick, sends = pl.pallas_call(
        functools.partial(route_kernel, n_seq, cap, rows_dev),
        grid=(1,),
        in_specs=[whole(tokens // 128, 128), whole(tokens, WIDTHS[0])],
        out_specs=[whole(slots, tokens), whole(n_seq, cap + ID_ROWS, WIDTHS[0])],
        out_shape=[
            shape((slots, tokens), BF16),
            shape((n_seq, cap + ID_ROWS, WIDTHS[0]), BF16),
        ],
        compiler_params=params(20),
        cost_estimate=cost(4e9, 4e6),
        name="route",
    )(image_map.reshape(tokens // 128, 128), emb)
    got_parts = [exchange(sends)]

    rest = WIDTHS[1:]
    packed = pl.pallas_call(
        functools.partial(pack_kernel, n_seq, cap, WIDTHS[0], rest),
        grid=(1,),
        in_specs=[whole(slots, tokens), whole(tokens, dim)],
        out_specs=[whole(n_seq, cap, w) for w in rest],
        out_shape=[shape((n_seq, cap, w), BF16) for w in rest],
        compiler_params=params(40),
        cost_estimate=cost(4e9, 8e6),
        name="pack",
    )(pick, emb)
    got_parts += [exchange(p) for p in packed]

    mine_t, away_t, slope = pl.pallas_call(
        functools.partial(hidden_kernel, height),
        grid=(hid // GROUP,),
        in_specs=[smem, pl.BlockSpec((rows_dev, GROUP), lambda i: (0, i))],
        out_specs=[pl.BlockSpec((GROUP // 2, rows_dev), lambda i: (i, 0))] * 2
        + [pl.BlockSpec((rows_dev, GROUP), lambda i: (0, i))],
        out_shape=[shape((hid // 2, rows_dev), BF16)] * 2 + [shape((rows_dev, hid), F32)],
        compiler_params=params(40),
        cost_estimate=cost(4e9, 21e6),
        name="hidden",
    )(me, pre)
    theirs_t = swap(away_t, "dp", 0)
    land = pl.pallas_call(
        functools.partial(landing_kernel, n_seq, cap, rows_dev),
        grid=(1,),
        in_specs=[whole(n_seq, cap + ID_ROWS, WIDTHS[0])],
        out_specs=whole(rows_dev, slots),
        out_shape=shape((rows_dev, slots), BF16),
        compiler_params=params(16),
        cost_estimate=cost(1e9, 3e6),
        name="landing",
    )(got_parts[0])

    normalizer = 1.0 / math.sqrt(n_dp * rows_dev * n_seq)
    n_pairs = n_dp // 2
    kept = n_seq * n_pairs // 2
    placed_parts, grads = [], []
    for c in range(n_parts):
        width = WIDTHS[c]
        got = got_parts[c]
        after = []
        placed = pl.pallas_call(
            functools.partial(place_kernel, n_seq, cap, len(after)),
            grid=(1,),
            in_specs=[whole(rows_dev, slots), whole(*got.shape)] + [anywhere] * len(after),
            out_specs=whole(rows_dev, width),
            out_shape=shape((rows_dev, width), BF16),
            compiler_params=params(16),
            cost_estimate=cost(2 * rows_dev * width * slots, 4e6),
            name="place",
        )(land, got, *after)
        placed_parts.append(placed)
        other = swap(placed, "dp", 0)
        away, keep = pl.pallas_call(
            functools.partial(share_kernel, n_seq, n_pairs, height),
            grid=(hid // GROUP,),
            in_specs=[smem]
            + [pl.BlockSpec((GROUP // 2, rows_dev), lambda i: (i, 0))] * 2
            + [whole(rows_dev, width)] * 2,
            out_specs=[whole(kept, height, width)] * 2,
            out_shape=[shape((kept, height, width), BF16), shape((kept, height, width), F32)],
            compiler_params=params(24),
            cost_estimate=cost(2 * rows_dev * width * hid, 8e6),
            name="share",
        )(me, mine_t, theirs_t, placed, other)
        total = keep + swap(away, "dp", dp_bits - 1).astype(F32)
        order = [("dp", bit) for bit in reversed(range(1, dp_bits - 1))]
        order += [("seq", bit) for bit in range(seq_bits)]
        for axis, bit in order:
            n = total.shape[0] // 2
            total = total[:n] + swap(total[n:].astype(BF16), axis, bit).astype(F32)
        grads.append(lax.all_gather(total[0] * normalizer, "dp", axis=0, tiled=True))

    n_pieces = GROUP // (2 * height)

    def w_spec(k):
        def index(i, me_ref):
            flat = i * n_pieces + k
            s, pair = lax.div(flat, n_pairs), lax.rem(flat, n_pairs)
            u = lax.bitwise_xor(s, me_ref[0])
            v = lax.bitwise_xor(pair, lax.shift_right_logical(me_ref[1], 1))
            return (reverse(v, dp_bits - 1) * n_seq + reverse(u, seq_bits), 0, 0)

        return pl.BlockSpec((1, height, dim), index)

    act_grad = pl.pallas_call(
        functools.partial(act_kernel, n_pieces, n_parts),
        grid_spec=pltpu.PrefetchScalarGridSpec(
            num_scalar_prefetch=1,
            grid=(hid // GROUP,),
            in_specs=[whole(rows_dev, w) for w in WIDTHS]
            + [w_spec(k) for k in range(n_pieces)] * 2
            + [pl.BlockSpec((rows_dev, GROUP), lambda i, m: (0, i))],
            out_specs=pl.BlockSpec((rows_dev, GROUP), lambda i, m: (0, i)),
        ),
        out_shape=shape((rows_dev, hid), BF16),
        compiler_params=params(48),
        cost_estimate=cost(2 * rows_dev * dim * hid, 29e6),
        name="act",
    )(me, *placed_parts, *([weights] * n_pieces), *([their_weights] * n_pieces), slope)
    return act_grad[None], jnp.concatenate(grads, axis=1)


def solution(mesh):
    placed = (P("dp", "seq", None), P("dp", "seq"), P("dp", "seq", None), P("seq", None))
    return jax.shard_map(
        local,
        mesh=mesh,
        in_specs=placed,
        out_specs=(P("dp", "seq", None), P("seq", None)),
        check_vma=False,
    )
```

time: 477 us -> 345 us (0.72)
  waiting for transfers between devices: 363 us -> 95.7 us
  blocking collectives: 0 us -> 97 us
  Pallas kernels: 0 us -> 61.6 us
  starting transfers between devices: 11.9 us -> 65.6 us
  matrix products: 34.7 us -> 0 us
  local copies, waits for them, and re-layouts: 39.2 us -> 17.8 us
  between operations: 15.6 us -> 1.21 us
  other arithmetic: 12.1 us -> 5.02 us
    reduce_scatter x1 -> x0, waiting for transfers between devices: 286 us -> none  [local(): lax.psum_scatter(lax.dot_general(hidden, placed, (((0,), (0,)), ((), ()))...]
    ppermute x0 -> x31, waiting for transfers between devices: none -> 95.7 us  [swap(): return lax.ppermute(value, axis, [(i, i ^ 1 << bit) for i in range(size)])]
    all_to_all x2, waiting for transfers between devices: 71.7 us -> 0.01 us  [exchange(): lax.all_to_all(blocks, 'seq', split_axis=0, concat_axis=0, tiled=True)]
    pallas_call x0 -> x15, Pallas kernels: none -> 61.6 us  [the longest x5 22.4 us: local(): pl.pallas_call(functools.partial(share_kernel, n_seq, n_pairs, height), g...]
    all_to_all x0 -> x3, blocking collectives: none -> 56.9 us  [exchange(): lax.all_to_all(blocks, 'seq', split_axis=0, concat_axis=0, tiled=True)]
    ppermute x0 -> x31, starting transfers between devices: none -> 56.5 us  [swap(): return lax.ppermute(value, axis, [(i, i ^ 1 << bit) for i in range(size)])]
    all_gather x0 -> x5, blocking collectives: none -> 40.1 us  [local(): lax.all_gather(total[0] * normalizer, 'dp', axis=0, tiled=True)]
    dot_general x2 -> x0, matrix products: 34.7 us -> none  [the longest x1 17.9 us: local(): lax.dot_general(placed, lax.all_gather(w_down, 'seq', axis=0, tiled=True)...]
  transfers between devices with their start and end apart: 5 -> 33, of which waited for: 3 -> 14; matrix products, arithmetic and copies ran while one was open for 10% -> 4% of each run, Pallas kernels for 0% -> 11%
where the time goes in v1:
time: 345 us; the launch traced here: 344 us
  blocking collectives  97 us (28%)
  waiting for transfers between devices  95.7 us (28%)
  starting transfers between devices  65.6 us (19%)
  Pallas kernels  61.6 us (18%)
  local copies, waits for them, and re-layouts  17.8 us (5%)
  other arithmetic  5.02 us (1%)
    ppermute x31, waiting for transfers between devices, swap(): return lax.ppermute(value, axis, [(i, i ^ 1 << bit) for i in range(size)])  95.7 us
    all_to_all x3, blocking collectives, exchange(): lax.all_to_all(blocks, 'seq', split_axis=0, concat_axis=0, tiled=True)  56.9 us
    ppermute x31, starting transfers between devices, swap(): return lax.ppermute(value, axis, [(i, i ^ 1 << bit) for i in range(size)])  56.5 us
    all_gather x5, blocking collectives, local(): lax.all_gather(total[0] * normalizer, 'dp', axis=0, tiled=True)  40.1 us
    pallas_call x5, Pallas kernels, local(): pl.pallas_call(functools.partial(share_kernel, n_seq, n_pairs, height), g...  22.4 us
    pallas_call x1, Pallas kernels, local(): pl.pallas_call(functools.partial(act_kernel, n_pieces, n_parts), grid_spe...  17.5 us
    unnamed x46, local copies, waits for them, and re-layouts  16 us
    all_to_all x2, starting transfers between devices, exchange(): lax.all_to_all(blocks, 'seq', split_axis=0, concat_axis=0, tiled=True)  9.14 us
  transfers between devices with their start and end apart: 33, of which 14 were waited for; matrix products, arithmetic and copies ran while one was open for 4% of the time, Pallas kernels for 11%

profile of v1, /device:TPU:1, one launch (start us, length us, event | category | flops | bytes accessed | tf_op | source)
XLA Modules:
  0.0 344.0 jit_solution(8848620656444219663)
XLA Ops:
  5.4 3.9 %pack.1 = (bf16[8,128,512]{2,1,0:T(8,128)(2,1)}, bf16[8,128,512]{2,1,0:T(8,128)(2,1)}, bf16[8,128,256]{2,1,0:T(8,128)(2,1)S(1)}, bf16[8,128,256]{2,1,0:T(8,128)(2,1)S(1)}) custom-call(bf16[1024,1024]{1,0:T(8,128)(2,1)S(1)} %get-tuple-element.22.pick_ref, bf16[1024,1792]{1,0:T(8,128)(2,1)S(1)} %bitcast.21), custom_call_target="tpu_custom_call" | custom-call | flops 4000000000 | bytes 8000000 | tf_op jit(solution)/shard_map/pack/pallas_call | solution.py:219
  9.3 19.9 %all_to_all.25.got_ref = bf16[8,128,256]{2,1,0:T(8,128)(2,1)} all-to-all(bf16[8,128,256]{2,1,0:T(8,128)(2,1)S(1)} %get-tuple-element.26), channel_id=1, replica_groups=mesh['seq'=8,'dp'=4] {'seq'}, dimensions={0} | all-to-all | bytes 1048576 | tf_op jit(solution)/shard_map/all_to_all | solution.py:201
  29.2 17.5 %all_to_all.26.got_ref = bf16[8,128,256]{2,1,0:T(8,128)(2,1)} all-to-all(bf16[8,128,256]{2,1,0:T(8,128)(2,1)S(1)} %get-tuple-element.25), channel_id=1, replica_groups=mesh['seq'=8,'dp'=4] {'seq'}, dimensions={0} | all-to-all | bytes 1048576 | tf_op jit(solution)/shard_map/all_to_all | solution.py:201
  46.7 19.4 %all_to_all.27.got_ref = bf16[8,144,256]{2,1,0:T(8,128)(2,1)S(1)} all-to-all(bf16[8,144,256]{2,1,0:T(8,128)(2,1)S(1)} %get-tuple-element.21), channel_id=1, replica_groups=mesh['seq'=8,'dp'=4] {'seq'}, dimensions={0} | all-to-all | bytes 1179648 | tf_op jit(solution)/shard_map/all_to_all | solution.py:201
  66.1 3.6 %all-to-all-start.2 = ((bf16[8,128,512]{2,1,0:T(8,128)(2,1)}), bf16[8,128,512]{2,1,0:T(8,128)(2,1)S(1)}, u32[]{:S(2)}, u32[]{:S(2)}) async-start(bf16[8,128,512]{2,1,0:T(8,128)(2,1)} %get-tuple-element.24), calls=%async_computation.2 | async-start | bytes 2097152 | tf_op jit(solution)/shard_map/all_to_all | solution.py:201
  76.3 7.8 %hidden.1 = (bf16[1280,1024]{1,0:T(8,128)(2,1)S(1)}, bf16[1280,1024]{1,0:T(8,128)(2,1)}, f32[1024,2560]{1,0:T(8,128)}) custom-call(s32[2]{0:T(128)S(1)} %pad_add_fusion.me_ref, bf16[1024,2560]{1,0:T(8,128)(2,1)S(1)} %bitcast.19), custom_call_target="tpu_custom_call" | custom-call | flops 4000000000 | bytes 21000000 | tf_op jit(solution)/shard_map/hidden/pallas_call | solution.py:231
  88.1 18.1 %collective-permute-done = bf16[1,80,1792]{2,1,0:T(8,128)(2,1)S(1)} collective-permute-done((bf16[1,80,1792]{2,1,0:T(8,128)(2,1)S(1)}, bf16[1,80,1792]{2,1,0:T(8,128)(2,1)S(1)}, u32[]{:S(2)}, u32[]{:S(2)}) %collective-permute-start) | collective-permute-done | bytes 286752 | tf_op jit(solution)/shard_map/ppermute | solution.py:173
  107.2 5.6 %all-to-all-start.1 = ((bf16[8,128,512]{2,1,0:T(8,128)(2,1)}), bf16[8,128,512]{2,1,0:T(8,128)(2,1)}, u32[]{:S(2)}, u32[]{:S(2)}) async-start(bf16[8,128,512]{2,1,0:T(8,128)(2,1)} %get-tuple-element.23), calls=%async_computation.1 | async-start | bytes 2097152 | tf_op jit(solution)/shard_map/all_to_all | solution.py:201
  112.8 6.5 %collective-permute-done.1 = bf16[2,80,1792]{2,1,0:T(8,128)(2,1)S(1)} collective-permute-done((bf16[2,80,1792]{2,1,0:T(8,128)(2,1)}, bf16[2,80,1792]{2,1,0:T(8,128)(2,1)S(1)}, u32[]{:S(2)}, u32[]{:S(2)}) %collective-permute-start.1) | collective-permute-done | bytes 573472 | tf_op jit(solution)/shard_map/ppermute | solution.py:173
  120.6 6.3 %collective-permute-start.2 = (bf16[4,80,1792]{2,1,0:T(8,128)(2,1)}, bf16[4,80,1792]{2,1,0:T(8,128)(2,1)}, u32[]{:S(2)}, u32[]{:S(2)}) collective-permute-start(bf16[4,80,1792]{2,1,0:T(8,128)(2,1)} %pad_maximum_fusion.1), channel_id=1, source_target_pairs={{0,4},{4,0},{8,12},{12,8},{16,20},{20,16},{24,28},{28,24},{1,5},{5... | collective-permute-start | bytes 3440648 | tf_op jit(solution)/shard_map/ppermute | solution.py:173
  128.7 11.3 %collective-permute-start.26 = (bf16[1024,256]{1,0:T(8,128)(2,1)S(1)}, bf16[1024,256]{1,0:T(8,128)(2,1)}, u32[]{:S(2)}, u32[]{:S(2)}) collective-permute-start(bf16[1024,256]{1,0:T(8,128)(2,1)S(1)} %place.9.refs_4_.own_ref), channel_id=1, source_target_pairs={{0,1},{1,0},{2,3},{3,2},{4,5},{5,4},{6,7},{7,6},{8,9},{9,8},{10,11... | collective-permute-start | bytes 1572872 | tf_op jit(solution)/shard_map/ppermute | solution.py:173
  151.0 8.0 %collective-permute-start.11 = (bf16[1024,512]{1,0:T(8,128)(2,1)S(1)}, bf16[1024,512]{1,0:T(8,128)(2,1)S(1)}, u32[]{:S(2)}, u32[]{:S(2)}) collective-permute-start(bf16[1024,512]{1,0:T(8,128)(2,1)S(1)} %place.6.refs_1_.own_ref), channel_id=1, source_target_pairs={{0,1},{1,0},{2,3},{3,2},{4,5},{5,4},{6,7},{7,6},{8,9},{9,8},{10,11... | collective-permute-start | bytes 3145736 | tf_op jit(solution)/shard_map/ppermute | solution.py:173
  164.3 4.0 %share.9 = (bf16[8,80,256]{2,1,0:T(8,128)(2,1)S(1)}, f32[8,80,256]{2,1,0:T(8,128)S(1)}) custom-call(s32[2]{0:T(128)S(1)} %pad_add_fusion.me_ref, bf16[1280,1024]{1,0:T(8,128)(2,1)S(1)} %copy-done.1, bf16[1280,1024]{1,0:T(8,128)(2,1)} %collective-permute-done.5.theirs_ref, bf16[1024,256]{1,0:T(8,128)(2,1)S(1)} %place.9.refs_4_.own_ref, ...), custom_call_target="tpu_custom_call" | custom-call | flops 1342177280 | bytes 8000000 | tf_op jit(solution)/shard_map/share/pallas_call | solution.py:274
  168.6 4.2 %share.8 = (bf16[8,80,256]{2,1,0:T(8,128)(2,1)S(1)}, f32[8,80,256]{2,1,0:T(8,128)S(1)}) custom-call(s32[2]{0:T(128)S(1)} %pad_add_fusion.me_ref, bf16[1280,1024]{1,0:T(8,128)(2,1)S(1)} %copy-done.1, bf16[1280,1024]{1,0:T(8,128)(2,1)} %collective-permute-done.5.theirs_ref, bf16[1024,256]{1,0:T(8,128)(2,1)} %place.8.refs_3_.own_ref, ...), custom_call_target="tpu_custom_call" | custom-call | flops 1342177280 | bytes 8000000 | tf_op jit(solution)/shard_map/share/pallas_call | solution.py:274
  174.1 3.8 %share.5 = (bf16[8,80,256]{2,1,0:T(8,128)(2,1)S(1)}, f32[8,80,256]{2,1,0:T(8,128)S(1)}) custom-call(s32[2]{0:T(128)S(1)} %pad_add_fusion.me_ref, bf16[1280,1024]{1,0:T(8,128)(2,1)S(1)} %copy-done.1, bf16[1280,1024]{1,0:T(8,128)(2,1)} %collective-permute-done.5.theirs_ref, bf16[1024,256]{1,0:T(8,128)(2,1)S(1)} %place.5.refs_0_.own_ref, ...), custom_call_target="tpu_custom_call" | custom-call | flops 1342177280 | bytes 8000000 | tf_op jit(solution)/shard_map/share/pallas_call | solution.py:274
  178.3 5.5 %share.7 = (bf16[8,80,512]{2,1,0:T(8,128)(2,1)S(1)}, f32[8,80,512]{2,1,0:T(8,128)S(1)}) custom-call(s32[2]{0:T(128)S(1)} %pad_add_fusion.me_ref, bf16[1280,1024]{1,0:T(8,128)(2,1)S(1)} %copy-done.1, bf16[1280,1024]{1,0:T(8,128)(2,1)} %collective-permute-done.5.theirs_ref, bf16[1024,512]{1,0:T(8,128)(2,1)} %place.7.refs_2_.own_ref, ...), custom_call_target="tpu_custom_call" | custom-call | flops 2684354560 | bytes 8000000 | tf_op jit(solution)/shard_map/share/pallas_call | solution.py:274
  185.1 4.9 %share.6 = (bf16[8,80,512]{2,1,0:T(8,128)(2,1)S(1)}, f32[8,80,512]{2,1,0:T(8,128)S(1)}) custom-call(s32[2]{0:T(128)S(1)} %pad_add_fusion.me_ref, bf16[1280,1024]{1,0:T(8,128)(2,1)S(1)} %copy-done.1, bf16[1280,1024]{1,0:T(8,128)(2,1)} %collective-permute-done.5.theirs_ref, bf16[1024,512]{1,0:T(8,128)(2,1)S(1)} %place.6.refs_1_.own_ref, ...), custom_call_target="tpu_custom_call" | custom-call | flops 2684354560 | bytes 8000000 | tf_op jit(solution)/shard_map/share/pallas_call | solution.py:274
  190.0 31.6 %collective-permute-done.27 = bf16[8,80,256]{2,1,0:T(8,128)(2,1)S(1)} collective-permute-done((bf16[8,80,256]{2,1,0:T(8,128)(2,1)S(1)}, bf16[8,80,256]{2,1,0:T(8,128)(2,1)S(1)}, u32[]{:S(2)}, u32[]{:S(2)}) %collective-permute-start.27) | collective-permute-done | bytes 327712 | tf_op jit(solution)/shard_map/ppermute | solution.py:173
  222.9 5.7 %collective-permute-done.22 = bf16[8,80,256]{2,1,0:T(8,128)(2,1)S(1)} collective-permute-done((bf16[8,80,256]{2,1,0:T(8,128)(2,1)S(1)}, bf16[8,80,256]{2,1,0:T(8,128)(2,1)S(1)}, u32[]{:S(2)}, u32[]{:S(2)}) %collective-permute-start.22) | collective-permute-done | bytes 327712 | tf_op jit(solution)/shard_map/ppermute | solution.py:173
  228.7 6.9 %collective-permute-done.7 = bf16[8,80,256]{2,1,0:T(8,128)(2,1)S(1)} collective-permute-done((bf16[8,80,256]{2,1,0:T(8,128)(2,1)S(1)}, bf16[8,80,256]{2,1,0:T(8,128)(2,1)S(1)}, u32[]{:S(2)}, u32[]{:S(2)}) %collective-permute-start.7) | collective-permute-done | bytes 327712 | tf_op jit(solution)/shard_map/ppermute | solution.py:173
  240.2 3.5 %collective-permute-done.8 = bf16[4,80,256]{2,1,0:T(8,128)(2,1)S(1)} collective-permute-done((bf16[4,80,256]{2,1,0:T(8,128)(2,1)S(1)}, bf16[4,80,256]{2,1,0:T(8,128)(2,1)S(1)}, u32[]{:S(2)}, u32[]{:S(2)}) %collective-permute-start.8) | collective-permute-done | bytes 163872 | tf_op jit(solution)/shard_map/ppermute | solution.py:173
  247.3 3.8 %collective-permute-start.30 = (bf16[1,80,256]{2,1,0:T(8,128)(2,1)S(1)}, bf16[1,80,256]{2,1,0:T(8,128)(2,1)S(1)}, u32[]{:S(2)}, u32[]{:S(2)}) collective-permute-start(bf16[1,80,256]{2,1,0:T(8,128)(2,1)S(1)} %slice.217), channel_id=1, source_target_pairs={{0,16},{4,20},{8,24},{12,28},{16,0},{20,4},{24,8},{28,12},{1,17},{... | collective-permute-start | bytes 122888 | tf_op jit(solution)/shard_map/ppermute | solution.py:173
  256.5 5.2 %collective-permute-start.4 = (bf16[16,80,1792]{2,1,0:T(8,128)(2,1)}, bf16[16,80,1792]{2,1,0:T(8,128)(2,1)S(1)}, u32[]{:S(2)}, u32[]{:S(2)}) collective-permute-start(bf16[16,80,1792]{2,1,0:T(8,128)(2,1)} %constant_dynamic-update-slice_fusion.refs_5_.refs_6_.refs_7_.refs_8_), channel_id=1, source_target_pairs={{0,1},{1,0},{2,3},{3,2},{4,5},{5,4},{6,7},{7,6},{8,9},{9,8},{10,11... | collective-permute-start | bytes 13762568 | tf_op jit(solution)/shard_map/ppermute | solution.py:173
  261.7 8.5 %all-gather.4 = f32[1,320,256]{2,1,0:T(8,128)S(1)} all-gather(f32[1,80,256]{2,1,0:T(8,128)S(1)} %fusion.2), channel_id=6, replica_groups=mesh['seq'=8,'dp'=4] {'dp'}, dimensions={1}, use_global_device_ids=true | all-gather | bytes 409600 | tf_op jit(solution)/shard_map/all_gather | solution.py:292
  270.3 6.2 %all-gather = f32[1,320,256]{2,1,0:T(8,128)S(1)} all-gather(f32[1,80,256]{2,1,0:T(8,128)S(1)} %fusion.4), channel_id=2, replica_groups=mesh['seq'=8,'dp'=4] {'dp'}, dimensions={1}, use_global_device_ids=true | all-gather | bytes 409600 | tf_op jit(solution)/shard_map/all_gather | solution.py:292
  278.7 6.7 %all-gather.3 = f32[1,320,256]{2,1,0:T(8,128)S(1)} all-gather(f32[1,80,256]{2,1,0:T(8,128)S(1)} %fusion.3), channel_id=5, replica_groups=mesh['seq'=8,'dp'=4] {'dp'}, dimensions={1}, use_global_device_ids=true | all-gather | bytes 409600 | tf_op jit(solution)/shard_map/all_gather | solution.py:292
  286.4 6.7 %collective-permute-done.13 = bf16[4,80,512]{2,1,0:T(8,128)(2,1)S(1)} collective-permute-done((bf16[4,80,512]{2,1,0:T(8,128)(2,1)S(1)}, bf16[4,80,512]{2,1,0:T(8,128)(2,1)S(1)}, u32[]{:S(2)}, u32[]{:S(2)}) %collective-permute-start.13) | collective-permute-done | bytes 327712 | tf_op jit(solution)/shard_map/ppermute | solution.py:173
  295.2 3.9 %collective-permute-done.14 = bf16[2,80,512]{2,1,0:T(8,128)(2,1)S(1)} collective-permute-done((bf16[2,80,512]{2,1,0:T(8,128)(2,1)S(1)}, bf16[2,80,512]{2,1,0:T(8,128)(2,1)S(1)}, u32[]{:S(2)}, u32[]{:S(2)}) %collective-permute-start.14) | collective-permute-done | bytes 163872 | tf_op jit(solution)/shard_map/ppermute | solution.py:173
  299.4 4.7 %collective-permute-done.15 = bf16[1,80,512]{2,1,0:T(8,128)(2,1)S(1)} collective-permute-done((bf16[1,80,512]{2,1,0:T(8,128)(2,1)S(1)}, bf16[1,80,512]{2,1,0:T(8,128)(2,1)S(1)}, u32[]{:S(2)}, u32[]{:S(2)}) %collective-permute-start.15) | collective-permute-done | bytes 81952 | tf_op jit(solution)/shard_map/ppermute | solution.py:173
  304.1 10.7 %all-gather.2 = f32[1,320,512]{2,1,0:T(8,128)S(1)} all-gather(f32[1,80,512]{2,1,0:T(8,128)S(1)} %fusion), channel_id=4, replica_groups=mesh['seq'=8,'dp'=4] {'dp'}, dimensions={1}, use_global_device_ids=true | all-gather | bytes 819200 | tf_op jit(solution)/shard_map/all_gather | solution.py:292
  314.9 8.0 %all-gather.1 = f32[1,320,512]{2,1,0:T(8,128)S(1)} all-gather(f32[1,80,512]{2,1,0:T(8,128)S(1)} %fusion.1), channel_id=3, replica_groups=mesh['seq'=8,'dp'=4] {'dp'}, dimensions={1}, use_global_device_ids=true | all-gather | bytes 819200 | tf_op jit(solution)/shard_map/all_gather | solution.py:292
  326.5 17.5 %act.1 = bf16[1024,2560]{1,0:T(8,128)(2,1)} custom-call(s32[2]{0:T(128)S(1)} %pad_add_fusion.me_ref, bf16[1024,256]{1,0:T(8,128)(2,1)S(1)} %place.5.refs_0_.own_ref, bf16[1024,512]{1,0:T(8,128)(2,1)S(1)} %place.6.refs_1_.own_ref, bf16[1024,512]{1,0:T(8,128)(2,1)} %place.7.refs_2_.own_ref, bf16[1024,256]{1,0:T(8,128)(2,1)} %place.8.refs_3_.own_ref, ...), custom_call_target="tpu_custom_call" | custom-call | flops 9395240960 | bytes 29000000 | tf_op jit(solution)/shard_map/act/pallas_call | solution.py:306
  (144 shorter events, 62.8 us)
Async XLA Ops:
  66.1 41.1 %all-to-all-start.2 = ((bf16[8,128,512]{2,1,0:T(8,128)(2,1)}), bf16[8,128,512]{2,1,0:T(8,128)(2,1)S(1)}, u32[]{:S(2)}, u32[]{:S(2)}) async-start(bf16[8,128,512]{2,1,0:T(8,128)(2,1)} %get-tuple-element.24), calls=%async_computation.2 | async-start | bytes 2097152 | tf_op jit(solution)/shard_map/all_to_all | solution.py:201
  71.4 34.8 %collective-permute-start = (bf16[1,80,1792]{2,1,0:T(8,128)(2,1)S(1)}, bf16[1,80,1792]{2,1,0:T(8,128)(2,1)S(1)}, u32[]{:S(2)}, u32[]{:S(2)}) collective-permute-start(bf16[1,80,1792]{2,1,0:T(8,128)(2,1)S(1)} %get-tuple-element.41), channel_id=1, source_target_pairs={{0,16},{4,20},{8,24},{12,28},{16,0},{20,4},{24,8},{28,12},{1,17},{... | collective-permute-start | bytes 860168 | tf_op jit(solution)/shard_map/ppermute | solution.py:173
  85.5 77.5 %collective-permute-start.5 = (bf16[1280,1024]{1,0:T(8,128)(2,1)}, bf16[1280,1024]{1,0:T(8,128)(2,1)}, u32[]{:S(2)}, u32[]{:S(2)}) collective-permute-start(bf16[1280,1024]{1,0:T(8,128)(2,1)} %get-tuple-element.29), channel_id=1, source_target_pairs={{0,1},{1,0},{2,3},{3,2},{4,5},{5,4},{6,7},{7,6},{8,9},{9,8},{10,11... | collective-permute-start | bytes 7864328 | tf_op jit(solution)/shard_map/ppermute | solution.py:173
  107.2 12.1 %collective-permute-start.1 = (bf16[2,80,1792]{2,1,0:T(8,128)(2,1)}, bf16[2,80,1792]{2,1,0:T(8,128)(2,1)S(1)}, u32[]{:S(2)}, u32[]{:S(2)}) collective-permute-start(bf16[2,80,1792]{2,1,0:T(8,128)(2,1)} %pad_maximum_fusion.2), channel_id=1, source_target_pairs={{0,8},{4,12},{8,0},{12,4},{16,24},{20,28},{24,16},{28,20},{1,9},{5... | collective-permute-start | bytes 1720328 | tf_op jit(solution)/shard_map/ppermute | solution.py:173
  107.2 38.6 %all-to-all-start.1 = ((bf16[8,128,512]{2,1,0:T(8,128)(2,1)}), bf16[8,128,512]{2,1,0:T(8,128)(2,1)}, u32[]{:S(2)}, u32[]{:S(2)}) async-start(bf16[8,128,512]{2,1,0:T(8,128)(2,1)} %get-tuple-element.23), calls=%async_computation.1 | async-start | bytes 2097152 | tf_op jit(solution)/shard_map/all_to_all | solution.py:201
  120.6 30.5 %collective-permute-start.2 = (bf16[4,80,1792]{2,1,0:T(8,128)(2,1)}, bf16[4,80,1792]{2,1,0:T(8,128)(2,1)}, u32[]{:S(2)}, u32[]{:S(2)}) collective-permute-start(bf16[4,80,1792]{2,1,0:T(8,128)(2,1)} %pad_maximum_fusion.1), channel_id=1, source_target_pairs={{0,4},{4,0},{8,12},{12,8},{16,20},{20,16},{24,28},{28,24},{1,5},{5... | collective-permute-start | bytes 3440648 | tf_op jit(solution)/shard_map/ppermute | solution.py:173
  128.7 19.7 %collective-permute-start.26 = (bf16[1024,256]{1,0:T(8,128)(2,1)S(1)}, bf16[1024,256]{1,0:T(8,128)(2,1)}, u32[]{:S(2)}, u32[]{:S(2)}) collective-permute-start(bf16[1024,256]{1,0:T(8,128)(2,1)S(1)} %place.9.refs_4_.own_ref), channel_id=1, source_target_pairs={{0,1},{1,0},{2,3},{3,2},{4,5},{5,4},{6,7},{7,6},{8,9},{9,8},{10,11... | collective-permute-start | bytes 1572872 | tf_op jit(solution)/shard_map/ppermute | solution.py:173
  142.4 26.0 %collective-permute-start.21 = (bf16[1024,256]{1,0:T(8,128)(2,1)}, bf16[1024,256]{1,0:T(8,128)(2,1)}, u32[]{:S(2)}, u32[]{:S(2)}) collective-permute-start(bf16[1024,256]{1,0:T(8,128)(2,1)} %place.8.refs_3_.own_ref), channel_id=1, source_target_pairs={{0,1},{1,0},{2,3},{3,2},{4,5},{5,4},{6,7},{7,6},{8,9},{9,8},{10,11... | collective-permute-start | bytes 1572872 | tf_op jit(solution)/shard_map/ppermute | solution.py:173
  144.8 33.1 %collective-permute-start.16 = (bf16[1024,512]{1,0:T(8,128)(2,1)}, bf16[1024,512]{1,0:T(8,128)(2,1)}, u32[]{:S(2)}, u32[]{:S(2)}) collective-permute-start(bf16[1024,512]{1,0:T(8,128)(2,1)} %place.7.refs_2_.own_ref), channel_id=1, source_target_pairs={{0,1},{1,0},{2,3},{3,2},{4,5},{5,4},{6,7},{7,6},{8,9},{9,8},{10,11... | collective-permute-start | bytes 3145736 | tf_op jit(solution)/shard_map/ppermute | solution.py:173
  148.4 24.4 %collective-permute-start.6 = (bf16[1024,256]{1,0:T(8,128)(2,1)S(1)}, bf16[1024,256]{1,0:T(8,128)(2,1)S(1)}, u32[]{:S(2)}, u32[]{:S(2)}) collective-permute-start(bf16[1024,256]{1,0:T(8,128)(2,1)S(1)} %place.5.refs_0_.own_ref), channel_id=1, source_target_pairs={{0,1},{1,0},{2,3},{3,2},{4,5},{5,4},{6,7},{7,6},{8,9},{9,8},{10,11... | collective-permute-start | bytes 1572872 | tf_op jit(solution)/shard_map/ppermute | solution.py:173
  151.0 32.8 %collective-permute-start.11 = (bf16[1024,512]{1,0:T(8,128)(2,1)S(1)}, bf16[1024,512]{1,0:T(8,128)(2,1)S(1)}, u32[]{:S(2)}, u32[]{:S(2)}) collective-permute-start(bf16[1024,512]{1,0:T(8,128)(2,1)S(1)} %place.6.refs_1_.own_ref), channel_id=1, source_target_pairs={{0,1},{1,0},{2,3},{3,2},{4,5},{5,4},{6,7},{7,6},{8,9},{9,8},{10,11... | collective-permute-start | bytes 3145736 | tf_op jit(solution)/shard_map/ppermute | solution.py:173
  163.1 91.9 %collective-permute-start.3 = (bf16[8,80,1792]{2,1,0:T(8,128)(2,1)S(1)}, bf16[8,80,1792]{2,1,0:T(8,128)(2,1)S(1)}, u32[]{:S(2)}, u32[]{:S(2)}) collective-permute-start(bf16[8,80,1792]{2,1,0:T(8,128)(2,1)S(1)} %pad_maximum_fusion), channel_id=1, source_target_pairs={{0,2},{1,3},{2,0},{3,1},{4,6},{5,7},{6,4},{7,5},{8,10},{9,11},{10,... | collective-permute-start | bytes 6881288 | tf_op jit(solution)/shard_map/ppermute | solution.py:173
  168.3 53.2 %collective-permute-start.27 = (bf16[8,80,256]{2,1,0:T(8,128)(2,1)S(1)}, bf16[8,80,256]{2,1,0:T(8,128)(2,1)S(1)}, u32[]{:S(2)}, u32[]{:S(2)}) collective-permute-start(bf16[8,80,256]{2,1,0:T(8,128)(2,1)S(1)} %get-tuple-element.39), channel_id=1, source_target_pairs={{0,2},{1,3},{2,0},{3,1},{4,6},{5,7},{6,4},{7,5},{8,10},{9,11},{10,... | collective-permute-start | bytes 983048 | tf_op jit(solution)/shard_map/ppermute | solution.py:173
  172.8 55.8 %collective-permute-start.22 = (bf16[8,80,256]{2,1,0:T(8,128)(2,1)S(1)}, bf16[8,80,256]{2,1,0:T(8,128)(2,1)S(1)}, u32[]{:S(2)}, u32[]{:S(2)}) collective-permute-start(bf16[8,80,256]{2,1,0:T(8,128)(2,1)S(1)} %get-tuple-element.37), channel_id=1, source_target_pairs={{0,2},{1,3},{2,0},{3,1},{4,6},{5,7},{6,4},{7,5},{8,10},{9,11},{10,... | collective-permute-start | bytes 983048 | tf_op jit(solution)/shard_map/ppermute | solution.py:173
  178.0 57.6 %collective-permute-start.7 = (bf16[8,80,256]{2,1,0:T(8,128)(2,1)S(1)}, bf16[8,80,256]{2,1,0:T(8,128)(2,1)S(1)}, u32[]{:S(2)}, u32[]{:S(2)}) collective-permute-start(bf16[8,80,256]{2,1,0:T(8,128)(2,1)S(1)} %get-tuple-element.31), channel_id=1, source_target_pairs={{0,2},{1,3},{2,0},{3,1},{4,6},{5,7},{6,4},{7,5},{8,10},{9,11},{10,... | collective-permute-start | bytes 983048 | tf_op jit(solution)/shard_map/ppermute | solution.py:173
  183.8 92.7 %collective-permute-start.17 = (bf16[8,80,512]{2,1,0:T(8,128)(2,1)S(1)}, bf16[8,80,512]{2,1,0:T(8,128)(2,1)S(1)}, u32[]{:S(2)}, u32[]{:S(2)}) collective-permute-start(bf16[8,80,512]{2,1,0:T(8,128)(2,1)S(1)} %get-tuple-element.35), channel_id=1, source_target_pairs={{0,2},{1,3},{2,0},{3,1},{4,6},{5,7},{6,4},{7,5},{8,10},{9,11},{10,... | collective-permute-start | bytes 1966088 | tf_op jit(solution)/shard_map/ppermute | solution.py:173
  221.5 55.3 %collective-permute-start.12 = (bf16[8,80,512]{2,1,0:T(8,128)(2,1)S(1)}, bf16[8,80,512]{2,1,0:T(8,128)(2,1)S(1)}, u32[]{:S(2)}, u32[]{:S(2)}) collective-permute-start(bf16[8,80,512]{2,1,0:T(8,128)(2,1)S(1)} %get-tuple-element.33), channel_id=1, source_target_pairs={{0,2},{1,3},{2,0},{3,1},{4,6},{5,7},{6,4},{7,5},{8,10},{9,11},{10,... | collective-permute-start | bytes 1966088 | tf_op jit(solution)/shard_map/ppermute | solution.py:173
  228.6 7.1 %collective-permute-start.28 = (bf16[4,80,256]{2,1,0:T(8,128)(2,1)S(1)}, bf16[4,80,256]{2,1,0:T(8,128)(2,1)S(1)}, u32[]{:S(2)}, u32[]{:S(2)}) collective-permute-start(bf16[4,80,256]{2,1,0:T(8,128)(2,1)S(1)} %slice.207), channel_id=1, source_target_pairs={{0,4},{4,0},{8,12},{12,8},{16,20},{20,16},{24,28},{28,24},{1,5},{5... | collective-permute-start | bytes 491528 | tf_op jit(solution)/shard_map/ppermute | solution.py:173
  235.6 4.5 %collective-permute-start.23 = (bf16[4,80,256]{2,1,0:T(8,128)(2,1)S(1)}, bf16[4,80,256]{2,1,0:T(8,128)(2,1)S(1)}, u32[]{:S(2)}, u32[]{:S(2)}) collective-permute-start(bf16[4,80,256]{2,1,0:T(8,128)(2,1)S(1)} %slice.208), channel_id=1, source_target_pairs={{0,4},{4,0},{8,12},{12,8},{16,20},{20,16},{24,28},{28,24},{1,5},{5... | collective-permute-start | bytes 491528 | tf_op jit(solution)/shard_map/ppermute | solution.py:173
  235.7 7.9 %collective-permute-start.8 = (bf16[4,80,256]{2,1,0:T(8,128)(2,1)S(1)}, bf16[4,80,256]{2,1,0:T(8,128)(2,1)S(1)}, u32[]{:S(2)}, u32[]{:S(2)}) collective-permute-start(bf16[4,80,256]{2,1,0:T(8,128)(2,1)S(1)} %slice.211), channel_id=1, source_target_pairs={{0,4},{4,0},{8,12},{12,8},{16,20},{20,16},{24,28},{28,24},{1,5},{5... | collective-permute-start | bytes 491528 | tf_op jit(solution)/shard_map/ppermute | solution.py:173
  243.6 3.7 %collective-permute-start.24 = (bf16[2,80,256]{2,1,0:T(8,128)(2,1)S(1)}, bf16[2,80,256]{2,1,0:T(8,128)(2,1)S(1)}, u32[]{:S(2)}, u32[]{:S(2)}) collective-permute-start(bf16[2,80,256]{2,1,0:T(8,128)(2,1)S(1)} %slice.213), channel_id=1, source_target_pairs={{0,8},{4,12},{8,0},{12,4},{16,24},{20,28},{24,16},{28,20},{1,9},{5... | collective-permute-start | bytes 245768 | tf_op jit(solution)/shard_map/ppermute | solution.py:173
  243.7 7.5 %collective-permute-start.9 = (bf16[2,80,256]{2,1,0:T(8,128)(2,1)S(1)}, bf16[2,80,256]{2,1,0:T(8,128)(2,1)S(1)}, u32[]{:S(2)}, u32[]{:S(2)}) collective-permute-start(bf16[2,80,256]{2,1,0:T(8,128)(2,1)S(1)} %slice.216), channel_id=1, source_target_pairs={{0,8},{4,12},{8,0},{12,4},{16,24},{20,28},{24,16},{28,20},{1,9},{5... | collective-permute-start | bytes 245768 | tf_op jit(solution)/shard_map/ppermute | solution.py:173
  247.3 5.2 %collective-permute-start.30 = (bf16[1,80,256]{2,1,0:T(8,128)(2,1)S(1)}, bf16[1,80,256]{2,1,0:T(8,128)(2,1)S(1)}, u32[]{:S(2)}, u32[]{:S(2)}) collective-permute-start(bf16[1,80,256]{2,1,0:T(8,128)(2,1)S(1)} %slice.217), channel_id=1, source_target_pairs={{0,16},{4,20},{8,24},{12,28},{16,0},{20,4},{24,8},{28,12},{1,17},{... | collective-permute-start | bytes 122888 | tf_op jit(solution)/shard_map/ppermute | solution.py:173
  251.1 10.6 %collective-permute-start.25 = (bf16[1,80,256]{2,1,0:T(8,128)(2,1)S(1)}, bf16[1,80,256]{2,1,0:T(8,128)(2,1)S(1)}, u32[]{:S(2)}, u32[]{:S(2)}) collective-permute-start(bf16[1,80,256]{2,1,0:T(8,128)(2,1)S(1)} %slice.218), channel_id=1, source_target_pairs={{0,16},{4,20},{8,24},{12,28},{16,0},{20,4},{24,8},{28,12},{1,17},{... | collective-permute-start | bytes 122888 | tf_op jit(solution)/shard_map/ppermute | solution.py:173
  252.5 17.7 %collective-permute-start.10 = (bf16[1,80,256]{2,1,0:T(8,128)(2,1)S(1)}, bf16[1,80,256]{2,1,0:T(8,128)(2,1)S(1)}, u32[]{:S(2)}, u32[]{:S(2)}) collective-permute-start(bf16[1,80,256]{2,1,0:T(8,128)(2,1)S(1)} %slice.219), channel_id=1, source_target_pairs={{0,16},{4,20},{8,24},{12,28},{16,0},{20,4},{24,8},{28,12},{1,17},{... | collective-permute-start | bytes 122888 | tf_op jit(solution)/shard_map/ppermute | solution.py:173
  256.5 66.5 %collective-permute-start.4 = (bf16[16,80,1792]{2,1,0:T(8,128)(2,1)}, bf16[16,80,1792]{2,1,0:T(8,128)(2,1)S(1)}, u32[]{:S(2)}, u32[]{:S(2)}) collective-permute-start(bf16[16,80,1792]{2,1,0:T(8,128)(2,1)} %constant_dynamic-update-slice_fusion.refs_5_.refs_6_.refs_7_.refs_8_), channel_id=1, source_target_pairs={{0,1},{1,0},{2,3},{3,2},{4,5},{5,4},{6,7},{7,6},{8,9},{9,8},{10,11... | collective-permute-start | bytes 13762568 | tf_op jit(solution)/shard_map/ppermute | solution.py:173
  276.8 9.2 %collective-permute-start.18 = (bf16[4,80,512]{2,1,0:T(8,128)(2,1)S(1)}, bf16[4,80,512]{2,1,0:T(8,128)(2,1)S(1)}, u32[]{:S(2)}, u32[]{:S(2)}) collective-permute-start(bf16[4,80,512]{2,1,0:T(8,128)(2,1)S(1)} %slice.205), channel_id=1, source_target_pairs={{0,4},{4,0},{8,12},{12,8},{16,20},{20,16},{24,28},{28,24},{1,5},{5... | collective-permute-start | bytes 983048 | tf_op jit(solution)/shard_map/ppermute | solution.py:173
  277.2 15.9 %collective-permute-start.13 = (bf16[4,80,512]{2,1,0:T(8,128)(2,1)S(1)}, bf16[4,80,512]{2,1,0:T(8,128)(2,1)S(1)}, u32[]{:S(2)}, u32[]{:S(2)}) collective-permute-start(bf16[4,80,512]{2,1,0:T(8,128)(2,1)S(1)} %slice.206), channel_id=1, source_target_pairs={{0,4},{4,0},{8,12},{12,8},{16,20},{20,16},{24,28},{28,24},{1,5},{5... | collective-permute-start | bytes 983048 | tf_op jit(solution)/shard_map/ppermute | solution.py:173
  286.1 7.2 %collective-permute-start.19 = (bf16[2,80,512]{2,1,0:T(8,128)(2,1)S(1)}, bf16[2,80,512]{2,1,0:T(8,128)(2,1)S(1)}, u32[]{:S(2)}, u32[]{:S(2)}) collective-permute-start(bf16[2,80,512]{2,1,0:T(8,128)(2,1)S(1)} %slice.209), channel_id=1, source_target_pairs={{0,8},{4,12},{8,0},{12,4},{16,24},{20,28},{24,16},{28,20},{1,9},{5... | collective-permute-start | bytes 491528 | tf_op jit(solution)/shard_map/ppermute | solution.py:173
  293.2 6.0 %collective-permute-start.14 = (bf16[2,80,512]{2,1,0:T(8,128)(2,1)S(1)}, bf16[2,80,512]{2,1,0:T(8,128)(2,1)S(1)}, u32[]{:S(2)}, u32[]{:S(2)}) collective-permute-start(bf16[2,80,512]{2,1,0:T(8,128)(2,1)S(1)} %slice.210), channel_id=1, source_target_pairs={{0,8},{4,12},{8,0},{12,4},{16,24},{20,28},{24,16},{28,20},{1,9},{5... | collective-permute-start | bytes 491528 | tf_op jit(solution)/shard_map/ppermute | solution.py:173
  293.5 5.9 %collective-permute-start.20 = (bf16[1,80,512]{2,1,0:T(8,128)(2,1)S(1)}, bf16[1,80,512]{2,1,0:T(8,128)(2,1)S(1)}, u32[]{:S(2)}, u32[]{:S(2)}) collective-permute-start(bf16[1,80,512]{2,1,0:T(8,128)(2,1)S(1)} %slice.214), channel_id=1, source_target_pairs={{0,16},{4,20},{8,24},{12,28},{16,0},{20,4},{24,8},{28,12},{1,17},{... | collective-permute-start | bytes 245768 | tf_op jit(solution)/shard_map/ppermute | solution.py:173
  299.2 4.9 %collective-permute-start.15 = (bf16[1,80,512]{2,1,0:T(8,128)(2,1)S(1)}, bf16[1,80,512]{2,1,0:T(8,128)(2,1)S(1)}, u32[]{:S(2)}, u32[]{:S(2)}) collective-permute-start(bf16[1,80,512]{2,1,0:T(8,128)(2,1)S(1)} %slice.215), channel_id=1, source_target_pairs={{0,16},{4,20},{8,24},{12,28},{16,0},{20,4},{24,8},{28,12},{1,17},{... | collective-permute-start | bytes 245768 | tf_op jit(solution)/shard_map/ppermute | solution.py:173
  (20 other events, 205.6 us)

commit v2 on v1

v2 whole, which is shorter than its diff:
```python
import functools
import math

import jax
import jax.numpy as jnp
from jax import lax
from jax.experimental import pallas as pl
from jax.experimental.pallas import tpu as pltpu
from jax.sharding import PartitionSpec as P

F32, BF16, I32 = jnp.float32, jnp.bfloat16, jnp.int32
MIB = 2**20
WIDTHS = (1280, 512)
ID_BASE = 32
ID_ROWS = 16
GROUP = 640


def dot(a, b, dims=((1,), (0,))):
    return lax.dot_general(a, b, (dims, ((), ())), preferred_element_type=F32)


def params(mib):
    return pltpu.CompilerParams(vmem_limit_bytes=mib * MIB)


def cost(flops, nbytes):
    return pl.CostEstimate(flops=int(flops), bytes_accessed=int(nbytes), transcendentals=0)


def whole(*dims):
    return pl.BlockSpec(dims, lambda *_: (0,) * len(dims))


def reverse(index, bits):
    back = 0
    for bit in range(bits):
        one = lax.bitwise_and(lax.shift_right_logical(index, bit), 1)
        back = back + one * (1 << (bits - 1 - bit))
    return back


def route_kernel(n_seq, cap, rows_dev, map_ref, emb_ref, pick_ref, send_ref):
    targets = map_ref[...]
    groups, lanes = targets.shape
    live = targets >= 0
    safe = jnp.where(live, targets, 0)
    owner = jnp.where(live, lax.div(safe, rows_dev), n_seq)
    members = [(owner == j).astype(F32) for j in range(n_seq)]
    table = jnp.concatenate(members, axis=0).astype(BF16)
    upper = (
        lax.broadcasted_iota(I32, (lanes, lanes), 0) < lax.broadcasted_iota(I32, (lanes, lanes), 1)
    ).astype(F32).astype(BF16)
    inside = dot(table, upper)
    total = n_seq * groups
    row = lax.broadcasted_iota(I32, (total, total), 0)
    col = lax.broadcasted_iota(I32, (total, total), 1)
    earlier = ((lax.div(row, groups) == lax.div(col, groups)) & (col < row)).astype(F32).astype(BF16)
    counts = dot(table, jnp.ones((lanes, lanes), BF16))
    rank_all = inside + dot(earlier, counts.astype(BF16))
    rank = jnp.zeros((groups, lanes), F32)
    for j in range(n_seq):
        rank = rank + members[j] * rank_all[j * groups : (j + 1) * groups]
    slot = jnp.where(live, owner * cap + rank.astype(I32), -1)
    number = jnp.where(live, safe - owner * rows_dev + 1, 0)
    high = lax.div(number, ID_BASE)
    low = (number - high * ID_BASE).astype(F32).astype(BF16)
    high = high.astype(F32).astype(BF16)
    slots = n_seq * cap
    place = lax.broadcasted_iota(I32, (slots, lanes), 0)
    ids = jnp.zeros((ID_ROWS, slots), F32)
    for g in range(groups):
        part = (place == slot[g : g + 1]).astype(F32).astype(BF16)
        pick_ref[:, g * lanes : (g + 1) * lanes] = part
        pair = jnp.concatenate(
            [
                jnp.broadcast_to(high[g : g + 1], (ID_ROWS // 2, lanes)),
                jnp.broadcast_to(low[g : g + 1], (ID_ROWS // 2, lanes)),
            ],
            axis=0,
        )
        ids = ids + dot(pair, part, ((1,), (1,)))
    ids = ids.astype(BF16)
    moved = dot(pick_ref[...], emb_ref[...]).astype(BF16)
    width = emb_ref.shape[1]
    for j in range(n_seq):
        send_ref[j, :cap] = moved[j * cap : (j + 1) * cap]
        digits = ids[:, j * cap : (j + 1) * cap]
        rest = jnp.zeros((ID_ROWS, width - cap), BF16)
        send_ref[j, cap:] = jnp.concatenate([digits, rest], axis=1)


def pack_kernel(n_seq, cap, start, widths, pick_ref, emb_ref, *send_refs):
    first = start
    for send_ref, width in zip(send_refs, widths):
        moved = dot(pick_ref[...], emb_ref[:, first : first + width]).astype(BF16)
        for j in range(n_seq):
            send_ref[j] = moved[j * cap : (j + 1) * cap]
        first += width


def hidden_kernel(height, me_ref, pre_ref, mine_ref, theirs_ref, slope_ref):
    values = pre_ref[...].astype(F32)
    normal_cdf = 0.5 * (1.0 + lax.erf(values * (1.0 / math.sqrt(2.0))))
    density = jnp.exp(-0.5 * values * values) * (1.0 / math.sqrt(2.0 * math.pi))
    slope_ref[...] = normal_cdf + values * density
    hidden = (values * normal_cdf).astype(BF16).T
    even_mine = lax.bitwise_and(me_ref[1], 1) == 0
    for k in range(mine_ref.shape[0] // height):
        even = hidden[2 * k * height : (2 * k + 1) * height]
        odd = hidden[(2 * k + 1) * height : (2 * k + 2) * height]
        mine_ref[k * height : (k + 1) * height] = jnp.where(even_mine, even, odd)
        theirs_ref[k * height : (k + 1) * height] = jnp.where(even_mine, odd, even)


def landing_kernel(n_seq, cap, rows_dev, got_ref, land_ref):
    lows = ID_ROWS // 2
    ids = []
    for i in range(n_seq):
        digits = got_ref[i, cap:].astype(F32)[:, :cap]
        ids.append(digits[0:1] * float(ID_BASE) + digits[lows : lows + 1])
    ids = jnp.concatenate(ids, axis=1).astype(I32) - 1
    slots = ids.shape[1]
    step = 128
    for first in range(0, rows_dev, step):
        row = lax.broadcasted_iota(I32, (step, slots), 0) + first
        land_ref[first : first + step] = (row == ids).astype(F32).astype(BF16)


def place_kernel(n_seq, cap, land_ref, got_ref, placed_ref):
    got = jnp.concatenate([got_ref[i, :cap] for i in range(n_seq)], axis=0)
    placed_ref[...] = dot(land_ref[...], got).astype(BF16)


def share_kernel(n_seq, n_pairs, height, me_ref, mine_ref, theirs_ref, own_ref, other_ref, *refs):
    away_a, keep_a, away_b, keep_b = refs
    step = pl.program_id(0)
    share = dot(mine_ref[...], own_ref[...]) + dot(theirs_ref[...], other_ref[...])
    width = share.shape[1] // 2
    n_far = n_seq // 2
    my_low = lax.bitwise_and(me_ref[0], 1)
    my_pair = lax.shift_right_logical(me_ref[1], 1)
    per_step = mine_ref.shape[0] // (height * n_pairs)
    half = n_pairs // 2

    def block(a, p, column):
        first = (a * n_pairs + p) * height
        return share[first : first + height, column : column + width]

    for a in range(per_step):
        far = (step * per_step + a) // 2
        for p in range(half):
            low, high = block(a, p, 0), block(a, p + half, 0)
            low_mine = my_pair < half
            at = lax.bitwise_xor(p, lax.bitwise_and(my_pair, half - 1)) * n_seq
            at = at + lax.bitwise_xor(a % 2, my_low) * n_far + far
            keep_a[at] = jnp.where(low_mine, low, high)
            away_a[at] = jnp.where(low_mine, high, low).astype(BF16)
    for a in range(0, per_step, 2):
        far = (step * per_step + a) // 2
        for p in range(n_pairs):
            low, high = block(a, p, width), block(a + 1, p, width)
            at = lax.bitwise_xor(p, my_pair) * n_far + far
            keep_b[at] = jnp.where(my_low == 0, low, high)
            away_b[at] = jnp.where(my_low == 0, high, low).astype(BF16)


def add_kernel(keep_a, come_a, keep_b, come_b, send_a, stay_a, send_b, stay_b):
    for keep, come, send, stay in ((keep_a, come_a, send_a, stay_a), (keep_b, come_b, send_b, stay_b)):
        n = stay.shape[0]
        stay[...] = keep[:n] + come[:n].astype(F32)
        send[...] = (keep[n:] + come[n:].astype(F32)).astype(BF16)


def add_join_kernel(keep_a, come_a, keep_b, come_b, out_ref):
    half = keep_a.shape[2]
    out_ref[:, :, :half] = (keep_a[...] + come_a[...].astype(F32)).astype(BF16)
    out_ref[:, :, half:] = (keep_b[...] + come_b[...].astype(F32)).astype(BF16)


def total_kernel(normalizer, come_ref, out_ref):
    total = come_ref[0].astype(F32)
    for k in range(1, come_ref.shape[0]):
        total = total + come_ref[k].astype(F32)
    out_ref[0] = total * normalizer


def weight_kernel(n_pieces, me_ref, *refs):
    refs, out_refs = refs[: 4 * n_pieces], refs[4 * n_pieces :]
    even_mine = lax.bitwise_and(me_ref[1], 1) == 0
    start = 0
    for k in range(2):
        mine_refs, their_refs, refs = refs[:n_pieces], refs[n_pieces : 2 * n_pieces], refs[2 * n_pieces :]
        blocks = []
        for mine, theirs in zip(mine_refs, their_refs):
            blocks.append(jnp.where(even_mine, mine[0], theirs[0]))
            blocks.append(jnp.where(even_mine, theirs[0], mine[0]))
        columns = jnp.concatenate(blocks, axis=0).T
        stop = start + columns.shape[0]
        first = 0
        for out_ref in out_refs:
            low, high = max(start, first), min(stop, first + out_ref.shape[0])
            if low < high:
                out_ref[low - first : high - first] = columns[low - start : high - start]
            first += out_ref.shape[0]
        start = stop


def act_kernel(n_parts, *refs):
    placed_refs, weight_refs, refs = refs[:n_parts], refs[n_parts : 2 * n_parts], refs[2 * n_parts :]
    slope_ref, out_ref = refs
    grad = dot(placed_refs[0][...], weight_refs[0][...])
    for placed_ref, weight_ref in zip(placed_refs[1:], weight_refs[1:]):
        grad = grad + dot(placed_ref[...], weight_ref[...])
    out_ref[...] = (grad * slope_ref[...]).astype(BF16)


def join_kernel(n_dp, me_ref, *refs):
    out_ref = refs[-1]
    height = out_ref.shape[0] // n_dp
    for q in range(n_dp):
        v = lax.bitwise_xor(me_ref[1], q)
        value = refs[0][0]
        for r in range(1, n_dp):
            value = jnp.where(v == r, refs[r][0], value)
        out_ref[q * height : (q + 1) * height] = value


def swap(value, axis, bit):
    size = lax.axis_size(axis)
    return lax.ppermute(value, axis, [(i, i ^ (1 << bit)) for i in range(size)])


def local(emb_grad, image_map, pre_act, w_down):
    n_seq, n_dp = lax.axis_size("seq"), lax.axis_size("dp")
    seq_bits, dp_bits = n_seq.bit_length() - 1, n_dp.bit_length() - 1
    me_s = lax.axis_index("seq").astype(I32)
    me_d = lax.axis_index("dp").astype(I32)
    me = jnp.stack([me_s, me_d])
    tokens, dim = emb_grad.shape[1:]
    rows_dev, hid = pre_act.shape[1:]
    cap = rows_dev // n_seq
    slots = n_seq * cap
    emb, pre = emb_grad[0], pre_act[0]
    n_parts = len(WIDTHS)
    last = n_parts - 1
    height = hid // (n_seq * n_dp)
    n_pairs = n_dp // 2
    kept = n_seq * n_pairs // 2
    normalizer = 1.0 / math.sqrt(n_dp * rows_dev * n_seq)
    smem = pl.BlockSpec(memory_space=pltpu.SMEM)
    anywhere = pl.BlockSpec(memory_space=pl.ANY)
    shape = jax.ShapeDtypeStruct
    cheap = cost(1e6, 1e5)
    clock = None
    flying = {}

    def call(body, operands, in_specs, outs, mib, name, grid=(1,), scratch=(), aliases=None):
        nonlocal clock
        given = [] if clock is None else [clock]

        def timed(*refs):
            n_in = len(operands)
            ins, refs = refs[:n_in], refs[n_in + len(given) :]
            refs[len(outs)][...] = jnp.zeros((8, 128), F32)
            body(*ins, *refs[: len(outs)], *refs[len(outs) + 1 :])

        *results, clock = pl.pallas_call(
            timed,
            grid=grid,
            in_specs=list(in_specs) + [anywhere] * len(given),
            out_specs=[block for _, block in outs] + [whole(8, 128)],
            out_shape=[one for one, _ in outs] + [shape((8, 128), F32)],
            scratch_shapes=list(scratch),
            input_output_aliases=aliases or {},
            compiler_params=params(mib),
            cost_estimate=cheap,
            name=name,
        )(*operands, *given)
        return results

    def order(*values):
        nonlocal clock
        *values, clock = lax.optimization_barrier((*values, clock))
        return values

    def boundary(*beyond):
        names = [n for n in flying if n not in beyond]
        values = order(*[flying.pop(n) for n in names])
        return dict(zip(names, values))

    def exchange(blocks):
        return lax.all_to_all(blocks, "seq", split_axis=0, concat_axis=0, tiled=True)

    w_near = [lax.dynamic_slice(w_down, (me_d * height, 0), (height, dim))[None]]
    w_bits = [("seq", bit) for bit in reversed(range(1, seq_bits))]
    far = [("dp", bit) for bit in reversed(range(1, dp_bits))]
    w_orders = [w_bits + [("seq", 0)] + far, w_bits + far + [("seq", 0)]]
    w_done = [0]
    w_names = (("w", 0), ("w", 1))

    def more_weights():
        at = w_done[0]
        if at:
            for k in range(len(w_near)):
                come = landed["w", k]
                bit = lax.bitwise_and(
                    lax.shift_right_logical(me_s if w_orders[k][at - 1][0] == "seq" else me_d, w_orders[k][at - 1][1]), 1
                )
                halves = jnp.where(bit == 0, w_near[k], come), jnp.where(bit == 0, come, w_near[k])
                w_near[k] = jnp.concatenate(halves, axis=0)
        if at == len(w_bits):
            w_near[:] = [w_near[0][:, :, : dim // 2], w_near[0][:, :, dim // 2 :]]
        for k in range(len(w_near)):
            flying["w", k] = swap(w_near[k], *(w_orders[k][at] if at < len(w_orders[k]) else ("dp", 0)))
        w_done[0] += 1

    more_weights()

    pick, sends = call(
        functools.partial(route_kernel, n_seq, cap, rows_dev),
        [image_map.reshape(tokens // 128, 128), emb],
        [whole(tokens // 128, 128), whole(tokens, WIDTHS[0])],
        [
            (shape((slots, tokens), BF16), whole(slots, tokens)),
            (
                shape((n_seq, cap + ID_ROWS, WIDTHS[0]), BF16),
                whole(n_seq, cap + ID_ROWS, WIDTHS[0]),
            ),
        ],
        60,
        "route",
    )
    rest = WIDTHS[1:]
    packed = call(
        functools.partial(pack_kernel, n_seq, cap, WIDTHS[0], rest),
        [pick, emb],
        [whole(slots, tokens), whole(tokens, dim)],
        [(shape((n_seq, cap, w), BF16), whole(n_seq, cap, w)) for w in rest],
        60,
        "pack",
    )
    landed = boundary()
    [sends] = order(sends)
    flying["got"] = exchange(sends)
    more_weights()
    mine_t, away_t, slope = call(
        functools.partial(hidden_kernel, height),
        [me, pre],
        [smem, pl.BlockSpec((rows_dev, GROUP), lambda i: (0, i))],
        [(shape((hid // 2, rows_dev), BF16), pl.BlockSpec((GROUP // 2, rows_dev), lambda i: (i, 0)))] * 2
        + [(shape((rows_dev, hid), F32), pl.BlockSpec((rows_dev, GROUP), lambda i: (0, i)))],
        60,
        "hidden",
        grid=(hid // GROUP,),
    )
    flying["hidden"] = swap(away_t, "dp", 0)

    far = [("dp", bit) for bit in reversed(range(1, dp_bits))]
    paths = (far + [("seq", 0)], [("seq", 0)] + far)
    columns = [[low + 2 * k for k in range(n_seq // 2)] for low in range(2)]
    placed_parts, sums, done, grads = [], [], [], {}

    def place(c):
        got = landed["got"]
        [placed] = call(
            functools.partial(place_kernel, n_seq, cap),
            [land, got],
            [whole(rows_dev, slots), whole(*got.shape)],
            [(shape((rows_dev, WIDTHS[c]), BF16), whole(rows_dev, WIDTHS[c]))],
            16,
            "place",
        )
        placed_parts.append(placed)
        return swap(placed, "dp", 0)

    def share(c, other):
        width = WIDTHS[c]
        half = width // 2
        *halves, = call(
            functools.partial(share_kernel, n_seq, n_pairs, height),
            [me, mine_t, theirs_t, placed_parts[c], other],
            [smem]
            + [pl.BlockSpec((GROUP // 2, rows_dev), lambda i: (i, 0))] * 2
            + [whole(rows_dev, width)] * 2,
            [(shape((kept, height, half), t), whole(kept, height, half)) for t in (BF16, F32, BF16, F32)],
            40,
            "share",
            grid=(hid // GROUP,),
        )
        sums.append([halves[1], halves[3]])
        done.append(1)
        for k in range(2):
            flying["sum", c, k] = swap(halves[2 * k], *paths[k][0])

    def advance():
        for c in reversed(range(len(sums))):
            names = [name for name in landed if name[0] == "sum" and name[1] == c]
            if not names:
                continue
            come = [landed[name] for name in names]
            at = done[c]
            done[c] += 1
            width = WIDTHS[c]
            if at > len(paths[0]):
                [grads[c]] = call(
                    functools.partial(total_kernel, normalizer),
                    come,
                    [whole(*come[0].shape)],
                    [(shape((1, height, width), F32), whole(1, height, width))],
                    24,
                    "total",
                )
                continue
            terms = [sums[c][0], come[0], sums[c][1], come[1]]
            specs = [whole(*one.shape) for one in terms]
            n = terms[0].shape[0]
            if at < len(paths[0]):
                sizes = (n // 2, height, width // 2)
                results = call(
                    add_kernel,
                    terms,
                    specs,
                    [(shape(sizes, t), whole(*sizes)) for t in (BF16, F32, BF16, F32)],
                    40,
                    "add",
                )
                sums[c] = [results[1], results[3]]
                for k in range(2):
                    flying["sum", c, k] = swap(results[2 * k], *paths[k][at])
            else:
                [sent] = call(
                    add_join_kernel,
                    terms,
                    specs,
                    [(shape((n, height, width), BF16), whole(n, height, width))],
                    40,
                    "add_join",
                )
                flying["sum", c, 0] = lax.all_to_all(
                    sent, "seq", split_axis=0, concat_axis=0, tiled=True, axis_index_groups=columns
                )

    spreads = {}

    def spread():
        for c in range(n_parts):
            if ("spread", c) in landed:
                found, bit = spreads[c]
                come = landed["spread", c]
                for at, v in enumerate(list(found)):
                    found[v + (1 << bit)] = come[at : at + 1]
            elif c not in spreads and c in grads:
                found, bit = {0: grads[c]}, dp_bits
            else:
                continue
            spreads[c] = (found, bit - 1)
            if bit:
                sent = jnp.concatenate(list(found.values()), axis=0) if len(found) > 1 else found[0]
                flying["spread", c] = swap(sent, "dp", bit - 1)

    def join(pieces, column, base):
        width = pieces[0].shape[2]
        block = math.gcd(column, width)
        more = [] if base is None else [base]
        return call(
            lambda *refs: join_kernel(n_dp, *refs[: n_dp + 1], refs[-1]),
            [me, *pieces, *more],
            [smem] + [pl.BlockSpec((1, height, block), lambda i: (0, 0, i))] * n_dp + [anywhere] * len(more),
            [
                (
                    shape((n_dp * height, dim), F32),
                    pl.BlockSpec((n_dp * height, block), lambda i: (0, i + column // block)),
                )
            ],
            24,
            "join",
            grid=(width // block,),
            aliases={n_dp + 1: 0} if more else {},
        )[0]

    def finish_weights(landed):
        n_pieces = GROUP // (2 * height)

        def spec(half, k):
            def index(i):
                flat = i * n_pieces + k
                s, d_high = lax.div(flat, n_pairs), lax.rem(flat, n_pairs)
                place = 0
                for at, (axis, bit) in enumerate(w_orders[half]):
                    one = lax.shift_right_logical(s, bit) if axis == "seq" else lax.shift_right_logical(d_high, bit - 1)
                    place = place + lax.bitwise_and(one, 1) * (1 << at)
                return (place, 0, 0)

            return pl.BlockSpec((1, height, dim // 2), index)

        return call(
            functools.partial(weight_kernel, n_pieces),
            [me, *[one for k in range(2) for part in (w_near[k], landed["w", k]) for one in [part] * n_pieces]],
            [smem] + [spec(half, k) for half in range(2) for _ in range(2) for k in range(n_pieces)],
            [(shape((w, hid), BF16), pl.BlockSpec((w, GROUP), lambda i: (0, i))) for w in WIDTHS],
            40,
            "weights",
            grid=(hid // GROUP,),
        )

    def act(first, blocks, base):
        block = 256
        tile = pl.BlockSpec((rows_dev, block), lambda i: (0, i + first))
        more = [] if base is None else [base]
        n_in = 2 * n_parts + 1
        return call(
            lambda *refs: act_kernel(n_parts, *refs[:n_in], refs[-1]),
            [*placed_parts, *weights_t, slope, *more],
            [whole(rows_dev, w) for w in WIDTHS]
            + [pl.BlockSpec((w, block), lambda i: (0, i + first)) for w in WIDTHS]
            + [tile]
            + [anywhere] * len(more),
            [(shape((rows_dev, hid), BF16), tile)],
            60,
            "act",
            grid=(blocks,),
            aliases={n_in: 0} if more else {},
        )[0]

    for _ in range(len(w_bits) - 2):
        landed = boundary("got", "hidden")
        more_weights()
    landed = boundary()
    theirs_t = landed["hidden"]
    [land] = call(
        functools.partial(landing_kernel, n_seq, cap, rows_dev),
        [landed["got"]],
        [whole(n_seq, cap + ID_ROWS, WIDTHS[0])],
        [(shape((rows_dev, slots), BF16), whole(rows_dev, slots))],
        16,
        "landing",
    )
    act_grad = None
    cuts = [(0, 6), (6, 4)]
    assert n_parts == 2
    for c in range(n_parts):
        if c < last:
            flying["got"] = exchange(packed[c])
        if w_names[0] in landed:
            more_weights()
        share(c, place(c))
        advance()
        landed = boundary()
    w_grad = None
    joined = 0
    while joined < n_parts:
        advance()
        spread()
        if w_names[0] in landed:
            more_weights()
            w_last = boundary(*[name for name in flying if name not in w_names])
            weights_t = finish_weights(w_last)
            act_grad = act(*cuts.pop(0), None)
        elif cuts:
            act_grad = act(*cuts.pop(0), act_grad)
        while joined < n_parts and joined in spreads and len(spreads[joined][0]) == n_dp:
            found = spreads[joined][0]
            w_grad = join([found[v] for v in range(n_dp)], sum(WIDTHS[:joined]), w_grad)
            joined += 1
        if flying:
            landed = boundary()
    return act_grad[None], w_grad


def solution(mesh):
    placed = (P("dp", "seq", None), P("dp", "seq"), P("dp", "seq", None), P("seq", None))
    return jax.shard_map(
        local,
        mesh=mesh,
        in_specs=placed,
        out_specs=(P("dp", "seq", None), P("seq", None)),
        check_vma=False,
    )
```

time: 345 us -> 267 us (0.77)
  blocking collectives: 97 us -> 0 us
  starting transfers between devices: 65.6 us -> 45.9 us
  waiting for transfers between devices: 95.7 us -> 115 us
  Pallas kernels: 61.6 us -> 80 us
  other arithmetic: 5.02 us -> 8.57 us
    all_to_all x3 -> x0, blocking collectives: 56.9 us -> none  [exchange(): lax.all_to_all(blocks, 'seq', split_axis=0, concat_axis=0, tiled=True)]
    all_gather x5 -> x0, blocking collectives: 40.1 us -> none  [local(): lax.all_gather(total[0] * normalizer, 'dp', axis=0, tiled=True)]
    ppermute x31 -> x23, starting transfers between devices: 56.5 us -> 27.5 us  [swap(): return lax.ppermute(value, axis, [(i, i ^ 1 << bit) for i in range(size)])]
    pallas_call x15 -> x19, Pallas kernels: 61.6 us -> 80 us  [call(): pl.pallas_call(timed, grid=grid, in_specs=list(in_specs) + [anywhere] * l...]
    all_to_all x2, waiting for transfers between devices: 0.01 us -> 9.7 us  [exchange(): lax.all_to_all(blocks, 'seq', split_axis=0, concat_axis=0, tiled=True)]
    ppermute x31 -> x23, waiting for transfers between devices: 95.7 us -> 105 us  [swap(): return lax.ppermute(value, axis, [(i, i ^ 1 << bit) for i in range(size)])]
    all_to_all x0 -> x2, starting transfers between devices: none -> 8.54 us  [advance(): lax.all_to_all(sent, 'seq', split_axis=0, concat_axis=0, tiled=True, axis...]
    select_n x0 -> x5, other arithmetic: none -> 4.6 us  [the longest x4 4.52 us: more_weights(): jnp.where(bit == 0, w_near[k], come)]
  transfers between devices with their start and end apart: 33 -> 27, of which waited for: 14 -> 12; matrix products, arithmetic and copies ran while one was open for 4% -> 3% of each run, Pallas kernels for 11% -> 27%
where the time goes in v2:
time: 267 us; the launch traced here: 265 us
  waiting for transfers between devices  115 us (43%)
  Pallas kernels  80 us (30%)
  starting transfers between devices  45.9 us (17%)
  local copies, waits for them, and re-layouts  14.9 us (6%)
  other arithmetic  8.57 us (3%)
    ppermute x23, waiting for transfers between devices, swap(): return lax.ppermute(value, axis, [(i, i ^ 1 << bit) for i in range(size)])  105 us
    pallas_call x19, Pallas kernels, call(): pl.pallas_call(timed, grid=grid, in_specs=list(in_specs) + [anywhere] * l...  80 us
    ppermute x23, starting transfers between devices, swap(): return lax.ppermute(value, axis, [(i, i ^ 1 << bit) for i in range(size)])  27.5 us
    unnamed x58, local copies, waits for them, and re-layouts  13.8 us
    all_to_all x2, starting transfers between devices, exchange(): lax.all_to_all(blocks, 'seq', split_axis=0, concat_axis=0, tiled=True)  9.93 us
    all_to_all x2, waiting for transfers between devices, exchange(): lax.all_to_all(blocks, 'seq', split_axis=0, concat_axis=0, tiled=True)  9.7 us
    all_to_all x2, starting transfers between devices, advance(): lax.all_to_all(sent, 'seq', split_axis=0, concat_axis=0, tiled=True, axis...  8.54 us
  transfers between devices with their start and end apart: 27, of which 12 were waited for; matrix products, arithmetic and copies ran while one was open for 3% of the time, Pallas kernels for 27%

profile of v2, /device:TPU:1, one launch (start us, length us, event | category | flops | bytes accessed | tf_op | source)
XLA Modules:
  0.0 265.4 jit_solution(3216464146021521023)
XLA Ops:
  1.6 3.2 %collective-permute-start = (bf16[1,80,1792]{2,1,0:T(8,128)(2,1)S(1)}, bf16[1,80,1792]{2,1,0:T(8,128)(2,1)}, u32[]{:S(2)}, u32[]{:S(2)}) collective-permute-start(bf16[1,80,1792]{2,1,0:T(8,128)(2,1)S(1)} %dynamic-slice_bitcast_fusion), channel_id=1, source_target_pairs={{0,16},{4,20},{8,24},{12,28},{16,0},{20,4},{24,8},{28,12},{1,17},{... | collective-permute-start | bytes 860168 | tf_op jit(solution)/shard_map/ppermute | solution.py:231
  4.8 7.5 %route.1 = (bf16[1024,1024]{1,0:T(8,128)(2,1)}, bf16[8,144,1280]{2,1,0:T(8,128)(2,1)}, f32[8,128]{1,0:T(8,128)}) custom-call(s32[8,128]{1,0:T(8,128)} %bitcast.14, bf16[1024,1792]{1,0:T(8,128)(2,1)} %bitcast.10), custom_call_target="tpu_custom_call" | custom-call | flops 1000000 | bytes 100000 | tf_op jit(solution)/shard_map/route/pallas_call | solution.py:268
  12.4 4.9 %pack.1 = (bf16[8,128,512]{2,1,0:T(8,128)(2,1)}, f32[8,128]{1,0:T(8,128)}) custom-call(bf16[1024,1024]{1,0:T(8,128)(2,1)} %get-tuple-element.92.refs_0_, bf16[1024,1792]{1,0:T(8,128)(2,1)} %bitcast.11, f32[8,128]{1,0:T(8,128)} %get-tuple-element.93.refs_2_), custom_call_target="tpu_custom_call" | custom-call | flops 1000000 | bytes 100000 | tf_op jit(solution)/shard_map/pack/pallas_call | solution.py:268
  17.6 6.2 %all-to-all-start = ((bf16[8,144,1280]{2,1,0:T(8,128)(2,1)}), bf16[8,144,1280]{2,1,0:T(8,128)(2,1)S(1)}, u32[]{:S(2)}, u32[]{:S(2)}) async-start(bf16[8,144,1280]{2,1,0:T(8,128)(2,1)} %get-tuple-element.96), calls=%async_computation | async-start | bytes 5898240 | tf_op jit(solution)/shard_map/all_to_all | solution.py:293
  24.4 10.3 %hidden.1 = (bf16[1280,1024]{1,0:T(8,128)(2,1)}, bf16[1280,1024]{1,0:T(8,128)(2,1)}, f32[1024,2560]{1,0:T(8,128)}, f32[8,128]{1,0:T(8,128)}) custom-call(s32[2]{0:T(128)} %pad_add_fusion.refs_0_, bf16[1024,2560]{1,0:T(8,128)(2,1)} %bitcast.12, f32[8,128]{1,0:T(8,128)} %get-tuple-element.98.refs_2_), custom_call_target="tpu_custom_call" | custom-call | flops 1000000 | bytes 100000 | tf_op jit(solution)/shard_map/hidden/pallas_call | solution.py:268
  36.7 1.8 collective-permute-start.1
  38.5 46.0 %collective-permute-done.1 = bf16[2,80,1792]{2,1,0:T(8,128)(2,1)S(1)} collective-permute-done((bf16[2,80,1792]{2,1,0:T(8,128)(2,1)S(1)}, bf16[2,80,1792]{2,1,0:T(8,128)(2,1)S(1)}, u32[]{:S(2)}, u32[]{:S(2)}) %collective-permute-start.1) | collective-permute-done | bytes 573472 | tf_op jit(solution)/shard_map/ppermute | solution.py:231
  85.3 4.3 %all-to-all-done.refs_0_.refs_1_ = bf16[8,144,1280]{2,1,0:T(8,128)(2,1)S(1)} async-done(((bf16[8,144,1280]{2,1,0:T(8,128)(2,1)}), bf16[8,144,1280]{2,1,0:T(8,128)(2,1)S(1)}, u32[]{:S(2)}, u32[]{:S(2)}) %all-to-all-start) | async-done | bytes 2949152 | tf_op jit(solution)/shard_map/all_to_all | solution.py:293
  90.0 4.5 %place.2 = (bf16[1024,1280]{1,0:T(8,128)(2,1)}, f32[8,128]{1,0:T(8,128)S(1)}) custom-call(bf16[1024,1024]{1,0:T(8,128)(2,1)S(1)} %get-tuple-element.103.refs_0_, bf16[8,144,1280]{2,1,0:T(8,128)(2,1)S(1)} %all-to-all-done.refs_0_.refs_1_, f32[8,128]{1,0:T(8,128)S(1)} %get-tuple-element.104.refs_2_), custom_call_target="tpu_custom_call" | custom-call | flops 1000000 | bytes 100000 | tf_op jit(solution)/shard_map/place/pallas_call | solution.py:268
  94.5 1.6 collective-permute-start.5
  96.1 3.7 %all-to-all-start.1 = ((bf16[8,128,512]{2,1,0:T(8,128)(2,1)}), bf16[8,128,512]{2,1,0:T(8,128)(2,1)S(1)}, u32[]{:S(2)}, u32[]{:S(2)}) async-start(bf16[8,128,512]{2,1,0:T(8,128)(2,1)} %get-tuple-element.106), calls=%async_computation.1 | async-start | bytes 2097152 | tf_op jit(solution)/shard_map/all_to_all | solution.py:293
  101.0 1.7 copy-done
  102.8 11.3 %share.2 = (bf16[8,80,640]{2,1,0:T(8,128)(2,1)}, f32[8,80,640]{2,1,0:T(8,128)S(1)}, bf16[8,80,640]{2,1,0:T(8,128)(2,1)}, f32[8,80,640]{2,1,0:T(8,128)S(1)}, f32[8,128]{1,0:T(8,128)S(1)}) custom-call(s32[2]{0:T(128)S(1)} %copy-done.19, bf16[1280,1024]{1,0:T(8,128)(2,1)S(1)} %copy-done, bf16[1280,1024]{1,0:T(8,128)(2,1)} %collective-permute-done.2.refs_2_, ...), custom_call_target="tpu_custom_call" | custom-call | flops 1000000 | bytes 100000 | tf_op jit(solution)/shard_map/share/pallas_call | solution.py:268
  120.0 5.4 %all-to-all-done.1.refs_1_ = bf16[8,128,512]{2,1,0:T(8,128)(2,1)S(1)} async-done(((bf16[8,128,512]{2,1,0:T(8,128)(2,1)}), bf16[8,128,512]{2,1,0:T(8,128)(2,1)S(1)}, u32[]{:S(2)}, u32[]{:S(2)}) %all-to-all-start.1) | async-done | bytes 1048608 | tf_op jit(solution)/shard_map/all_to_all | solution.py:293
  126.3 21.0 %collective-permute-done.4 = bf16[4,80,896]{2,1,0:T(8,128)(2,1)} collective-permute-done((bf16[4,80,896]{2,1,0:T(8,128)(2,1)}, bf16[4,80,896]{2,1,0:T(8,128)(2,1)}, u32[]{:S(2)}, u32[]{:S(2)}) %collective-permute-start.4) | collective-permute-done | bytes 573472 | tf_op jit(solution)/shard_map/ppermute | solution.py:231
  147.3 1.6 collective-permute-done.3
  156.8 1.9 collective-permute-start.9
  158.7 5.0 %share.3 = (bf16[8,80,256]{2,1,0:T(8,128)(2,1)S(1)}, f32[8,80,256]{2,1,0:T(8,128)S(1)}, bf16[8,80,256]{2,1,0:T(8,128)(2,1)S(1)}, f32[8,80,256]{2,1,0:T(8,128)S(1)}, f32[8,128]{1,0:T(8,128)S(1)}) custom-call(s32[2]{0:T(128)S(1)} %copy-done.19, bf16[1280,1024]{1,0:T(8,128)(2,1)S(1)} %copy-done.1, bf16[1280,1024]{1,0:T(8,128)(2,1)} %collective-permute-done.2.refs_2_, ...), custom_call_target="tpu_custom_call" | custom-call | flops 1000000 | bytes 100000 | tf_op jit(solution)/shard_map/share/pallas_call | solution.py:268
  163.8 1.8 add.8
  167.5 13.7 %collective-permute-done.8 = bf16[8,80,896]{2,1,0:T(8,128)(2,1)S(1)} collective-permute-done((bf16[8,80,896]{2,1,0:T(8,128)(2,1)S(1)}, bf16[8,80,896]{2,1,0:T(8,128)(2,1)S(1)}, u32[]{:S(2)}, u32[]{:S(2)}) %collective-permute-start.8) | collective-permute-done | bytes 1146912 | tf_op jit(solution)/shard_map/ppermute | solution.py:231
  181.1 2.2 collective-permute-start.12
  183.8 13.1 %collective-permute-done.11.refs_1_ = bf16[8,80,256]{2,1,0:T(8,128)(2,1)S(1)} collective-permute-done((bf16[8,80,256]{2,1,0:T(8,128)(2,1)S(1)}, bf16[8,80,256]{2,1,0:T(8,128)(2,1)S(1)}, u32[]{:S(2)}, u32[]{:S(2)}) %collective-permute-start.11) | collective-permute-done | bytes 327712 | tf_op jit(solution)/shard_map/ppermute | solution.py:231
  196.9 2.7 %collective-permute-done.12.refs_3_ = bf16[8,80,256]{2,1,0:T(8,128)(2,1)S(1)} collective-permute-done((bf16[8,80,256]{2,1,0:T(8,128)(2,1)S(1)}, bf16[8,80,256]{2,1,0:T(8,128)(2,1)S(1)}, u32[]{:S(2)}, u32[]{:S(2)}) %collective-permute-start.12) | collective-permute-done | bytes 327712 | tf_op jit(solution)/shard_map/ppermute | solution.py:231
  201.6 1.6 pad_maximum_fusion.1.refs_9_.refs_10_.refs_11_.refs_12_
  205.1 4.0 %all-to-all-start.2 = ((bf16[4,80,1280]{2,1,0:T(8,128)(2,1)}), bf16[4,80,1280]{2,1,0:T(8,128)(2,1)S(1)}, u32[]{:S(2)}, u32[]{:S(2)}) async-start(bf16[4,80,1280]{2,1,0:T(8,128)(2,1)} %copy-done.12), calls=%async_computation.2 | async-start | bytes 1638400 | tf_op jit(solution)/shard_map/all_to_all | solution.py:440
  211.9 7.8 %weights.1 = (bf16[1280,2560]{1,0:T(8,128)(2,1)}, bf16[512,2560]{1,0:T(8,128)(2,1)S(1)}, f32[8,128]{1,0:T(8,128)S(1)}) custom-call(s32[2]{0:T(128)S(1)} %copy-done.19, bf16[16,80,896]{2,1,0:T(8,128)(2,1)S(1)} %pad_maximum_fusion.refs_1_.refs_2_.refs_3_.refs_4_, bf16[16,80,896]{2,1,0:T(8,128)(2,1)S(1)} %pad_maximum_fusion.refs_1_.refs_2_.refs_3_.refs_4_, ...), custom_call_target="tpu_custom_call" | custom-call | flops 1000000 | bytes 100000 | tf_op jit(solution)/shard_map/weights/pallas_call | solution.py:268
  221.7 11.8 %act.2 = (bf16[1024,2560]{1,0:T(8,128)(2,1)}, f32[8,128]{1,0:T(8,128)}) custom-call(bf16[1024,1280]{1,0:T(8,128)(2,1)} %get-tuple-element.105.refs_3_.refs_0_, bf16[1024,512]{1,0:T(8,128)(2,1)} %copy-done.3, bf16[1280,2560]{1,0:T(8,128)(2,1)} %get-tuple-element.146.refs_2_, bf16[512,2560]{1,0:T(8,128)(2,1)} %copy-done.2, ...), custom_call_target="tpu_custom_call" | custom-call | flops 1000000 | bytes 100000 | tf_op jit(solution)/shard_map/act/pallas_call | solution.py:268
  238.1 4.5 %all-to-all-start.3 = ((bf16[4,80,512]{2,1,0:T(8,128)(2,1)}), bf16[4,80,512]{2,1,0:T(8,128)(2,1)S(1)}, u32[]{:S(2)}, u32[]{:S(2)}) async-start(bf16[4,80,512]{2,1,0:T(8,128)(2,1)} %get-tuple-element.164), calls=%async_computation.3 | async-start | bytes 655360 | tf_op jit(solution)/shard_map/all_to_all | solution.py:440
  243.4 8.8 %act.3 = (bf16[1024,2560]{1,0:T(8,128)(2,1)}, f32[8,128]{1,0:T(8,128)}) custom-call(bf16[1024,1280]{1,0:T(8,128)(2,1)} %get-tuple-element.105.refs_3_.refs_0_, bf16[1024,512]{1,0:T(8,128)(2,1)} %copy-done.3, bf16[1280,2560]{1,0:T(8,128)(2,1)} %get-tuple-element.146.refs_2_, bf16[512,2560]{1,0:T(8,128)(2,1)} %copy-done.2, ...), custom_call_target="tpu_custom_call", output_to_operand_aliasing={{0}: (5, {})} | custom-call | flops 1000000 | bytes 100000 | tf_op jit(solution)/shard_map/act/pallas_call | solution.py:268
  252.3 2.6 collective-permute-start.20
  255.6 5.2 %collective-permute-done.21.refs_3_ = f32[1,80,512]{2,1,0:T(8,128)S(1)} collective-permute-done((f32[1,80,512]{2,1,0:T(8,128)S(1)}, f32[1,80,512]{2,1,0:T(8,128)S(1)}, u32[]{:S(2)}, u32[]{:S(2)}) %collective-permute-start.21) | collective-permute-done | bytes 163872 | tf_op jit(solution)/shard_map/ppermute | solution.py:231
  261.7 2.1 join.2
  (116 shorter events, 40.6 us)
Async XLA Ops:
  1.6 16.0 %collective-permute-start = (bf16[1,80,1792]{2,1,0:T(8,128)(2,1)S(1)}, bf16[1,80,1792]{2,1,0:T(8,128)(2,1)}, u32[]{:S(2)}, u32[]{:S(2)}) collective-permute-start(bf16[1,80,1792]{2,1,0:T(8,128)(2,1)S(1)} %dynamic-slice_bitcast_fusion), channel_id=1, source_target_pairs={{0,16},{4,20},{8,24},{12,28},{16,0},{20,4},{24,8},{28,12},{1,17},{... | collective-permute-start | bytes 860168 | tf_op jit(solution)/shard_map/ppermute | solution.py:231
  17.6 72.0 %all-to-all-start = ((bf16[8,144,1280]{2,1,0:T(8,128)(2,1)}), bf16[8,144,1280]{2,1,0:T(8,128)(2,1)S(1)}, u32[]{:S(2)}, u32[]{:S(2)}) async-start(bf16[8,144,1280]{2,1,0:T(8,128)(2,1)} %get-tuple-element.96), calls=%async_computation | async-start | bytes 5898240 | tf_op jit(solution)/shard_map/all_to_all | solution.py:293
  34.7 50.6 %collective-permute-start.2 = (bf16[1280,1024]{1,0:T(8,128)(2,1)}, bf16[1280,1024]{1,0:T(8,128)(2,1)}, u32[]{:S(2)}, u32[]{:S(2)}) collective-permute-start(bf16[1280,1024]{1,0:T(8,128)(2,1)} %get-tuple-element.99), channel_id=1, source_target_pairs={{0,1},{1,0},{2,3},{3,2},{4,5},{5,4},{6,7},{7,6},{8,9},{9,8},{10,11... | collective-permute-start | bytes 7864328 | tf_op jit(solution)/shard_map/ppermute | solution.py:231
  35.5 54.2 %copy-start.20 = (f32[8,128]{1,0:T(8,128)S(1)}, f32[8,128]{1,0:T(8,128)}, u32[]{:S(2)}) copy-start(f32[8,128]{1,0:T(8,128)} %get-tuple-element.102.refs_1_) | copy-start | bytes 12292
  36.7 47.8 %collective-permute-start.1 = (bf16[2,80,1792]{2,1,0:T(8,128)(2,1)S(1)}, bf16[2,80,1792]{2,1,0:T(8,128)(2,1)S(1)}, u32[]{:S(2)}, u32[]{:S(2)}) collective-permute-start(bf16[2,80,1792]{2,1,0:T(8,128)(2,1)S(1)} %pad_maximum_fusion.6), channel_id=1, source_target_pairs={{0,8},{4,12},{8,0},{12,4},{16,24},{20,28},{24,16},{28,20},{1,9},{5... | collective-permute-start | bytes 1720328 | tf_op jit(solution)/shard_map/ppermute | solution.py:231
  94.5 6.5 %collective-permute-start.5 = (bf16[1024,1280]{1,0:T(8,128)(2,1)}, bf16[1024,1280]{1,0:T(8,128)(2,1)}, u32[]{:S(2)}, u32[]{:S(2)}) collective-permute-start(bf16[1024,1280]{1,0:T(8,128)(2,1)} %get-tuple-element.105.refs_3_.refs_0_), channel_id=1, source_target_pairs={{0,1},{1,0},{2,3},{3,2},{4,5},{5,4},{6,7},{7,6},{8,9},{9,8},{10,11... | collective-permute-start | bytes 7864328 | tf_op jit(solution)/shard_map/ppermute | solution.py:231
  96.1 29.2 %all-to-all-start.1 = ((bf16[8,128,512]{2,1,0:T(8,128)(2,1)}), bf16[8,128,512]{2,1,0:T(8,128)(2,1)S(1)}, u32[]{:S(2)}, u32[]{:S(2)}) async-start(bf16[8,128,512]{2,1,0:T(8,128)(2,1)} %get-tuple-element.106), calls=%async_computation.1 | async-start | bytes 2097152 | tf_op jit(solution)/shard_map/all_to_all | solution.py:293
  102.7 14.9 %copy-start.28 = (bf16[2,80,1792]{2,1,0:T(8,128)(2,1)S(1)}, bf16[2,80,1792]{2,1,0:T(8,128)(2,1)}, u32[]{:S(2)}) copy-start(bf16[2,80,1792]{2,1,0:T(8,128)(2,1)} %copy-done.27) | copy-start | bytes 1720324
  115.3 33.7 %collective-permute-start.6 = (bf16[8,80,640]{2,1,0:T(8,128)(2,1)}, bf16[8,80,640]{2,1,0:T(8,128)(2,1)}, u32[]{:S(2)}, u32[]{:S(2)}) collective-permute-start(bf16[8,80,640]{2,1,0:T(8,128)(2,1)} %get-tuple-element.111), channel_id=1, source_target_pairs={{0,2},{1,3},{2,0},{3,1},{4,6},{5,7},{6,4},{7,5},{8,10},{9,11},{10,... | collective-permute-start | bytes 2457608 | tf_op jit(solution)/shard_map/ppermute | solution.py:231
  116.5 32.5 %collective-permute-start.7 = (bf16[8,80,640]{2,1,0:T(8,128)(2,1)}, bf16[8,80,640]{2,1,0:T(8,128)(2,1)}, u32[]{:S(2)}, u32[]{:S(2)}) collective-permute-start(bf16[8,80,640]{2,1,0:T(8,128)(2,1)} %get-tuple-element.112), channel_id=1, source_target_pairs={{0,4},{4,0},{8,12},{12,8},{16,20},{20,16},{24,28},{28,24},{1,5},{5... | collective-permute-start | bytes 2457608 | tf_op jit(solution)/shard_map/ppermute | solution.py:231
  117.8 31.2 %copy-start.5 = (bf16[1024,1024]{1,0:T(8,128)(2,1)S(1)}, bf16[1024,1024]{1,0:T(8,128)(2,1)}, u32[]{:S(2)}) copy-start(bf16[1024,1024]{1,0:T(8,128)(2,1)} %copy-done.4) | copy-start | bytes 6291460
  118.9 28.4 %collective-permute-start.4 = (bf16[4,80,896]{2,1,0:T(8,128)(2,1)}, bf16[4,80,896]{2,1,0:T(8,128)(2,1)}, u32[]{:S(2)}, u32[]{:S(2)}) collective-permute-start(bf16[4,80,896]{2,1,0:T(8,128)(2,1)} %get-tuple-element.188), channel_id=1, source_target_pairs={{0,2},{1,3},{2,0},{3,1},{4,6},{5,7},{6,4},{7,5},{8,10},{9,11},{10,... | collective-permute-start | bytes 1720328 | tf_op jit(solution)/shard_map/ppermute | solution.py:231
  119.2 29.8 %collective-permute-start.3 = (bf16[4,80,896]{2,1,0:T(8,128)(2,1)}, bf16[4,80,896]{2,1,0:T(8,128)(2,1)}, u32[]{:S(2)}, u32[]{:S(2)}) collective-permute-start(bf16[4,80,896]{2,1,0:T(8,128)(2,1)} %get-tuple-element.189), channel_id=1, source_target_pairs={{0,4},{4,0},{8,12},{12,8},{16,20},{20,16},{24,28},{28,24},{1,5},{5... | collective-permute-start | bytes 1720328 | tf_op jit(solution)/shard_map/ppermute | solution.py:231
  151.4 7.3 %copy-start.3 = (bf16[1024,512]{1,0:T(8,128)(2,1)}, bf16[1024,512]{1,0:T(8,128)(2,1)S(1)}, u32[]{:S(2)}) copy-start(bf16[1024,512]{1,0:T(8,128)(2,1)S(1)} %get-tuple-element.116.refs_3_.refs_1_) | copy-start | bytes 3145732
  151.5 7.3 %collective-permute-start.10 = (bf16[1024,512]{1,0:T(8,128)(2,1)S(1)}, bf16[1024,512]{1,0:T(8,128)(2,1)S(1)}, u32[]{:S(2)}, u32[]{:S(2)}) collective-permute-start(bf16[1024,512]{1,0:T(8,128)(2,1)S(1)} %get-tuple-element.116.refs_3_.refs_1_), channel_id=1, source_target_pairs={{0,1},{1,0},{2,3},{3,2},{4,5},{5,4},{6,7},{7,6},{8,9},{9,8},{10,11... | collective-permute-start | bytes 3145736 | tf_op jit(solution)/shard_map/ppermute | solution.py:231
  154.5 26.6 %collective-permute-start.8 = (bf16[8,80,896]{2,1,0:T(8,128)(2,1)S(1)}, bf16[8,80,896]{2,1,0:T(8,128)(2,1)S(1)}, u32[]{:S(2)}, u32[]{:S(2)}) collective-permute-start(bf16[8,80,896]{2,1,0:T(8,128)(2,1)S(1)} %pad_maximum_fusion.2), channel_id=1, source_target_pairs={{0,2},{1,3},{2,0},{3,1},{4,6},{5,7},{6,4},{7,5},{8,10},{9,11},{10,... | collective-permute-start | bytes 3440648 | tf_op jit(solution)/shard_map/ppermute | solution.py:231
  156.8 27.0 %collective-permute-start.9 = (bf16[8,80,896]{2,1,0:T(8,128)(2,1)S(1)}, bf16[8,80,896]{2,1,0:T(8,128)(2,1)S(1)}, u32[]{:S(2)}, u32[]{:S(2)}) collective-permute-start(bf16[8,80,896]{2,1,0:T(8,128)(2,1)S(1)} %pad_maximum_fusion.3), channel_id=1, source_target_pairs={{0,4},{4,0},{8,12},{12,8},{16,20},{20,16},{24,28},{28,24},{1,5},{5... | collective-permute-start | bytes 3440648 | tf_op jit(solution)/shard_map/ppermute | solution.py:231
  165.6 34.0 %collective-permute-start.13 = (bf16[4,80,640]{2,1,0:T(8,128)(2,1)S(1)}, bf16[4,80,640]{2,1,0:T(8,128)(2,1)S(1)}, u32[]{:S(2)}, u32[]{:S(2)}) collective-permute-start(bf16[4,80,640]{2,1,0:T(8,128)(2,1)S(1)} %get-tuple-element.127), channel_id=1, source_target_pairs={{0,4},{4,0},{8,12},{12,8},{16,20},{20,16},{24,28},{28,24},{1,5},{5... | collective-permute-start | bytes 1228808 | tf_op jit(solution)/shard_map/ppermute | solution.py:231
  166.0 33.6 %collective-permute-start.14 = (bf16[4,80,640]{2,1,0:T(8,128)(2,1)S(1)}, bf16[4,80,640]{2,1,0:T(8,128)(2,1)S(1)}, u32[]{:S(2)}, u32[]{:S(2)}) collective-permute-start(bf16[4,80,640]{2,1,0:T(8,128)(2,1)S(1)} %get-tuple-element.128), channel_id=1, source_target_pairs={{0,2},{1,3},{2,0},{3,1},{4,6},{5,7},{6,4},{7,5},{8,10},{9,11},{10,... | collective-permute-start | bytes 1228808 | tf_op jit(solution)/shard_map/ppermute | solution.py:231
  167.2 29.7 %collective-permute-start.11 = (bf16[8,80,256]{2,1,0:T(8,128)(2,1)S(1)}, bf16[8,80,256]{2,1,0:T(8,128)(2,1)S(1)}, u32[]{:S(2)}, u32[]{:S(2)}) collective-permute-start(bf16[8,80,256]{2,1,0:T(8,128)(2,1)S(1)} %get-tuple-element.120), channel_id=1, source_target_pairs={{0,2},{1,3},{2,0},{3,1},{4,6},{5,7},{6,4},{7,5},{8,10},{9,11},{10,... | collective-permute-start | bytes 983048 | tf_op jit(solution)/shard_map/ppermute | solution.py:231
  181.1 18.5 %collective-permute-start.12 = (bf16[8,80,256]{2,1,0:T(8,128)(2,1)S(1)}, bf16[8,80,256]{2,1,0:T(8,128)(2,1)S(1)}, u32[]{:S(2)}, u32[]{:S(2)}) collective-permute-start(bf16[8,80,256]{2,1,0:T(8,128)(2,1)S(1)} %get-tuple-element.121), channel_id=1, source_target_pairs={{0,4},{4,0},{8,12},{12,8},{16,20},{20,16},{24,28},{28,24},{1,5},{5... | collective-permute-start | bytes 983048 | tf_op jit(solution)/shard_map/ppermute | solution.py:231
  200.4 11.5 %collective-permute-start.15 = (bf16[16,80,896]{2,1,0:T(8,128)(2,1)S(1)}, bf16[16,80,896]{2,1,0:T(8,128)(2,1)}, u32[]{:S(2)}, u32[]{:S(2)}) collective-permute-start(bf16[16,80,896]{2,1,0:T(8,128)(2,1)S(1)} %pad_maximum_fusion.refs_1_.refs_2_.refs_3_.refs_4_), channel_id=1, source_target_pairs={{0,1},{1,0},{2,3},{3,2},{4,5},{5,4},{6,7},{7,6},{8,9},{9,8},{10,11... | collective-permute-start | bytes 6881288 | tf_op jit(solution)/shard_map/ppermute | solution.py:231
  203.2 8.7 %collective-permute-start.16 = (bf16[16,80,896]{2,1,0:T(8,128)(2,1)}, bf16[16,80,896]{2,1,0:T(8,128)(2,1)}, u32[]{:S(2)}, u32[]{:S(2)}) collective-permute-start(bf16[16,80,896]{2,1,0:T(8,128)(2,1)} %pad_maximum_fusion.1.refs_9_.refs_10_.refs_11_.refs_12_), channel_id=1, source_target_pairs={{0,1},{1,0},{2,3},{3,2},{4,5},{5,4},{6,7},{7,6},{8,9},{9,8},{10,11... | collective-permute-start | bytes 6881288 | tf_op jit(solution)/shard_map/ppermute | solution.py:231
  205.1 29.7 %all-to-all-start.2 = ((bf16[4,80,1280]{2,1,0:T(8,128)(2,1)}), bf16[4,80,1280]{2,1,0:T(8,128)(2,1)S(1)}, u32[]{:S(2)}, u32[]{:S(2)}) async-start(bf16[4,80,1280]{2,1,0:T(8,128)(2,1)} %copy-done.12), calls=%async_computation.2 | async-start | bytes 1638400 | tf_op jit(solution)/shard_map/all_to_all | solution.py:440
  209.2 24.3 %collective-permute-start.17 = (bf16[4,80,256]{2,1,0:T(8,128)(2,1)}, bf16[4,80,256]{2,1,0:T(8,128)(2,1)S(1)}, u32[]{:S(2)}, u32[]{:S(2)}) collective-permute-start(bf16[4,80,256]{2,1,0:T(8,128)(2,1)} %copy-done.26), channel_id=1, source_target_pairs={{0,4},{4,0},{8,12},{12,8},{16,20},{20,16},{24,28},{28,24},{1,5},{5... | collective-permute-start | bytes 491528 | tf_op jit(solution)/shard_map/ppermute | solution.py:231
  210.6 23.5 %collective-permute-start.18 = (bf16[4,80,256]{2,1,0:T(8,128)(2,1)}, bf16[4,80,256]{2,1,0:T(8,128)(2,1)S(1)}, u32[]{:S(2)}, u32[]{:S(2)}) collective-permute-start(bf16[4,80,256]{2,1,0:T(8,128)(2,1)} %copy-done.25), channel_id=1, source_target_pairs={{0,2},{1,3},{2,0},{3,1},{4,6},{5,7},{6,4},{7,5},{8,10},{9,11},{10,... | collective-permute-start | bytes 491528 | tf_op jit(solution)/shard_map/ppermute | solution.py:231
  221.7 13.1 %copy-start.14 = (f32[4,80,256]{2,1,0:T(8,128)S(1)}, f32[4,80,256]{2,1,0:T(8,128)}, u32[]{:S(2)}) copy-start(f32[4,80,256]{2,1,0:T(8,128)} %copy-done.13) | copy-start | bytes 983044
  238.1 14.1 %all-to-all-start.3 = ((bf16[4,80,512]{2,1,0:T(8,128)(2,1)}), bf16[4,80,512]{2,1,0:T(8,128)(2,1)S(1)}, u32[]{:S(2)}, u32[]{:S(2)}) async-start(bf16[4,80,512]{2,1,0:T(8,128)(2,1)} %get-tuple-element.164), calls=%async_computation.3 | async-start | bytes 655360 | tf_op jit(solution)/shard_map/all_to_all | solution.py:440
  242.8 9.4 %collective-permute-start.19 = (f32[1,80,1280]{2,1,0:T(8,128)S(1)}, f32[1,80,1280]{2,1,0:T(8,128)S(1)}, u32[]{:S(2)}, u32[]{:S(2)}) collective-permute-start(f32[1,80,1280]{2,1,0:T(8,128)S(1)} %get-tuple-element.165.refs_1_), channel_id=1, source_target_pairs={{0,2},{1,3},{2,0},{3,1},{4,6},{5,7},{6,4},{7,5},{8,10},{9,11},{10,... | collective-permute-start | bytes 1228808 | tf_op jit(solution)/shard_map/ppermute | solution.py:231
  252.3 8.5 %collective-permute-start.20 = (f32[2,80,1280]{2,1,0:T(8,128)S(1)}, f32[2,80,1280]{2,1,0:T(8,128)S(1)}, u32[]{:S(2)}, u32[]{:S(2)}) collective-permute-start(f32[2,80,1280]{2,1,0:T(8,128)S(1)} %pad_maximum_fusion.4), channel_id=1, source_target_pairs={{0,1},{1,0},{2,3},{3,2},{4,5},{5,4},{6,7},{7,6},{8,9},{9,8},{10,11... | collective-permute-start | bytes 2457608 | tf_op jit(solution)/shard_map/ppermute | solution.py:231
  254.9 5.9 %collective-permute-start.21 = (f32[1,80,512]{2,1,0:T(8,128)S(1)}, f32[1,80,512]{2,1,0:T(8,128)S(1)}, u32[]{:S(2)}, u32[]{:S(2)}) collective-permute-start(f32[1,80,512]{2,1,0:T(8,128)S(1)} %get-tuple-element.169.refs_1_), channel_id=1, source_target_pairs={{0,2},{1,3},{2,0},{3,1},{4,6},{5,7},{6,4},{7,5},{8,10},{9,11},{10,... | collective-permute-start | bytes 491528 | tf_op jit(solution)/shard_map/ppermute | solution.py:231
  260.8 3.1 %collective-permute-start.22 = (f32[2,80,512]{2,1,0:T(8,128)S(1)}, f32[2,80,512]{2,1,0:T(8,128)S(1)}, u32[]{:S(2)}, u32[]{:S(2)}) collective-permute-start(f32[2,80,512]{2,1,0:T(8,128)S(1)} %pad_maximum_fusion.7), channel_id=1, source_target_pairs={{0,1},{1,0},{2,3},{3,2},{4,5},{5,4},{6,7},{7,6},{8,9},{9,8},{10,11... | collective-permute-start | bytes 983048 | tf_op jit(solution)/shard_map/ppermute | solution.py:231
  (24 other events, 45.7 us)

commit v3 on v2

--- a/solution.py
+++ b/solution.py
@@ -10,7 +10,7 @@
 
 F32, BF16, I32 = jnp.float32, jnp.bfloat16, jnp.int32
 MIB = 2**20
-WIDTHS = (1280, 512)
+WIDTHS = (1024, 768)
 ID_BASE = 32
 ID_ROWS = 16
 GROUP = 640
@@ -537,7 +537,7 @@
         "landing",
     )
     act_grad = None
-    cuts = [(0, 6), (6, 4)]
+    cuts = [(0, 5), (5, 5)]
     assert n_parts == 2
     for c in range(n_parts):
         if c < last:

time: 267 us -> 261 us (0.978)
  starting transfers between devices: 45.9 us -> 41.6 us
    ppermute x23, waiting for transfers between devices: 105 us -> 89.2 us  [swap(): return lax.ppermute(value, axis, [(i, i ^ 1 << bit) for i in range(size)])]
    all_to_all x2, waiting for transfers between devices: 9.7 us -> 22.9 us  [exchange(): lax.all_to_all(blocks, 'seq', split_axis=0, concat_axis=0, tiled=True)]
    ppermute x23, starting transfers between devices: 27.5 us -> 20.5 us  [swap(): return lax.ppermute(value, axis, [(i, i ^ 1 << bit) for i in range(size)])]
    unnamed x58 -> x70, local copies, waits for them, and re-layouts: 13.8 us -> 16.1 us
  transfers between devices with their start and end apart: 27 -> 27, of which waited for: 12 -> 12; matrix products, arithmetic and copies ran while one was open for 3% -> 2% of each run, Pallas kernels for 27% -> 26%
where the time goes in v3:
time: 261 us; the launch traced here: 260 us
  waiting for transfers between devices  114 us (44%)
  Pallas kernels  78.9 us (30%)
  starting transfers between devices  41.6 us (16%)
  local copies, waits for them, and re-layouts  17.2 us (7%)
  other arithmetic  7.12 us (3%)
    ppermute x23, waiting for transfers between devices, swap(): return lax.ppermute(value, axis, [(i, i ^ 1 << bit) for i in range(size)])  89.2 us
    pallas_call x19, Pallas kernels, call(): pl.pallas_call(timed, grid=grid, in_specs=list(in_specs) + [anywhere] * l...  78.9 us
    all_to_all x2, waiting for transfers between devices, exchange(): lax.all_to_all(blocks, 'seq', split_axis=0, concat_axis=0, tiled=True)  22.9 us
    ppermute x23, starting transfers between devices, swap(): return lax.ppermute(value, axis, [(i, i ^ 1 << bit) for i in range(size)])  20.5 us
    unnamed x70, local copies, waits for them, and re-layouts  16.1 us
    all_to_all x2, starting transfers between devices, exchange(): lax.all_to_all(blocks, 'seq', split_axis=0, concat_axis=0, tiled=True)  10.9 us
    all_to_all x2, starting transfers between devices, advance(): lax.all_to_all(sent, 'seq', split_axis=0, concat_axis=0, tiled=True, axis...  10.2 us
  transfers between devices with their start and end apart: 27, of which 12 were waited for; matrix products, arithmetic and copies ran while one was open for 2% of the time, Pallas kernels for 26%

profile of v3, /device:TPU:1, one launch (start us, length us, event | category | flops | bytes accessed | tf_op | source)
XLA Modules:
  0.0 260.1 jit_solution(16873482427400635109)
XLA Ops:
  1.6 3.2 %collective-permute-start = (bf16[1,80,1792]{2,1,0:T(8,128)(2,1)S(1)}, bf16[1,80,1792]{2,1,0:T(8,128)(2,1)S(1)}, u32[]{:S(2)}, u32[]{:S(2)}) collective-permute-start(bf16[1,80,1792]{2,1,0:T(8,128)(2,1)S(1)} %dynamic-slice_bitcast_fusion), channel_id=1, source_target_pairs={{0,16},{4,20},{8,24},{12,28},{16,0},{20,4},{24,8},{28,12},{1,17},{... | collective-permute-start | bytes 860168 | tf_op jit(solution)/shard_map/ppermute | solution.py:231
  4.8 6.7 %route.1 = (bf16[1024,1024]{1,0:T(8,128)(2,1)}, bf16[8,144,1024]{2,1,0:T(8,128)(2,1)}, f32[8,128]{1,0:T(8,128)}) custom-call(s32[8,128]{1,0:T(8,128)} %bitcast.14, bf16[1024,1792]{1,0:T(8,128)(2,1)} %bitcast.10), custom_call_target="tpu_custom_call" | custom-call | flops 1000000 | bytes 100000 | tf_op jit(solution)/shard_map/route/pallas_call | solution.py:268
  11.5 5.6 %pack.1 = (bf16[8,128,768]{2,1,0:T(8,128)(2,1)}, f32[8,128]{1,0:T(8,128)}) custom-call(bf16[1024,1024]{1,0:T(8,128)(2,1)} %get-tuple-element.92.refs_0_, bf16[1024,1792]{1,0:T(8,128)(2,1)} %bitcast.11, f32[8,128]{1,0:T(8,128)} %get-tuple-element.93.refs_2_), custom_call_target="tpu_custom_call" | custom-call | flops 1000000 | bytes 100000 | tf_op jit(solution)/shard_map/pack/pallas_call | solution.py:268
  17.5 6.2 %all-to-all-start = ((bf16[8,144,1024]{2,1,0:T(8,128)(2,1)}), bf16[8,144,1024]{2,1,0:T(8,128)(2,1)S(1)}, u32[]{:S(2)}, u32[]{:S(2)}) async-start(bf16[8,144,1024]{2,1,0:T(8,128)(2,1)} %get-tuple-element.96), calls=%async_computation | async-start | bytes 4718592 | tf_op jit(solution)/shard_map/all_to_all | solution.py:293
  24.4 10.2 %hidden.1 = (bf16[1280,1024]{1,0:T(8,128)(2,1)}, bf16[1280,1024]{1,0:T(8,128)(2,1)}, f32[1024,2560]{1,0:T(8,128)}, f32[8,128]{1,0:T(8,128)}) custom-call(s32[2]{0:T(128)} %pad_add_fusion.refs_0_, bf16[1024,2560]{1,0:T(8,128)(2,1)} %bitcast.12, f32[8,128]{1,0:T(8,128)} %get-tuple-element.98.refs_2_), custom_call_target="tpu_custom_call" | custom-call | flops 1000000 | bytes 100000 | tf_op jit(solution)/shard_map/hidden/pallas_call | solution.py:268
  36.5 1.8 collective-permute-start.1
  38.3 36.6 %collective-permute-done.1 = bf16[2,80,1792]{2,1,0:T(8,128)(2,1)S(1)} collective-permute-done((bf16[2,80,1792]{2,1,0:T(8,128)(2,1)S(1)}, bf16[2,80,1792]{2,1,0:T(8,128)(2,1)S(1)}, u32[]{:S(2)}, u32[]{:S(2)}) %collective-permute-start.1) | collective-permute-done | bytes 573472 | tf_op jit(solution)/shard_map/ppermute | solution.py:231
  77.3 3.7 %place.2 = (bf16[1024,1024]{1,0:T(8,128)(2,1)}, f32[8,128]{1,0:T(8,128)S(1)}) custom-call(bf16[1024,1024]{1,0:T(8,128)(2,1)S(1)} %get-tuple-element.103.refs_0_, bf16[8,144,1024]{2,1,0:T(8,128)(2,1)S(1)} %all-to-all-done.refs_0_.refs_1_, f32[8,128]{1,0:T(8,128)S(1)} %get-tuple-element.104.refs_2_), custom_call_target="tpu_custom_call" | custom-call | flops 1000000 | bytes 100000 | tf_op jit(solution)/shard_map/place/pallas_call | solution.py:268
  81.0 1.6 collective-permute-start.5
  82.6 4.7 %all-to-all-start.1 = ((bf16[8,128,768]{2,1,0:T(8,128)(2,1)}), bf16[8,128,768]{2,1,0:T(8,128)(2,1)}, u32[]{:S(2)}, u32[]{:S(2)}) async-start(bf16[8,128,768]{2,1,0:T(8,128)(2,1)} %get-tuple-element.106), calls=%async_computation.1 | async-start | bytes 3145728 | tf_op jit(solution)/shard_map/all_to_all | solution.py:293
  88.6 9.5 %share.2 = (bf16[8,80,512]{2,1,0:T(8,128)(2,1)}, f32[8,80,512]{2,1,0:T(8,128)S(1)}, bf16[8,80,512]{2,1,0:T(8,128)(2,1)}, f32[8,80,512]{2,1,0:T(8,128)S(1)}, f32[8,128]{1,0:T(8,128)S(1)}) custom-call(s32[2]{0:T(128)S(1)} %copy-done.21, bf16[1280,1024]{1,0:T(8,128)(2,1)S(1)} %copy-done.2, bf16[1280,1024]{1,0:T(8,128)(2,1)} %collective-permute-done.2.refs_2_, ...), custom_call_target="tpu_custom_call" | custom-call | flops 1000000 | bytes 100000 | tf_op jit(solution)/shard_map/share/pallas_call | solution.py:268
  102.6 21.8 %all-to-all-done.1.refs_1_ = bf16[8,128,768]{2,1,0:T(8,128)(2,1)} async-done(((bf16[8,128,768]{2,1,0:T(8,128)(2,1)}), bf16[8,128,768]{2,1,0:T(8,128)(2,1)}, u32[]{:S(2)}, u32[]{:S(2)}) %all-to-all-start.1) | async-done | bytes 1572896 | tf_op jit(solution)/shard_map/all_to_all | solution.py:293
  124.3 3.8 %collective-permute-done.4 = bf16[4,80,896]{2,1,0:T(8,128)(2,1)S(1)} collective-permute-done((bf16[4,80,896]{2,1,0:T(8,128)(2,1)S(1)}, bf16[4,80,896]{2,1,0:T(8,128)(2,1)S(1)}, u32[]{:S(2)}, u32[]{:S(2)}) %collective-permute-start.4) | collective-permute-done | bytes 573472 | tf_op jit(solution)/shard_map/ppermute | solution.py:231
  128.1 7.4 %collective-permute-done.3 = bf16[4,80,896]{2,1,0:T(8,128)(2,1)} collective-permute-done((bf16[4,80,896]{2,1,0:T(8,128)(2,1)S(1)}, bf16[4,80,896]{2,1,0:T(8,128)(2,1)}, u32[]{:S(2)}, u32[]{:S(2)}) %collective-permute-start.3) | collective-permute-done | bytes 573472 | tf_op jit(solution)/shard_map/ppermute | solution.py:231
  137.2 1.6 copy-done.5
  138.8 3.2 %place.3 = (bf16[1024,768]{1,0:T(8,128)(2,1)S(1)}, f32[8,128]{1,0:T(8,128)S(1)}) custom-call(bf16[1024,1024]{1,0:T(8,128)(2,1)S(1)} %copy-done.5, bf16[8,128,768]{2,1,0:T(8,128)(2,1)} %all-to-all-done.1.refs_1_, f32[8,128]{1,0:T(8,128)S(1)} %get-tuple-element.115.refs_2_), custom_call_target="tpu_custom_call" | custom-call | flops 1000000 | bytes 100000 | tf_op jit(solution)/shard_map/place/pallas_call | solution.py:268
  147.5 6.1 %share.3 = (bf16[8,80,384]{2,1,0:T(8,128)(2,1)S(1)}, f32[8,80,384]{2,1,0:T(8,128)S(1)}, bf16[8,80,384]{2,1,0:T(8,128)(2,1)S(1)}, f32[8,80,384]{2,1,0:T(8,128)S(1)}, f32[8,128]{1,0:T(8,128)S(1)}) custom-call(s32[2]{0:T(128)S(1)} %copy-done.21, bf16[1280,1024]{1,0:T(8,128)(2,1)S(1)} %copy-done.3, bf16[1280,1024]{1,0:T(8,128)(2,1)} %collective-permute-done.2.refs_2_, ...), custom_call_target="tpu_custom_call" | custom-call | flops 1000000 | bytes 100000 | tf_op jit(solution)/shard_map/share/pallas_call | solution.py:268
  154.5 1.5 collective-permute-start.13
  155.9 15.1 %collective-permute-done.8 = bf16[8,80,896]{2,1,0:T(8,128)(2,1)S(1)} collective-permute-done((bf16[8,80,896]{2,1,0:T(8,128)(2,1)S(1)}, bf16[8,80,896]{2,1,0:T(8,128)(2,1)S(1)}, u32[]{:S(2)}, u32[]{:S(2)}) %collective-permute-start.8) | collective-permute-done | bytes 1146912 | tf_op jit(solution)/shard_map/ppermute | solution.py:231
  172.4 17.6 %collective-permute-done.13.refs_1_ = bf16[4,80,512]{2,1,0:T(8,128)(2,1)S(1)} collective-permute-done((bf16[4,80,512]{2,1,0:T(8,128)(2,1)S(1)}, bf16[4,80,512]{2,1,0:T(8,128)(2,1)S(1)}, u32[]{:S(2)}, u32[]{:S(2)}) %collective-permute-start.13) | collective-permute-done | bytes 327712 | tf_op jit(solution)/shard_map/ppermute | solution.py:231
  192.1 1.6 pad_maximum_fusion.1.refs_9_.refs_10_.refs_11_.refs_12_
  196.4 5.7 %all-to-all-start.2 = ((bf16[4,80,1024]{2,1,0:T(8,128)(2,1)}), bf16[4,80,1024]{2,1,0:T(8,128)(2,1)S(1)}, u32[]{:S(2)}, u32[]{:S(2)}) async-start(bf16[4,80,1024]{2,1,0:T(8,128)(2,1)} %copy-done.10), calls=%async_computation.2 | async-start | bytes 1310720 | tf_op jit(solution)/shard_map/all_to_all | solution.py:440
  203.1 7.1 %weights.1 = (bf16[1024,2560]{1,0:T(8,128)(2,1)}, bf16[768,2560]{1,0:T(8,128)(2,1)S(1)}, f32[8,128]{1,0:T(8,128)S(1)}) custom-call(s32[2]{0:T(128)S(1)} %copy-done.21, bf16[16,80,896]{2,1,0:T(8,128)(2,1)S(1)} %pad_maximum_fusion.refs_1_.refs_2_.refs_3_.refs_4_, bf16[16,80,896]{2,1,0:T(8,128)(2,1)S(1)} %pad_maximum_fusion.refs_1_.refs_2_.refs_3_.refs_4_, ...), custom_call_target="tpu_custom_call" | custom-call | flops 1000000 | bytes 100000 | tf_op jit(solution)/shard_map/weights/pallas_call | solution.py:268
  210.2 1.9 copy-done
  212.7 10.5 %act.2 = (bf16[1024,2560]{1,0:T(8,128)(2,1)}, f32[8,128]{1,0:T(8,128)}) custom-call(bf16[1024,1024]{1,0:T(8,128)(2,1)} %get-tuple-element.105.refs_3_.refs_0_, bf16[1024,768]{1,0:T(8,128)(2,1)} %copy-done.1, bf16[1024,2560]{1,0:T(8,128)(2,1)} %get-tuple-element.146.refs_2_, bf16[768,2560]{1,0:T(8,128)(2,1)} %copy-done, ...), custom_call_target="tpu_custom_call" | custom-call | flops 1000000 | bytes 100000 | tf_op jit(solution)/shard_map/act/pallas_call | solution.py:268
  228.0 4.5 %all-to-all-start.3 = ((bf16[4,80,768]{2,1,0:T(8,128)(2,1)}), bf16[4,80,768]{2,1,0:T(8,128)(2,1)S(1)}, u32[]{:S(2)}, u32[]{:S(2)}) async-start(bf16[4,80,768]{2,1,0:T(8,128)(2,1)} %get-tuple-element.164), calls=%async_computation.3 | async-start | bytes 983040 | tf_op jit(solution)/shard_map/all_to_all | solution.py:440
  233.2 10.4 %act.3 = (bf16[1024,2560]{1,0:T(8,128)(2,1)}, f32[8,128]{1,0:T(8,128)}) custom-call(bf16[1024,1024]{1,0:T(8,128)(2,1)} %get-tuple-element.105.refs_3_.refs_0_, bf16[1024,768]{1,0:T(8,128)(2,1)} %copy-done.1, bf16[1024,2560]{1,0:T(8,128)(2,1)} %get-tuple-element.146.refs_2_, bf16[768,2560]{1,0:T(8,128)(2,1)} %copy-done, ...), custom_call_target="tpu_custom_call", output_to_operand_aliasing={{0}: (5, {})} | custom-call | flops 1000000 | bytes 100000 | tf_op jit(solution)/shard_map/act/pallas_call | solution.py:268
  243.6 2.1 all-to-all-done.3.refs_0_
  245.8 1.6 collective-permute-start.20
  248.0 7.1 %collective-permute-done.21.refs_3_ = f32[1,80,768]{2,1,0:T(8,128)S(1)} collective-permute-done((f32[1,80,768]{2,1,0:T(8,128)S(1)}, f32[1,80,768]{2,1,0:T(8,128)S(1)}, u32[]{:S(2)}, u32[]{:S(2)}) %collective-permute-start.21) | collective-permute-done | bytes 245792 | tf_op jit(solution)/shard_map/ppermute | solution.py:231
  256.0 1.8 join.2
  257.9 2.2 join.3
  (128 shorter events, 34.9 us)
Async XLA Ops:
  1.6 15.9 %collective-permute-start = (bf16[1,80,1792]{2,1,0:T(8,128)(2,1)S(1)}, bf16[1,80,1792]{2,1,0:T(8,128)(2,1)S(1)}, u32[]{:S(2)}, u32[]{:S(2)}) collective-permute-start(bf16[1,80,1792]{2,1,0:T(8,128)(2,1)S(1)} %dynamic-slice_bitcast_fusion), channel_id=1, source_target_pairs={{0,16},{4,20},{8,24},{12,28},{16,0},{20,4},{24,8},{28,12},{1,17},{... | collective-permute-start | bytes 860168 | tf_op jit(solution)/shard_map/ppermute | solution.py:231
  17.5 59.4 %all-to-all-start = ((bf16[8,144,1024]{2,1,0:T(8,128)(2,1)}), bf16[8,144,1024]{2,1,0:T(8,128)(2,1)S(1)}, u32[]{:S(2)}, u32[]{:S(2)}) async-start(bf16[8,144,1024]{2,1,0:T(8,128)(2,1)} %get-tuple-element.96), calls=%async_computation | async-start | bytes 4718592 | tf_op jit(solution)/shard_map/all_to_all | solution.py:293
  34.6 41.2 %collective-permute-start.2 = (bf16[1280,1024]{1,0:T(8,128)(2,1)}, bf16[1280,1024]{1,0:T(8,128)(2,1)}, u32[]{:S(2)}, u32[]{:S(2)}) collective-permute-start(bf16[1280,1024]{1,0:T(8,128)(2,1)} %get-tuple-element.99), channel_id=1, source_target_pairs={{0,1},{1,0},{2,3},{3,2},{4,5},{5,4},{6,7},{7,6},{8,9},{9,8},{10,11... | collective-permute-start | bytes 7864328 | tf_op jit(solution)/shard_map/ppermute | solution.py:231
  35.3 41.6 %copy-start.22 = (f32[8,128]{1,0:T(8,128)S(1)}, f32[8,128]{1,0:T(8,128)}, u32[]{:S(2)}) copy-start(f32[8,128]{1,0:T(8,128)} %get-tuple-element.102.refs_1_) | copy-start | bytes 12292
  36.5 38.4 %collective-permute-start.1 = (bf16[2,80,1792]{2,1,0:T(8,128)(2,1)S(1)}, bf16[2,80,1792]{2,1,0:T(8,128)(2,1)S(1)}, u32[]{:S(2)}, u32[]{:S(2)}) collective-permute-start(bf16[2,80,1792]{2,1,0:T(8,128)(2,1)S(1)} %pad_maximum_fusion.6), channel_id=1, source_target_pairs={{0,8},{4,12},{8,0},{12,4},{16,24},{20,28},{24,16},{28,20},{1,9},{5... | collective-permute-start | bytes 1720328 | tf_op jit(solution)/shard_map/ppermute | solution.py:231
  81.0 7.5 %collective-permute-start.5 = (bf16[1024,1024]{1,0:T(8,128)(2,1)}, bf16[1024,1024]{1,0:T(8,128)(2,1)}, u32[]{:S(2)}, u32[]{:S(2)}) collective-permute-start(bf16[1024,1024]{1,0:T(8,128)(2,1)} %get-tuple-element.105.refs_3_.refs_0_), channel_id=1, source_target_pairs={{0,1},{1,0},{2,3},{3,2},{4,5},{5,4},{6,7},{7,6},{8,9},{9,8},{10,11... | collective-permute-start | bytes 6291464 | tf_op jit(solution)/shard_map/ppermute | solution.py:231
  82.6 41.7 %all-to-all-start.1 = ((bf16[8,128,768]{2,1,0:T(8,128)(2,1)}), bf16[8,128,768]{2,1,0:T(8,128)(2,1)}, u32[]{:S(2)}, u32[]{:S(2)}) async-start(bf16[8,128,768]{2,1,0:T(8,128)(2,1)} %get-tuple-element.106), calls=%async_computation.1 | async-start | bytes 3145728 | tf_op jit(solution)/shard_map/all_to_all | solution.py:293
  99.1 36.3 %collective-permute-start.6 = (bf16[8,80,512]{2,1,0:T(8,128)(2,1)}, bf16[8,80,512]{2,1,0:T(8,128)(2,1)S(1)}, u32[]{:S(2)}, u32[]{:S(2)}) collective-permute-start(bf16[8,80,512]{2,1,0:T(8,128)(2,1)} %get-tuple-element.111), channel_id=1, source_target_pairs={{0,2},{1,3},{2,0},{3,1},{4,6},{5,7},{6,4},{7,5},{8,10},{9,11},{10,... | collective-permute-start | bytes 1966088 | tf_op jit(solution)/shard_map/ppermute | solution.py:231
  100.4 36.0 %collective-permute-start.7 = (bf16[8,80,512]{2,1,0:T(8,128)(2,1)}, bf16[8,80,512]{2,1,0:T(8,128)(2,1)S(1)}, u32[]{:S(2)}, u32[]{:S(2)}) collective-permute-start(bf16[8,80,512]{2,1,0:T(8,128)(2,1)} %get-tuple-element.112), channel_id=1, source_target_pairs={{0,4},{4,0},{8,12},{12,8},{16,20},{20,16},{24,28},{28,24},{1,5},{5... | collective-permute-start | bytes 1966088 | tf_op jit(solution)/shard_map/ppermute | solution.py:231
  101.6 34.7 %copy-start.29 = (bf16[4,80,896]{2,1,0:T(8,128)(2,1)}, bf16[4,80,896]{2,1,0:T(8,128)(2,1)S(1)}, u32[]{:S(2)}) copy-start(bf16[4,80,896]{2,1,0:T(8,128)(2,1)S(1)} %get-tuple-element.188) | copy-start | bytes 1720324
  101.6 40.3 %copy-start.31 = (bf16[4,80,896]{2,1,0:T(8,128)(2,1)}, bf16[4,80,896]{2,1,0:T(8,128)(2,1)S(1)}, u32[]{:S(2)}) copy-start(bf16[4,80,896]{2,1,0:T(8,128)(2,1)S(1)} %get-tuple-element.189) | copy-start | bytes 1720324
  101.6 26.5 %collective-permute-start.4 = (bf16[4,80,896]{2,1,0:T(8,128)(2,1)S(1)}, bf16[4,80,896]{2,1,0:T(8,128)(2,1)S(1)}, u32[]{:S(2)}, u32[]{:S(2)}) collective-permute-start(bf16[4,80,896]{2,1,0:T(8,128)(2,1)S(1)} %get-tuple-element.188), channel_id=1, source_target_pairs={{0,2},{1,3},{2,0},{3,1},{4,6},{5,7},{6,4},{7,5},{8,10},{9,11},{10,... | collective-permute-start | bytes 1720328 | tf_op jit(solution)/shard_map/ppermute | solution.py:231
  101.9 33.5 %collective-permute-start.3 = (bf16[4,80,896]{2,1,0:T(8,128)(2,1)S(1)}, bf16[4,80,896]{2,1,0:T(8,128)(2,1)}, u32[]{:S(2)}, u32[]{:S(2)}) collective-permute-start(bf16[4,80,896]{2,1,0:T(8,128)(2,1)S(1)} %get-tuple-element.189), channel_id=1, source_target_pairs={{0,4},{4,0},{8,12},{12,8},{16,20},{20,16},{24,28},{28,24},{1,5},{5... | collective-permute-start | bytes 1720328 | tf_op jit(solution)/shard_map/ppermute | solution.py:231
  128.1 13.9 %copy-start.32 = (bf16[4,80,896]{2,1,0:T(8,128)(2,1)}, bf16[4,80,896]{2,1,0:T(8,128)(2,1)S(1)}, u32[]{:S(2)}) copy-start(bf16[4,80,896]{2,1,0:T(8,128)(2,1)S(1)} %collective-permute-done.4) | copy-start | bytes 1720324
  142.0 4.2 %collective-permute-start.10 = (bf16[1024,768]{1,0:T(8,128)(2,1)S(1)}, bf16[1024,768]{1,0:T(8,128)(2,1)S(1)}, u32[]{:S(2)}, u32[]{:S(2)}) collective-permute-start(bf16[1024,768]{1,0:T(8,128)(2,1)S(1)} %get-tuple-element.116.refs_3_.refs_1_), channel_id=1, source_target_pairs={{0,1},{1,0},{2,3},{3,2},{4,5},{5,4},{6,7},{7,6},{8,9},{9,8},{10,11... | collective-permute-start | bytes 4718600 | tf_op jit(solution)/shard_map/ppermute | solution.py:231
  144.7 26.4 %collective-permute-start.8 = (bf16[8,80,896]{2,1,0:T(8,128)(2,1)S(1)}, bf16[8,80,896]{2,1,0:T(8,128)(2,1)S(1)}, u32[]{:S(2)}, u32[]{:S(2)}) collective-permute-start(bf16[8,80,896]{2,1,0:T(8,128)(2,1)S(1)} %pad_maximum_fusion.2), channel_id=1, source_target_pairs={{0,2},{1,3},{2,0},{3,1},{4,6},{5,7},{6,4},{7,5},{8,10},{9,11},{10,... | collective-permute-start | bytes 3440648 | tf_op jit(solution)/shard_map/ppermute | solution.py:231
  146.0 26.4 %collective-permute-start.9 = (bf16[8,80,896]{2,1,0:T(8,128)(2,1)S(1)}, bf16[8,80,896]{2,1,0:T(8,128)(2,1)S(1)}, u32[]{:S(2)}, u32[]{:S(2)}) collective-permute-start(bf16[8,80,896]{2,1,0:T(8,128)(2,1)S(1)} %pad_maximum_fusion.3), channel_id=1, source_target_pairs={{0,4},{4,0},{8,12},{12,8},{16,20},{20,16},{24,28},{28,24},{1,5},{5... | collective-permute-start | bytes 3440648 | tf_op jit(solution)/shard_map/ppermute | solution.py:231
  153.6 36.4 %collective-permute-start.11 = (bf16[8,80,384]{2,1,0:T(8,128)(2,1)S(1)}, bf16[8,80,384]{2,1,0:T(8,128)(2,1)S(1)}, u32[]{:S(2)}, u32[]{:S(2)}) collective-permute-start(bf16[8,80,384]{2,1,0:T(8,128)(2,1)S(1)} %get-tuple-element.120), channel_id=1, source_target_pairs={{0,2},{1,3},{2,0},{3,1},{4,6},{5,7},{6,4},{7,5},{8,10},{9,11},{10,... | collective-permute-start | bytes 1474568 | tf_op jit(solution)/shard_map/ppermute | solution.py:231
  154.1 35.8 %collective-permute-start.12 = (bf16[8,80,384]{2,1,0:T(8,128)(2,1)S(1)}, bf16[8,80,384]{2,1,0:T(8,128)(2,1)S(1)}, u32[]{:S(2)}, u32[]{:S(2)}) collective-permute-start(bf16[8,80,384]{2,1,0:T(8,128)(2,1)S(1)} %get-tuple-element.121), channel_id=1, source_target_pairs={{0,4},{4,0},{8,12},{12,8},{16,20},{20,16},{24,28},{28,24},{1,5},{5... | collective-permute-start | bytes 1474568 | tf_op jit(solution)/shard_map/ppermute | solution.py:231
  154.5 35.5 %collective-permute-start.13 = (bf16[4,80,512]{2,1,0:T(8,128)(2,1)S(1)}, bf16[4,80,512]{2,1,0:T(8,128)(2,1)S(1)}, u32[]{:S(2)}, u32[]{:S(2)}) collective-permute-start(bf16[4,80,512]{2,1,0:T(8,128)(2,1)S(1)} %get-tuple-element.127), channel_id=1, source_target_pairs={{0,4},{4,0},{8,12},{12,8},{16,20},{20,16},{24,28},{28,24},{1,5},{5... | collective-permute-start | bytes 983048 | tf_op jit(solution)/shard_map/ppermute | solution.py:231
  171.0 18.9 %collective-permute-start.14 = (bf16[4,80,512]{2,1,0:T(8,128)(2,1)S(1)}, bf16[4,80,512]{2,1,0:T(8,128)(2,1)S(1)}, u32[]{:S(2)}, u32[]{:S(2)}) collective-permute-start(bf16[4,80,512]{2,1,0:T(8,128)(2,1)S(1)} %get-tuple-element.128), channel_id=1, source_target_pairs={{0,2},{1,3},{2,0},{3,1},{4,6},{5,7},{6,4},{7,5},{8,10},{9,11},{10,... | collective-permute-start | bytes 983048 | tf_op jit(solution)/shard_map/ppermute | solution.py:231
  190.7 12.4 %collective-permute-start.15 = (bf16[16,80,896]{2,1,0:T(8,128)(2,1)S(1)}, bf16[16,80,896]{2,1,0:T(8,128)(2,1)}, u32[]{:S(2)}, u32[]{:S(2)}) collective-permute-start(bf16[16,80,896]{2,1,0:T(8,128)(2,1)S(1)} %pad_maximum_fusion.refs_1_.refs_2_.refs_3_.refs_4_), channel_id=1, source_target_pairs={{0,1},{1,0},{2,3},{3,2},{4,5},{5,4},{6,7},{7,6},{8,9},{9,8},{10,11... | collective-permute-start | bytes 6881288 | tf_op jit(solution)/shard_map/ppermute | solution.py:231
  193.7 9.4 %collective-permute-start.16 = (bf16[16,80,896]{2,1,0:T(8,128)(2,1)}, bf16[16,80,896]{2,1,0:T(8,128)(2,1)}, u32[]{:S(2)}, u32[]{:S(2)}) collective-permute-start(bf16[16,80,896]{2,1,0:T(8,128)(2,1)} %pad_maximum_fusion.1.refs_9_.refs_10_.refs_11_.refs_12_), channel_id=1, source_target_pairs={{0,1},{1,0},{2,3},{3,2},{4,5},{5,4},{6,7},{7,6},{8,9},{9,8},{10,11... | collective-permute-start | bytes 6881288 | tf_op jit(solution)/shard_map/ppermute | solution.py:231
  196.4 28.2 %all-to-all-start.2 = ((bf16[4,80,1024]{2,1,0:T(8,128)(2,1)}), bf16[4,80,1024]{2,1,0:T(8,128)(2,1)S(1)}, u32[]{:S(2)}, u32[]{:S(2)}) async-start(bf16[4,80,1024]{2,1,0:T(8,128)(2,1)} %copy-done.10), calls=%async_computation.2 | async-start | bytes 1310720 | tf_op jit(solution)/shard_map/all_to_all | solution.py:440
  202.1 21.1 %collective-permute-start.17 = (bf16[4,80,384]{2,1,0:T(8,128)(2,1)}, bf16[4,80,384]{2,1,0:T(8,128)(2,1)S(1)}, u32[]{:S(2)}, u32[]{:S(2)}) collective-permute-start(bf16[4,80,384]{2,1,0:T(8,128)(2,1)} %copy-done.28), channel_id=1, source_target_pairs={{0,4},{4,0},{8,12},{12,8},{16,20},{20,16},{24,28},{28,24},{1,5},{5... | collective-permute-start | bytes 737288 | tf_op jit(solution)/shard_map/ppermute | solution.py:231
  202.1 21.8 %collective-permute-start.18 = (bf16[4,80,384]{2,1,0:T(8,128)(2,1)}, bf16[4,80,384]{2,1,0:T(8,128)(2,1)S(1)}, u32[]{:S(2)}, u32[]{:S(2)}) collective-permute-start(bf16[4,80,384]{2,1,0:T(8,128)(2,1)} %copy-done.27), channel_id=1, source_target_pairs={{0,2},{1,3},{2,0},{3,1},{4,6},{5,7},{6,4},{7,5},{8,10},{9,11},{10,... | collective-permute-start | bytes 737288 | tf_op jit(solution)/shard_map/ppermute | solution.py:231
  212.7 11.9 %copy-start.16 = (f32[4,80,384]{2,1,0:T(8,128)S(1)}, f32[4,80,384]{2,1,0:T(8,128)}, u32[]{:S(2)}) copy-start(f32[4,80,384]{2,1,0:T(8,128)} %copy-done.15) | copy-start | bytes 1474564
  228.0 17.8 %all-to-all-start.3 = ((bf16[4,80,768]{2,1,0:T(8,128)(2,1)}), bf16[4,80,768]{2,1,0:T(8,128)(2,1)S(1)}, u32[]{:S(2)}, u32[]{:S(2)}) async-start(bf16[4,80,768]{2,1,0:T(8,128)(2,1)} %get-tuple-element.164), calls=%async_computation.3 | async-start | bytes 983040 | tf_op jit(solution)/shard_map/all_to_all | solution.py:440
  232.6 11.0 %collective-permute-start.19 = (f32[1,80,1024]{2,1,0:T(8,128)S(1)}, f32[1,80,1024]{2,1,0:T(8,128)S(1)}, u32[]{:S(2)}, u32[]{:S(2)}) collective-permute-start(f32[1,80,1024]{2,1,0:T(8,128)S(1)} %get-tuple-element.165.refs_1_), channel_id=1, source_target_pairs={{0,2},{1,3},{2,0},{3,1},{4,6},{5,7},{6,4},{7,5},{8,10},{9,11},{10,... | collective-permute-start | bytes 983048 | tf_op jit(solution)/shard_map/ppermute | solution.py:231
  245.8 9.3 %collective-permute-start.20 = (f32[2,80,1024]{2,1,0:T(8,128)S(1)}, f32[2,80,1024]{2,1,0:T(8,128)S(1)}, u32[]{:S(2)}, u32[]{:S(2)}) collective-permute-start(f32[2,80,1024]{2,1,0:T(8,128)S(1)} %pad_maximum_fusion.4), channel_id=1, source_target_pairs={{0,1},{1,0},{2,3},{3,2},{4,5},{5,4},{6,7},{7,6},{8,9},{9,8},{10,11... | collective-permute-start | bytes 1966088 | tf_op jit(solution)/shard_map/ppermute | solution.py:231
  247.4 7.6 %collective-permute-start.21 = (f32[1,80,768]{2,1,0:T(8,128)S(1)}, f32[1,80,768]{2,1,0:T(8,128)S(1)}, u32[]{:S(2)}, u32[]{:S(2)}) collective-permute-start(f32[1,80,768]{2,1,0:T(8,128)S(1)} %get-tuple-element.169.refs_1_), channel_id=1, source_target_pairs={{0,2},{1,3},{2,0},{3,1},{4,6},{5,7},{6,4},{7,5},{8,10},{9,11},{10,... | collective-permute-start | bytes 737288 | tf_op jit(solution)/shard_map/ppermute | solution.py:231
  255.1 2.8 %collective-permute-start.22 = (f32[2,80,768]{2,1,0:T(8,128)S(1)}, f32[2,80,768]{2,1,0:T(8,128)S(1)}, u32[]{:S(2)}, u32[]{:S(2)}) collective-permute-start(f32[2,80,768]{2,1,0:T(8,128)S(1)} %pad_maximum_fusion.7), channel_id=1, source_target_pairs={{0,1},{1,0},{2,3},{3,2},{4,5},{5,4},{6,7},{7,6},{8,9},{9,8},{10,11... | collective-permute-start | bytes 1474568 | tf_op jit(solution)/shard_map/ppermute | solution.py:231
  (30 other events, 67.4 us)

commit v4 on v3

--- a/solution.py
+++ b/solution.py
@@ -331,17 +331,8 @@
         60,
         "route",
     )
-    rest = WIDTHS[1:]
-    packed = call(
-        functools.partial(pack_kernel, n_seq, cap, WIDTHS[0], rest),
-        [pick, emb],
-        [whole(slots, tokens), whole(tokens, dim)],
-        [(shape((n_seq, cap, w), BF16), whole(n_seq, cap, w)) for w in rest],
-        60,
-        "pack",
-    )
     landed = boundary()
-    [sends] = order(sends)
+
     flying["got"] = exchange(sends)
     more_weights()
     mine_t, away_t, slope = call(
@@ -355,6 +346,15 @@
         grid=(hid // GROUP,),
     )
     flying["hidden"] = swap(away_t, "dp", 0)
+    rest = WIDTHS[1:]
+    packed = call(
+        functools.partial(pack_kernel, n_seq, cap, WIDTHS[0], rest),
+        [pick, emb],
+        [whole(slots, tokens), whole(tokens, dim)],
+        [(shape((n_seq, cap, w), BF16), whole(n_seq, cap, w)) for w in rest],
+        60,
+        "pack",
+    )
 
     far = [("dp", bit) for bit in reversed(range(1, dp_bits))]
     paths = (far + [("seq", 0)], [("seq", 0)] + far)

time: 261 us -> 293 us (1.12)
  waiting for transfers between devices: 114 us -> 147 us
    ppermute x23, waiting for transfers between devices: 89.2 us -> 123 us  [swap(): return lax.ppermute(value, axis, [(i, i ^ 1 << bit) for i in range(size)])]
  transfers between devices with their start and end apart: 27 -> 27, of which waited for: 12 -> 11; matrix products, arithmetic and copies ran while one was open for 2% -> 3% of each run, Pallas kernels for 26% -> 21%
where the time goes in v4:
time: 293 us; the launch traced here: 292 us
  waiting for transfers between devices  147 us (50%)
  Pallas kernels  78.9 us (27%)
  starting transfers between devices  39.4 us (13%)
  local copies, waits for them, and re-layouts  17.8 us (6%)
  other arithmetic  7.86 us (3%)
    ppermute x23, waiting for transfers between devices, swap(): return lax.ppermute(value, axis, [(i, i ^ 1 << bit) for i in range(size)])  123 us
    pallas_call x19, Pallas kernels, call(): pl.pallas_call(timed, grid=grid, in_specs=list(in_specs) + [anywhere] * l...  78.9 us
    all_to_all x2, waiting for transfers between devices, exchange(): lax.all_to_all(blocks, 'seq', split_axis=0, concat_axis=0, tiled=True)  21.8 us
    ppermute x23, starting transfers between devices, swap(): return lax.ppermute(value, axis, [(i, i ^ 1 << bit) for i in range(size)])  18.1 us
    unnamed x70, local copies, waits for them, and re-layouts  16.8 us
    all_to_all x2, starting transfers between devices, exchange(): lax.all_to_all(blocks, 'seq', split_axis=0, concat_axis=0, tiled=True)  11.1 us
    all_to_all x2, starting transfers between devices, advance(): lax.all_to_all(sent, 'seq', split_axis=0, concat_axis=0, tiled=True, axis...  10.2 us
  transfers between devices with their start and end apart: 27, of which 11 were waited for; matrix products, arithmetic and copies ran while one was open for 3% of the time, Pallas kernels for 21%

profile of v4, /device:TPU:1, one launch (start us, length us, event | category | flops | bytes accessed | tf_op | source)
XLA Modules:
  0.0 291.6 jit_solution(15735702829092691238)
XLA Ops:
  0.6 6.7 %route.1 = (bf16[1024,1024]{1,0:T(8,128)(2,1)}, bf16[8,144,1024]{2,1,0:T(8,128)(2,1)}, f32[8,128]{1,0:T(8,128)}) custom-call(s32[8,128]{1,0:T(8,128)} %bitcast.14, bf16[1024,1792]{1,0:T(8,128)(2,1)} %bitcast.10), custom_call_target="tpu_custom_call" | custom-call | flops 1000000 | bytes 100000 | tf_op jit(solution)/shard_map/route/pallas_call | solution.py:268
  7.3 6.4 %all-to-all-start = ((bf16[8,144,1024]{2,1,0:T(8,128)(2,1)}), bf16[8,144,1024]{2,1,0:T(8,128)(2,1)S(1)}, u32[]{:S(2)}, u32[]{:S(2)}) async-start(bf16[8,144,1024]{2,1,0:T(8,128)(2,1)} %get-tuple-element.89), calls=%async_computation | async-start | bytes 4718592 | tf_op jit(solution)/shard_map/all_to_all | solution.py:293
  14.6 2.4 collective-permute-start
  17.6 61.3 %collective-permute-done = bf16[1,80,1792]{2,1,0:T(8,128)(2,1)S(1)} collective-permute-done((bf16[1,80,1792]{2,1,0:T(8,128)(2,1)S(1)}, bf16[1,80,1792]{2,1,0:T(8,128)(2,1)S(1)}, u32[]{:S(2)}, u32[]{:S(2)}) %collective-permute-start) | collective-permute-done | bytes 286752 | tf_op jit(solution)/shard_map/ppermute | solution.py:231
  78.9 10.2 %hidden.1 = (bf16[1280,1024]{1,0:T(8,128)(2,1)}, bf16[1280,1024]{1,0:T(8,128)(2,1)}, f32[1024,2560]{1,0:T(8,128)}, f32[8,128]{1,0:T(8,128)}) custom-call(s32[2]{0:T(128)} %pad_add_fusion.refs_0_, bf16[1024,2560]{1,0:T(8,128)(2,1)} %bitcast.12, f32[8,128]{1,0:T(8,128)} %get-tuple-element.92.refs_2_), custom_call_target="tpu_custom_call" | custom-call | flops 1000000 | bytes 100000 | tf_op jit(solution)/shard_map/hidden/pallas_call | solution.py:268
  89.1 1.8 collective-permute-start.2
  92.9 5.6 %pack.1 = (bf16[8,128,768]{2,1,0:T(8,128)(2,1)}, f32[8,128]{1,0:T(8,128)}) custom-call(bf16[1024,1024]{1,0:T(8,128)(2,1)} %get-tuple-element.94.refs_0_, bf16[1024,1792]{1,0:T(8,128)(2,1)} %bitcast.11, f32[8,128]{1,0:T(8,128)} %get-tuple-element.95.refs_2_), custom_call_target="tpu_custom_call" | custom-call | flops 1000000 | bytes 100000 | tf_op jit(solution)/shard_map/pack/pallas_call | solution.py:268
  98.5 9.2 %collective-permute-done.1 = bf16[2,80,1792]{2,1,0:T(8,128)(2,1)S(1)} collective-permute-done((bf16[2,80,1792]{2,1,0:T(8,128)(2,1)}, bf16[2,80,1792]{2,1,0:T(8,128)(2,1)S(1)}, u32[]{:S(2)}, u32[]{:S(2)}) %collective-permute-start.1) | collective-permute-done | bytes 573472 | tf_op jit(solution)/shard_map/ppermute | solution.py:231
  109.6 3.7 %place.2 = (bf16[1024,1024]{1,0:T(8,128)(2,1)}, f32[8,128]{1,0:T(8,128)S(1)}) custom-call(bf16[1024,1024]{1,0:T(8,128)(2,1)S(1)} %get-tuple-element.99.refs_0_, bf16[8,144,1024]{2,1,0:T(8,128)(2,1)S(1)} %all-to-all-done.refs_0_.refs_1_, f32[8,128]{1,0:T(8,128)S(1)} %get-tuple-element.100.refs_2_), custom_call_target="tpu_custom_call" | custom-call | flops 1000000 | bytes 100000 | tf_op jit(solution)/shard_map/place/pallas_call | solution.py:268
  114.1 4.7 %all-to-all-start.1 = ((bf16[8,128,768]{2,1,0:T(8,128)(2,1)}), bf16[8,128,768]{2,1,0:T(8,128)(2,1)}, u32[]{:S(2)}, u32[]{:S(2)}) async-start(bf16[8,128,768]{2,1,0:T(8,128)(2,1)} %get-tuple-element.102), calls=%async_computation.1 | async-start | bytes 3145728 | tf_op jit(solution)/shard_map/all_to_all | solution.py:293
  120.0 9.5 %share.2 = (bf16[8,80,512]{2,1,0:T(8,128)(2,1)}, f32[8,80,512]{2,1,0:T(8,128)S(1)}, bf16[8,80,512]{2,1,0:T(8,128)(2,1)}, f32[8,80,512]{2,1,0:T(8,128)S(1)}, f32[8,128]{1,0:T(8,128)S(1)}) custom-call(s32[2]{0:T(128)S(1)} %copy-done.21, bf16[1280,1024]{1,0:T(8,128)(2,1)S(1)} %copy-done.2, bf16[1280,1024]{1,0:T(8,128)(2,1)} %collective-permute-done.2.refs_2_, ...), custom_call_target="tpu_custom_call" | custom-call | flops 1000000 | bytes 100000 | tf_op jit(solution)/shard_map/share/pallas_call | solution.py:268
  134.0 21.8 %all-to-all-done.1.refs_1_ = bf16[8,128,768]{2,1,0:T(8,128)(2,1)} async-done(((bf16[8,128,768]{2,1,0:T(8,128)(2,1)}), bf16[8,128,768]{2,1,0:T(8,128)(2,1)}, u32[]{:S(2)}, u32[]{:S(2)}) %all-to-all-start.1) | async-done | bytes 1572896 | tf_op jit(solution)/shard_map/all_to_all | solution.py:293
  155.8 3.7 %collective-permute-done.4 = bf16[4,80,896]{2,1,0:T(8,128)(2,1)S(1)} collective-permute-done((bf16[4,80,896]{2,1,0:T(8,128)(2,1)S(1)}, bf16[4,80,896]{2,1,0:T(8,128)(2,1)S(1)}, u32[]{:S(2)}, u32[]{:S(2)}) %collective-permute-start.4) | collective-permute-done | bytes 573472 | tf_op jit(solution)/shard_map/ppermute | solution.py:231
  159.5 7.4 %collective-permute-done.3 = bf16[4,80,896]{2,1,0:T(8,128)(2,1)} collective-permute-done((bf16[4,80,896]{2,1,0:T(8,128)(2,1)S(1)}, bf16[4,80,896]{2,1,0:T(8,128)(2,1)}, u32[]{:S(2)}, u32[]{:S(2)}) %collective-permute-start.3) | collective-permute-done | bytes 573472 | tf_op jit(solution)/shard_map/ppermute | solution.py:231
  168.6 1.6 copy-done.5
  170.2 3.2 %place.3 = (bf16[1024,768]{1,0:T(8,128)(2,1)S(1)}, f32[8,128]{1,0:T(8,128)S(1)}) custom-call(bf16[1024,1024]{1,0:T(8,128)(2,1)S(1)} %copy-done.5, bf16[8,128,768]{2,1,0:T(8,128)(2,1)} %all-to-all-done.1.refs_1_, f32[8,128]{1,0:T(8,128)S(1)} %get-tuple-element.111.refs_2_), custom_call_target="tpu_custom_call" | custom-call | flops 1000000 | bytes 100000 | tf_op jit(solution)/shard_map/place/pallas_call | solution.py:268
  179.0 6.1 %share.3 = (bf16[8,80,384]{2,1,0:T(8,128)(2,1)S(1)}, f32[8,80,384]{2,1,0:T(8,128)S(1)}, bf16[8,80,384]{2,1,0:T(8,128)(2,1)S(1)}, f32[8,80,384]{2,1,0:T(8,128)S(1)}, f32[8,128]{1,0:T(8,128)S(1)}) custom-call(s32[2]{0:T(128)S(1)} %copy-done.21, bf16[1280,1024]{1,0:T(8,128)(2,1)S(1)} %copy-done.3, bf16[1280,1024]{1,0:T(8,128)(2,1)} %collective-permute-done.2.refs_2_, ...), custom_call_target="tpu_custom_call" | custom-call | flops 1000000 | bytes 100000 | tf_op jit(solution)/shard_map/share/pallas_call | solution.py:268
  185.9 1.5 collective-permute-start.13
  187.4 15.1 %collective-permute-done.8 = bf16[8,80,896]{2,1,0:T(8,128)(2,1)S(1)} collective-permute-done((bf16[8,80,896]{2,1,0:T(8,128)(2,1)S(1)}, bf16[8,80,896]{2,1,0:T(8,128)(2,1)S(1)}, u32[]{:S(2)}, u32[]{:S(2)}) %collective-permute-start.8) | collective-permute-done | bytes 1146912 | tf_op jit(solution)/shard_map/ppermute | solution.py:231
  203.8 17.6 %collective-permute-done.13.refs_1_ = bf16[4,80,512]{2,1,0:T(8,128)(2,1)S(1)} collective-permute-done((bf16[4,80,512]{2,1,0:T(8,128)(2,1)S(1)}, bf16[4,80,512]{2,1,0:T(8,128)(2,1)S(1)}, u32[]{:S(2)}, u32[]{:S(2)}) %collective-permute-start.13) | collective-permute-done | bytes 327712 | tf_op jit(solution)/shard_map/ppermute | solution.py:231
  223.6 1.6 pad_maximum_fusion.1.refs_9_.refs_10_.refs_11_.refs_12_
  227.8 5.7 %all-to-all-start.2 = ((bf16[4,80,1024]{2,1,0:T(8,128)(2,1)}), bf16[4,80,1024]{2,1,0:T(8,128)(2,1)S(1)}, u32[]{:S(2)}, u32[]{:S(2)}) async-start(bf16[4,80,1024]{2,1,0:T(8,128)(2,1)} %copy-done.10), calls=%async_computation.2 | async-start | bytes 1310720 | tf_op jit(solution)/shard_map/all_to_all | solution.py:440
  234.5 7.1 %weights.1 = (bf16[1024,2560]{1,0:T(8,128)(2,1)}, bf16[768,2560]{1,0:T(8,128)(2,1)S(1)}, f32[8,128]{1,0:T(8,128)S(1)}) custom-call(s32[2]{0:T(128)S(1)} %copy-done.21, bf16[16,80,896]{2,1,0:T(8,128)(2,1)S(1)} %pad_maximum_fusion.refs_1_.refs_2_.refs_3_.refs_4_, bf16[16,80,896]{2,1,0:T(8,128)(2,1)S(1)} %pad_maximum_fusion.refs_1_.refs_2_.refs_3_.refs_4_, ...), custom_call_target="tpu_custom_call" | custom-call | flops 1000000 | bytes 100000 | tf_op jit(solution)/shard_map/weights/pallas_call | solution.py:268
  241.7 1.9 copy-done
  244.1 10.5 %act.2 = (bf16[1024,2560]{1,0:T(8,128)(2,1)}, f32[8,128]{1,0:T(8,128)}) custom-call(bf16[1024,1024]{1,0:T(8,128)(2,1)} %get-tuple-element.101.refs_3_.refs_0_, bf16[1024,768]{1,0:T(8,128)(2,1)} %copy-done.1, bf16[1024,2560]{1,0:T(8,128)(2,1)} %get-tuple-element.142.refs_2_, bf16[768,2560]{1,0:T(8,128)(2,1)} %copy-done, ...), custom_call_target="tpu_custom_call" | custom-call | flops 1000000 | bytes 100000 | tf_op jit(solution)/shard_map/act/pallas_call | solution.py:268
  259.4 4.5 %all-to-all-start.3 = ((bf16[4,80,768]{2,1,0:T(8,128)(2,1)}), bf16[4,80,768]{2,1,0:T(8,128)(2,1)S(1)}, u32[]{:S(2)}, u32[]{:S(2)}) async-start(bf16[4,80,768]{2,1,0:T(8,128)(2,1)} %get-tuple-element.160), calls=%async_computation.3 | async-start | bytes 983040 | tf_op jit(solution)/shard_map/all_to_all | solution.py:440
  264.6 10.4 %act.3 = (bf16[1024,2560]{1,0:T(8,128)(2,1)}, f32[8,128]{1,0:T(8,128)}) custom-call(bf16[1024,1024]{1,0:T(8,128)(2,1)} %get-tuple-element.101.refs_3_.refs_0_, bf16[1024,768]{1,0:T(8,128)(2,1)} %copy-done.1, bf16[1024,2560]{1,0:T(8,128)(2,1)} %get-tuple-element.142.refs_2_, bf16[768,2560]{1,0:T(8,128)(2,1)} %copy-done, ...), custom_call_target="tpu_custom_call", output_to_operand_aliasing={{0}: (5, {})} | custom-call | flops 1000000 | bytes 100000 | tf_op jit(solution)/shard_map/act/pallas_call | solution.py:268
  275.1 2.1 all-to-all-done.3.refs_0_
  277.3 1.6 collective-permute-start.20
  279.4 7.1 %collective-permute-done.21.refs_3_ = f32[1,80,768]{2,1,0:T(8,128)S(1)} collective-permute-done((f32[1,80,768]{2,1,0:T(8,128)S(1)}, f32[1,80,768]{2,1,0:T(8,128)S(1)}, u32[]{:S(2)}, u32[]{:S(2)}) %collective-permute-start.21) | collective-permute-done | bytes 245792 | tf_op jit(solution)/shard_map/ppermute | solution.py:231
  287.5 1.8 join.2
  289.4 2.2 join.3
  (128 shorter events, 34.7 us)
Async XLA Ops:
  7.3 101.2 %all-to-all-start = ((bf16[8,144,1024]{2,1,0:T(8,128)(2,1)}), bf16[8,144,1024]{2,1,0:T(8,128)(2,1)S(1)}, u32[]{:S(2)}, u32[]{:S(2)}) async-start(bf16[8,144,1024]{2,1,0:T(8,128)(2,1)} %get-tuple-element.89), calls=%async_computation | async-start | bytes 4718592 | tf_op jit(solution)/shard_map/all_to_all | solution.py:293
  14.6 64.3 %collective-permute-start = (bf16[1,80,1792]{2,1,0:T(8,128)(2,1)S(1)}, bf16[1,80,1792]{2,1,0:T(8,128)(2,1)S(1)}, u32[]{:S(2)}, u32[]{:S(2)}) collective-permute-start(bf16[1,80,1792]{2,1,0:T(8,128)(2,1)S(1)} %dynamic-slice_bitcast_fusion), channel_id=1, source_target_pairs={{0,16},{4,20},{8,24},{12,28},{16,0},{20,4},{24,8},{28,12},{1,17},{... | collective-permute-start | bytes 860168 | tf_op jit(solution)/shard_map/ppermute | solution.py:231
  89.1 19.4 %collective-permute-start.2 = (bf16[1280,1024]{1,0:T(8,128)(2,1)}, bf16[1280,1024]{1,0:T(8,128)(2,1)}, u32[]{:S(2)}, u32[]{:S(2)}) collective-permute-start(bf16[1280,1024]{1,0:T(8,128)(2,1)} %get-tuple-element.93), channel_id=1, source_target_pairs={{0,1},{1,0},{2,3},{3,2},{4,5},{5,4},{6,7},{7,6},{8,9},{9,8},{10,11... | collective-permute-start | bytes 7864328 | tf_op jit(solution)/shard_map/ppermute | solution.py:231
  92.9 14.8 %collective-permute-start.1 = (bf16[2,80,1792]{2,1,0:T(8,128)(2,1)}, bf16[2,80,1792]{2,1,0:T(8,128)(2,1)S(1)}, u32[]{:S(2)}, u32[]{:S(2)}) collective-permute-start(bf16[2,80,1792]{2,1,0:T(8,128)(2,1)} %pad_maximum_fusion.6), channel_id=1, source_target_pairs={{0,8},{4,12},{8,0},{12,4},{16,24},{20,28},{24,16},{28,20},{1,9},{5... | collective-permute-start | bytes 1720328 | tf_op jit(solution)/shard_map/ppermute | solution.py:231
  113.3 6.7 %collective-permute-start.5 = (bf16[1024,1024]{1,0:T(8,128)(2,1)}, bf16[1024,1024]{1,0:T(8,128)(2,1)}, u32[]{:S(2)}, u32[]{:S(2)}) collective-permute-start(bf16[1024,1024]{1,0:T(8,128)(2,1)} %get-tuple-element.101.refs_3_.refs_0_), channel_id=1, source_target_pairs={{0,1},{1,0},{2,3},{3,2},{4,5},{5,4},{6,7},{7,6},{8,9},{9,8},{10,11... | collective-permute-start | bytes 6291464 | tf_op jit(solution)/shard_map/ppermute | solution.py:231
  114.1 41.7 %all-to-all-start.1 = ((bf16[8,128,768]{2,1,0:T(8,128)(2,1)}), bf16[8,128,768]{2,1,0:T(8,128)(2,1)}, u32[]{:S(2)}, u32[]{:S(2)}) async-start(bf16[8,128,768]{2,1,0:T(8,128)(2,1)} %get-tuple-element.102), calls=%async_computation.1 | async-start | bytes 3145728 | tf_op jit(solution)/shard_map/all_to_all | solution.py:293
  130.6 36.3 %collective-permute-start.6 = (bf16[8,80,512]{2,1,0:T(8,128)(2,1)}, bf16[8,80,512]{2,1,0:T(8,128)(2,1)S(1)}, u32[]{:S(2)}, u32[]{:S(2)}) collective-permute-start(bf16[8,80,512]{2,1,0:T(8,128)(2,1)} %get-tuple-element.107), channel_id=1, source_target_pairs={{0,2},{1,3},{2,0},{3,1},{4,6},{5,7},{6,4},{7,5},{8,10},{9,11},{10,... | collective-permute-start | bytes 1966088 | tf_op jit(solution)/shard_map/ppermute | solution.py:231
  131.8 36.0 %collective-permute-start.7 = (bf16[8,80,512]{2,1,0:T(8,128)(2,1)}, bf16[8,80,512]{2,1,0:T(8,128)(2,1)S(1)}, u32[]{:S(2)}, u32[]{:S(2)}) collective-permute-start(bf16[8,80,512]{2,1,0:T(8,128)(2,1)} %get-tuple-element.108), channel_id=1, source_target_pairs={{0,4},{4,0},{8,12},{12,8},{16,20},{20,16},{24,28},{28,24},{1,5},{5... | collective-permute-start | bytes 1966088 | tf_op jit(solution)/shard_map/ppermute | solution.py:231
  133.1 34.7 %copy-start.29 = (bf16[4,80,896]{2,1,0:T(8,128)(2,1)}, bf16[4,80,896]{2,1,0:T(8,128)(2,1)S(1)}, u32[]{:S(2)}) copy-start(bf16[4,80,896]{2,1,0:T(8,128)(2,1)S(1)} %get-tuple-element.184) | copy-start | bytes 1720324
  133.1 40.4 %copy-start.31 = (bf16[4,80,896]{2,1,0:T(8,128)(2,1)}, bf16[4,80,896]{2,1,0:T(8,128)(2,1)S(1)}, u32[]{:S(2)}) copy-start(bf16[4,80,896]{2,1,0:T(8,128)(2,1)S(1)} %get-tuple-element.185) | copy-start | bytes 1720324
  133.1 26.5 %collective-permute-start.4 = (bf16[4,80,896]{2,1,0:T(8,128)(2,1)S(1)}, bf16[4,80,896]{2,1,0:T(8,128)(2,1)S(1)}, u32[]{:S(2)}, u32[]{:S(2)}) collective-permute-start(bf16[4,80,896]{2,1,0:T(8,128)(2,1)S(1)} %get-tuple-element.184), channel_id=1, source_target_pairs={{0,2},{1,3},{2,0},{3,1},{4,6},{5,7},{6,4},{7,5},{8,10},{9,11},{10,... | collective-permute-start | bytes 1720328 | tf_op jit(solution)/shard_map/ppermute | solution.py:231
  133.4 33.5 %collective-permute-start.3 = (bf16[4,80,896]{2,1,0:T(8,128)(2,1)S(1)}, bf16[4,80,896]{2,1,0:T(8,128)(2,1)}, u32[]{:S(2)}, u32[]{:S(2)}) collective-permute-start(bf16[4,80,896]{2,1,0:T(8,128)(2,1)S(1)} %get-tuple-element.185), channel_id=1, source_target_pairs={{0,4},{4,0},{8,12},{12,8},{16,20},{20,16},{24,28},{28,24},{1,5},{5... | collective-permute-start | bytes 1720328 | tf_op jit(solution)/shard_map/ppermute | solution.py:231
  159.5 13.9 %copy-start.32 = (bf16[4,80,896]{2,1,0:T(8,128)(2,1)}, bf16[4,80,896]{2,1,0:T(8,128)(2,1)S(1)}, u32[]{:S(2)}) copy-start(bf16[4,80,896]{2,1,0:T(8,128)(2,1)S(1)} %collective-permute-done.4) | copy-start | bytes 1720324
  173.5 4.2 %collective-permute-start.10 = (bf16[1024,768]{1,0:T(8,128)(2,1)S(1)}, bf16[1024,768]{1,0:T(8,128)(2,1)S(1)}, u32[]{:S(2)}, u32[]{:S(2)}) collective-permute-start(bf16[1024,768]{1,0:T(8,128)(2,1)S(1)} %get-tuple-element.112.refs_3_.refs_1_), channel_id=1, source_target_pairs={{0,1},{1,0},{2,3},{3,2},{4,5},{5,4},{6,7},{7,6},{8,9},{9,8},{10,11... | collective-permute-start | bytes 4718600 | tf_op jit(solution)/shard_map/ppermute | solution.py:231
  176.1 26.4 %collective-permute-start.8 = (bf16[8,80,896]{2,1,0:T(8,128)(2,1)S(1)}, bf16[8,80,896]{2,1,0:T(8,128)(2,1)S(1)}, u32[]{:S(2)}, u32[]{:S(2)}) collective-permute-start(bf16[8,80,896]{2,1,0:T(8,128)(2,1)S(1)} %pad_maximum_fusion.2), channel_id=1, source_target_pairs={{0,2},{1,3},{2,0},{3,1},{4,6},{5,7},{6,4},{7,5},{8,10},{9,11},{10,... | collective-permute-start | bytes 3440648 | tf_op jit(solution)/shard_map/ppermute | solution.py:231
  177.4 26.4 %collective-permute-start.9 = (bf16[8,80,896]{2,1,0:T(8,128)(2,1)S(1)}, bf16[8,80,896]{2,1,0:T(8,128)(2,1)S(1)}, u32[]{:S(2)}, u32[]{:S(2)}) collective-permute-start(bf16[8,80,896]{2,1,0:T(8,128)(2,1)S(1)} %pad_maximum_fusion.3), channel_id=1, source_target_pairs={{0,4},{4,0},{8,12},{12,8},{16,20},{20,16},{24,28},{28,24},{1,5},{5... | collective-permute-start | bytes 3440648 | tf_op jit(solution)/shard_map/ppermute | solution.py:231
  178.9 6.7 %copy-start.14 = (bf16[8,80,512]{2,1,0:T(8,128)(2,1)S(1)}, bf16[8,80,512]{2,1,0:T(8,128)(2,1)}, u32[]{:S(2)}) copy-start(bf16[8,80,512]{2,1,0:T(8,128)(2,1)} %copy-done.13) | copy-start | bytes 1966084
  185.0 36.4 %collective-permute-start.11 = (bf16[8,80,384]{2,1,0:T(8,128)(2,1)S(1)}, bf16[8,80,384]{2,1,0:T(8,128)(2,1)S(1)}, u32[]{:S(2)}, u32[]{:S(2)}) collective-permute-start(bf16[8,80,384]{2,1,0:T(8,128)(2,1)S(1)} %get-tuple-element.116), channel_id=1, source_target_pairs={{0,2},{1,3},{2,0},{3,1},{4,6},{5,7},{6,4},{7,5},{8,10},{9,11},{10,... | collective-permute-start | bytes 1474568 | tf_op jit(solution)/shard_map/ppermute | solution.py:231
  185.6 35.8 %collective-permute-start.12 = (bf16[8,80,384]{2,1,0:T(8,128)(2,1)S(1)}, bf16[8,80,384]{2,1,0:T(8,128)(2,1)S(1)}, u32[]{:S(2)}, u32[]{:S(2)}) collective-permute-start(bf16[8,80,384]{2,1,0:T(8,128)(2,1)S(1)} %get-tuple-element.117), channel_id=1, source_target_pairs={{0,4},{4,0},{8,12},{12,8},{16,20},{20,16},{24,28},{28,24},{1,5},{5... | collective-permute-start | bytes 1474568 | tf_op jit(solution)/shard_map/ppermute | solution.py:231
  185.9 35.5 %collective-permute-start.13 = (bf16[4,80,512]{2,1,0:T(8,128)(2,1)S(1)}, bf16[4,80,512]{2,1,0:T(8,128)(2,1)S(1)}, u32[]{:S(2)}, u32[]{:S(2)}) collective-permute-start(bf16[4,80,512]{2,1,0:T(8,128)(2,1)S(1)} %get-tuple-element.123), channel_id=1, source_target_pairs={{0,4},{4,0},{8,12},{12,8},{16,20},{20,16},{24,28},{28,24},{1,5},{5... | collective-permute-start | bytes 983048 | tf_op jit(solution)/shard_map/ppermute | solution.py:231
  202.5 18.9 %collective-permute-start.14 = (bf16[4,80,512]{2,1,0:T(8,128)(2,1)S(1)}, bf16[4,80,512]{2,1,0:T(8,128)(2,1)S(1)}, u32[]{:S(2)}, u32[]{:S(2)}) collective-permute-start(bf16[4,80,512]{2,1,0:T(8,128)(2,1)S(1)} %get-tuple-element.124), channel_id=1, source_target_pairs={{0,2},{1,3},{2,0},{3,1},{4,6},{5,7},{6,4},{7,5},{8,10},{9,11},{10,... | collective-permute-start | bytes 983048 | tf_op jit(solution)/shard_map/ppermute | solution.py:231
  222.1 12.4 %collective-permute-start.15 = (bf16[16,80,896]{2,1,0:T(8,128)(2,1)S(1)}, bf16[16,80,896]{2,1,0:T(8,128)(2,1)}, u32[]{:S(2)}, u32[]{:S(2)}) collective-permute-start(bf16[16,80,896]{2,1,0:T(8,128)(2,1)S(1)} %pad_maximum_fusion.refs_1_.refs_2_.refs_3_.refs_4_), channel_id=1, source_target_pairs={{0,1},{1,0},{2,3},{3,2},{4,5},{5,4},{6,7},{7,6},{8,9},{9,8},{10,11... | collective-permute-start | bytes 6881288 | tf_op jit(solution)/shard_map/ppermute | solution.py:231
  225.2 9.4 %collective-permute-start.16 = (bf16[16,80,896]{2,1,0:T(8,128)(2,1)}, bf16[16,80,896]{2,1,0:T(8,128)(2,1)}, u32[]{:S(2)}, u32[]{:S(2)}) collective-permute-start(bf16[16,80,896]{2,1,0:T(8,128)(2,1)} %pad_maximum_fusion.1.refs_9_.refs_10_.refs_11_.refs_12_), channel_id=1, source_target_pairs={{0,1},{1,0},{2,3},{3,2},{4,5},{5,4},{6,7},{7,6},{8,9},{9,8},{10,11... | collective-permute-start | bytes 6881288 | tf_op jit(solution)/shard_map/ppermute | solution.py:231
  227.8 28.2 %all-to-all-start.2 = ((bf16[4,80,1024]{2,1,0:T(8,128)(2,1)}), bf16[4,80,1024]{2,1,0:T(8,128)(2,1)S(1)}, u32[]{:S(2)}, u32[]{:S(2)}) async-start(bf16[4,80,1024]{2,1,0:T(8,128)(2,1)} %copy-done.10), calls=%async_computation.2 | async-start | bytes 1310720 | tf_op jit(solution)/shard_map/all_to_all | solution.py:440
  233.5 21.1 %collective-permute-start.17 = (bf16[4,80,384]{2,1,0:T(8,128)(2,1)}, bf16[4,80,384]{2,1,0:T(8,128)(2,1)S(1)}, u32[]{:S(2)}, u32[]{:S(2)}) collective-permute-start(bf16[4,80,384]{2,1,0:T(8,128)(2,1)} %copy-done.28), channel_id=1, source_target_pairs={{0,4},{4,0},{8,12},{12,8},{16,20},{20,16},{24,28},{28,24},{1,5},{5... | collective-permute-start | bytes 737288 | tf_op jit(solution)/shard_map/ppermute | solution.py:231
  233.5 21.8 %collective-permute-start.18 = (bf16[4,80,384]{2,1,0:T(8,128)(2,1)}, bf16[4,80,384]{2,1,0:T(8,128)(2,1)S(1)}, u32[]{:S(2)}, u32[]{:S(2)}) collective-permute-start(bf16[4,80,384]{2,1,0:T(8,128)(2,1)} %copy-done.27), channel_id=1, source_target_pairs={{0,2},{1,3},{2,0},{3,1},{4,6},{5,7},{6,4},{7,5},{8,10},{9,11},{10,... | collective-permute-start | bytes 737288 | tf_op jit(solution)/shard_map/ppermute | solution.py:231
  244.1 11.9 %copy-start.16 = (f32[4,80,384]{2,1,0:T(8,128)S(1)}, f32[4,80,384]{2,1,0:T(8,128)}, u32[]{:S(2)}) copy-start(f32[4,80,384]{2,1,0:T(8,128)} %copy-done.15) | copy-start | bytes 1474564
  259.4 17.8 %all-to-all-start.3 = ((bf16[4,80,768]{2,1,0:T(8,128)(2,1)}), bf16[4,80,768]{2,1,0:T(8,128)(2,1)S(1)}, u32[]{:S(2)}, u32[]{:S(2)}) async-start(bf16[4,80,768]{2,1,0:T(8,128)(2,1)} %get-tuple-element.160), calls=%async_computation.3 | async-start | bytes 983040 | tf_op jit(solution)/shard_map/all_to_all | solution.py:440
  264.1 11.0 %collective-permute-start.19 = (f32[1,80,1024]{2,1,0:T(8,128)S(1)}, f32[1,80,1024]{2,1,0:T(8,128)S(1)}, u32[]{:S(2)}, u32[]{:S(2)}) collective-permute-start(f32[1,80,1024]{2,1,0:T(8,128)S(1)} %get-tuple-element.161.refs_1_), channel_id=1, source_target_pairs={{0,2},{1,3},{2,0},{3,1},{4,6},{5,7},{6,4},{7,5},{8,10},{9,11},{10,... | collective-permute-start | bytes 983048 | tf_op jit(solution)/shard_map/ppermute | solution.py:231
  277.3 9.3 %collective-permute-start.20 = (f32[2,80,1024]{2,1,0:T(8,128)S(1)}, f32[2,80,1024]{2,1,0:T(8,128)S(1)}, u32[]{:S(2)}, u32[]{:S(2)}) collective-permute-start(f32[2,80,1024]{2,1,0:T(8,128)S(1)} %pad_maximum_fusion.4), channel_id=1, source_target_pairs={{0,1},{1,0},{2,3},{3,2},{4,5},{5,4},{6,7},{7,6},{8,9},{9,8},{10,11... | collective-permute-start | bytes 1966088 | tf_op jit(solution)/shard_map/ppermute | solution.py:231
  278.9 7.6 %collective-permute-start.21 = (f32[1,80,768]{2,1,0:T(8,128)S(1)}, f32[1,80,768]{2,1,0:T(8,128)S(1)}, u32[]{:S(2)}, u32[]{:S(2)}) collective-permute-start(f32[1,80,768]{2,1,0:T(8,128)S(1)} %get-tuple-element.165.refs_1_), channel_id=1, source_target_pairs={{0,2},{1,3},{2,0},{3,1},{4,6},{5,7},{6,4},{7,5},{8,10},{9,11},{10,... | collective-permute-start | bytes 737288 | tf_op jit(solution)/shard_map/ppermute | solution.py:231
  286.6 2.8 collective-permute-start.22
  (30 other events, 61.4 us)
